TPU v7x, 32 devices: a whole 2x2x4 slice. The times are simulated.
32 devices in a mesh: expert: 16 (over z, y, x), hsplit: 2 (over core).
Axes of the slice: x: 2, y: 2, z: 4, core: 2. Of those that a mesh axis runs over, the one named last changes fastest.
Arguments:
- tokens: bfloat16 [256, 7168], P('expert'), may hold values from -6 to 6
- routes: int32 [256, 8], P('expert'), may hold values from 0 to 15, all different within a row; in each aligned block of 16 rows (0 to 15, 16 to 31, ...) at most 16 rows name the same one
- route_weights: float32 [256, 8], P('expert'), may hold values from 0.05 to 0.6
- gate_weight: bfloat16 [16, 7168, 2048], P('expert', None, 'hsplit'), may hold values from -0.0625 to 0.0625
- up_weight: bfloat16 [16, 7168, 2048], P('expert', None, 'hsplit'), may hold values from -0.0625 to 0.0625
- down_weight: bfloat16 [16, 2048, 7168], P('expert', 'hsplit'), may hold values from -0.125 to 0.125
Outputs:
- routed_out: bfloat16 [256, 7168], P('expert', 'hsplit')
Inputs may be any that keep to these rules, and one draw needn't show every extreme that they name: `routes`: each token names 8 different experts. In each aligned block of 16 tokens (one of 1 block of the tokens of one index of the expert axis) some expert is named by every token of the block.
All inputs are finite; a program needn't handle non-finite values.
Results may differ from a plain program's by a relative error of at most 0.02.
Values may be sent and summed in bfloat16 or wider, within the bound.
No kernel may reach another device: no remote copies, remote signals or barrier semaphores. Data moves between devices by JAX's collectives and lax.ppermute only.
A program may use at most 128 MiB of HBM per device.

v0:
```python
import jax
import jax.numpy as jnp
from jax import lax
from jax.sharding import PartitionSpec as P

EXPERTS = 16


def as_sent(array):

    def short(part):
        return part.astype(jnp.bfloat16) if part.dtype == jnp.float32 else part

    return jax.tree.map(short, array)


def swapped(block, axis, apart):
    count = lax.axis_size(axis)
    route = []
    for low in range(count):
        high = low | 1 << apart
        if high != low and high < count:
            route += [(low, high), (high, low)]
    return lax.ppermute(block, axis, route)


def expert_rows(tok_rows, full_gate, full_up, full_down):
    gate_value = jnp.dot(tok_rows, full_gate, preferred_element_type=jnp.float32)
    up_value = jnp.dot(tok_rows, full_up, preferred_element_type=jnp.float32)
    hidden = (jax.nn.silu(gate_value) * up_value).astype(jnp.bfloat16)
    partial_value = jnp.dot(hidden, full_down, preferred_element_type=jnp.float32)
    return lax.optimization_barrier(partial_value.astype(jnp.bfloat16))


def local(tokens, routes, route_weights, gate_weight, up_weight, down_weight):
    tok_dev, model_width = tokens.shape
    top_k = routes.shape[1]
    owners = lax.axis_size("expert")
    splits = lax.axis_size("hsplit")
    group_size = owners // EXPERTS
    group_bits = group_size.bit_length() - 1
    most = tok_dev // group_size
    slot_count = owners * most
    slice_width = model_width // group_size
    piece_width = slice_width // splits
    position = lax.axis_index("expert")
    token_group = lax.broadcasted_iota(jnp.int32, (tok_dev, top_k), 0) // most
    owner_of = (group_size * routes + token_group).reshape(-1)
    owner_hit = (owner_of[:, None] == jnp.arange(owners, dtype=jnp.int32)[None, :]).astype(
        jnp.int32
    )
    earlier = jnp.cumsum(owner_hit, axis=0) - owner_hit
    ranking = jnp.sum(earlier * owner_hit, axis=1)
    slot_of = owner_of * most + ranking
    slot_grid = slot_of.reshape(tok_dev, top_k)
    selector = jnp.any(
        slot_grid[:, :, None] == jnp.arange(slot_count, dtype=jnp.int32)[None, None, :], axis=1
    ).astype(jnp.bfloat16)
    outgoing = jnp.einsum("ts,td->sd", selector, tokens, preferred_element_type=jnp.float32).astype(
        jnp.bfloat16
    )
    outgoing = outgoing.reshape(owners, most, model_width)
    stacked = (gate_weight, up_weight, down_weight)
    for level in range(group_bits):
        partner = jax.tree.map(
            lambda part, own: part.astype(own.dtype),
            swapped(as_sent(stacked), "expert", level),
            stacked,
        )
        upper = position >> level & 1 == 1
        stacked = tuple(
            (
                jnp.where(
                    upper,
                    jnp.concatenate([far_piece, near_piece], axis=0),
                    jnp.concatenate([near_piece, far_piece], axis=0),
                )
                for near_piece, far_piece in zip(stacked, partner)
            )
        )
    share_units = gate_weight.shape[2]
    full_gate = stacked[0].reshape(model_width, share_units)
    full_up = stacked[1].reshape(model_width, share_units)
    full_down = stacked[2].transpose(1, 0, 2).reshape(share_units, group_size, splits, piece_width)
    full_down = full_down.transpose(0, 2, 1, 3).reshape(share_units, model_width)
    arrived = lax.all_to_all(outgoing, "expert", split_axis=0, concat_axis=0, tiled=True)
    flat_rows = arrived.reshape(-1, model_width)
    partials = expert_rows(flat_rows, full_gate, full_up, full_down).reshape(arrived.shape)
    partials = partials.reshape(slot_count, model_width)
    summed = lax.psum_scatter(
        partials.astype(jnp.float32).astype(jnp.bfloat16), "hsplit", scatter_dimension=1, tiled=True
    )
    results = summed.reshape(owners, most, -1)
    returned = lax.all_to_all(results, "expert", split_axis=0, concat_axis=0, tiled=True)
    picked = returned.reshape(slot_count, -1)[slot_of].astype(jnp.float32)
    weighted = picked.reshape(tok_dev, top_k, -1) * route_weights[:, :, None]
    return jnp.sum(weighted, axis=1).astype(jnp.bfloat16)


def solution(mesh):
    placed = (
        P("expert", None),
        P("expert", None),
        P("expert", None),
        P("expert", None, "hsplit"),
        P("expert", None, "hsplit"),
        P("expert", "hsplit", None),
    )
    return jax.shard_map(
        local, mesh=mesh, in_specs=placed, out_specs=P("expert", "hsplit"), check_vma=False
    )
```

profile of v0, /device:TPU:0, one launch (start us, length us, event | category | flops | bytes accessed | tf_op | source)
XLA Modules:
  0.0 194.1 jit_solution(3957490405812996887)
XLA Ops:
  6.5 0.0 copy-start
  6.5 0.0 reduce-scatter.2.cloned.1.call-start
  6.6 0.8 copy.11
  7.4 0.1 broadcast_multiply_fusion
  7.4 0.1 eq.28
  7.5 0.1 fusion.25
  7.6 0.2 reduce_window_sum.11
  7.8 0.2 select_reduce_fusion
  8.0 0.1 reduce_sum.23
  8.1 0.1 fusion.24
  8.2 0.0 copy-done
  8.2 1.1 convolution_convert_fusion
  9.4 90.7 %all_to_all.10 = bf16[16,16,7168]{2,1,0:T(8,128)(2,1)S(1)} all-to-all(bf16[16,16,7168]{2,1,0:T(8,128)(2,1)S(1)} %bitcast.35), channel_id=1, replica_groups=mesh['expert'=16,'hsplit'=2] {'expert'}, dimensions={0} | all-to-all | bytes 7340032 | tf_op jit(solution)/shard_map/all_to_all | solution.py:86
  100.0 0.0 copy-start.1
  100.0 1.8 copy-done.1
  101.9 7.2 %fusion.4 = f32[256,1024]{1,0:T(8,128)S(1)} fusion(bf16[256,7168]{1,0:T(8,128)(2,1)S(1)} %bitcast.36, bf16[1,7168,1024]{2,1,0:T(8,128)(2,1)} %param.9), kind=kOutput, calls=%fused_computation.5 | convolution fusion | flops 3758096384 | bytes 19398656 | tf_op jit(solution)/shard_map/dot_general | solution.py:28
  109.1 20.1 %fusion.6 = bf16[256,7168]{1,0:T(8,128)(2,1)} fusion(bf16[1,1024,7168]{2,1,0:T(8,128)(2,1)} %param.11, bf16[256,7168]{1,0:T(8,128)(2,1)} %bitcast.37, bf16[1,7168,1024]{2,1,0:T(8,128)(2,1)} %param.10, f32[256,1024]{1,0:T(8,128)S(1)} %fusion.4), kind=kOutput, calls=%fused_computation.7 | convolution fusion | flops 7519600640 | bytes 37748736 | tf_op jit(solution)/shard_map/dot_general | solution.py:31
  129.2 0.0 copy-start.2
  129.2 0.0 reduce-scatter.2.cloned.1.call-update
  129.3 10.0 %reduce-scatter.2.cloned.1.call-done = bf16[256,3584]{1,0:T(8,128)(2,1)} async-done(((bf16[256,7168]{1,0:T(8,128)(2,1)}), bf16[256,3584]{1,0:T(8,128)(2,1)}) %reduce-scatter.2.cloned.1.call-update) | async-done | bytes 1835024 | tf_op jit(solution)/shard_map/reduce_scatter | solution.py:90
  139.2 6.7 %all-to-all-start.1 = ((bf16[16,16,3584]{2,1,0:T(8,128)(2,1)}), bf16[16,16,3584]{2,1,0:T(8,128)(2,1)S(1)}, u32[]{:S(2)}, u32[]{:S(2)}) async-start(bf16[16,16,3584]{2,1,0:T(8,128)(2,1)} %bitcast.38), calls=%async_computation.2 | async-start | bytes 3670016 | tf_op jit(solution)/shard_map/all_to_all | solution.py:94
  146.0 0.1 mul.41
  146.1 0.0 copy-done.2
  146.1 0.1 copy.12
  146.2 38.6 %all-to-all-done.1 = bf16[16,16,3584]{2,1,0:T(8,128)(2,1)S(1)} async-done(((bf16[16,16,3584]{2,1,0:T(8,128)(2,1)}), bf16[16,16,3584]{2,1,0:T(8,128)(2,1)S(1)}, u32[]{:S(2)}, u32[]{:S(2)}) %all-to-all-start.1) | async-done | bytes 1835040 | tf_op jit(solution)/shard_map/all_to_all | solution.py:94
  184.8 1.1 gather_fusion
  185.9 1.3 fusion.9
  (5 shorter events, 0.0 us)
Async XLA Ops:
  6.5 1.7 copy-start
  6.5 132.7 %reduce-scatter.2.cloned.1.call-start = ((), (), s32[]{:S(2)}) async-start(), calls=%async_computation.3 | async-start | bytes 5505024 | tf_op jit(solution)/shard_map/reduce_scatter | solution.py:90
  100.0 1.8 copy-start.1
  129.2 16.9 %copy-start.2 = (f32[16,8]{0,1:T(8,128)S(1)}, f32[16,8]{0,1:T(8,128)}, u32[]{:S(2)}) copy-start(f32[16,8]{0,1:T(8,128)} %param.8) | copy-start | bytes 1540
  139.2 45.5 %all-to-all-start.1 = ((bf16[16,16,3584]{2,1,0:T(8,128)(2,1)}), bf16[16,16,3584]{2,1,0:T(8,128)(2,1)S(1)}, u32[]{:S(2)}, u32[]{:S(2)}) async-start(bf16[16,16,3584]{2,1,0:T(8,128)(2,1)} %bitcast.38), calls=%async_computation.2 | async-start | bytes 3670016 | tf_op jit(solution)/shard_map/all_to_all | solution.py:94
Sparse Core Ops, SparseCore 0:
  129.4 9.8 reduce-scatter.1
where the time goes:
time: 197 us; the launch traced here: 194 us
  blocking collectives  90.7 us (46%)
  waiting for transfers between devices  48.6 us (25%)
  matrix products  28.5 us (14%)
  between operations  13.5 us (7%)
  starting transfers between devices  6.75 us (3%)
  local copies, waits for them, and re-layouts  4.08 us (2%)
  other arithmetic  2.02 us (1%)
    all_to_all x1, blocking collectives, local(): lax.all_to_all(outgoing, 'expert', split_axis=0, concat_axis=0, tiled=True)  90.7 us
    all_to_all x1, waiting for transfers between devices, local(): lax.all_to_all(results, 'expert', split_axis=0, concat_axis=0, tiled=True)  38.6 us
    dot_general x1, matrix products, expert_rows(): jnp.dot(hidden, full_down, preferred_element_type=jnp.float32)  20.1 us
    reduce_scatter x1, waiting for transfers between devices, local(): lax.psum_scatter(partials.astype(jnp.float32).astype(jnp.bfloat16), 'hspl...  9.98 us
    dot_general x1, matrix products, expert_rows(): jnp.dot(tok_rows, full_gate, preferred_element_type=jnp.float32)  7.24 us
    all_to_all x1, starting transfers between devices, local(): lax.all_to_all(results, 'expert', split_axis=0, concat_axis=0, tiled=True)  6.75 us
  transfers between devices with their start and end apart: 2, of which 2 were waited for; matrix products, arithmetic and copies ran while one was open for 0% of the time, Pallas kernels for 0%

commit v1 on v0

--- a/solution.py
+++ b/solution.py
@@ -1,9 +1,288 @@
+import functools
+
 import jax
 import jax.numpy as jnp
 from jax import lax
+from jax.experimental import pallas as pl
+from jax.experimental.pallas import tpu as pltpu
 from jax.sharding import PartitionSpec as P
 
 EXPERTS = 16
+LANES = 128
+INNER = 4
+
+
+def inner_route(count, apart):
+    return [(i, i ^ apart) for i in range(count)]
+
+
+def outer_route(count, apart):
+    return [(i, i ^ (INNER * apart)) for i in range(count)]
+
+
+def send(block, route):
+    return lax.ppermute(block, "expert", route)
+
+
+def other_core(block):
+    return lax.ppermute(block, "hsplit", [(0, 1), (1, 0)])
+
+
+def spread(block, routes):
+    return [block] + [send(block, route) for route in routes]
+
+
+def assemble(x_ref, a_refs, b_refs, rows, first):
+    for kp in range(INNER):
+        x_ref[kp * INNER * rows : (kp + 1) * INNER * rows, :first] = a_refs[kp][...]
+        for kz in range(INNER):
+            at = (kp * INNER + kz) * rows
+            x_ref[at : at + rows, first:] = b_refs[kz][
+                kp * rows : (kp + 1) * rows, : x_ref.shape[1] - first
+            ]
+
+
+def own_kernel(rows, first, where, *refs):
+    a_refs, b_refs = refs[:INNER], refs[INNER : 2 * INNER]
+    wg_ref, wu_ref, gate_ref, up_ref, x_ref = refs[2 * INNER :]
+
+    @pl.when(pl.program_id(0) == 0)
+    def _():
+        assemble(x_ref, a_refs, b_refs, rows, first)
+
+    gate_ref[...] = jnp.dot(x_ref[...], wg_ref[0], preferred_element_type=jnp.float32)
+    up_ref[...] = jnp.dot(x_ref[...], wu_ref[0], preferred_element_type=jnp.float32)
+
+
+def rest_kernel(rows, first, second, where, *refs):
+    a_refs, b_refs = refs[:INNER], refs[INNER : 2 * INNER]
+    wg_ref, wu_ref, gate_ref, up_ref, hid_ref, x_ref, scale_ref = refs[2 * INNER :]
+
+    @pl.when(pl.program_id(0) == 0)
+    def _():
+        assemble(x_ref, a_refs, b_refs, rows, first)
+        expert = where[1]
+        lane = lax.broadcasted_iota(jnp.int32, (rows, LANES), 1)
+        mine = (lane == expert) | (lane == expert + EXPERTS)
+        for kp in range(INNER):
+            for kz in range(INNER):
+                at = (kp * INNER + kz) * rows
+                extra = b_refs[kz][kp * rows : (kp + 1) * rows, second:].astype(jnp.float32)
+                total = jnp.sum(jnp.where(mine, extra, 0.0), axis=1, keepdims=True)
+                scale_ref[at : at + rows, :] = jnp.broadcast_to(total, (rows, LANES))
+
+    gate = gate_ref[...] + jnp.dot(x_ref[...], wg_ref[0], preferred_element_type=jnp.float32)
+    up = up_ref[...] + jnp.dot(x_ref[...], wu_ref[0], preferred_element_type=jnp.float32)
+    hidden = gate / (1.0 + jnp.exp(-gate)) * up * scale_ref[:, :1]
+    hid_ref[...] = hidden.astype(hid_ref.dtype)
+
+
+def down_kernel(where, hid_ref, w_ref, out_ref):
+    out_ref[...] = jnp.dot(hid_ref[...], w_ref[...], preferred_element_type=jnp.float32).astype(
+        out_ref.dtype
+    )
+
+
+def down_inner_kernel(rows, where, hid_ref, w_ref, far_ref, *out_refs):
+    total = jnp.dot(hid_ref[...], w_ref[...], preferred_element_type=jnp.float32)
+    total = (total + far_ref[...].astype(jnp.float32)).astype(jnp.bfloat16)
+    span = INNER * rows
+    for kp in range(INNER):
+        out_refs[kp][...] = total[kp * span : (kp + 1) * span]
+
+
+def down_outer_kernel(rows, where, hid_ref, w_ref, far_ref, *out_refs):
+    total = jnp.dot(hid_ref[...], w_ref[...], preferred_element_type=jnp.float32)
+    total = (total + far_ref[...].astype(jnp.float32)).astype(jnp.bfloat16)
+    for kz in range(INNER):
+        for kp in range(INNER):
+            at = (kp * INNER + kz) * rows
+            out_refs[kz][kp * rows : (kp + 1) * rows, :] = total[at : at + rows]
+
+
+def sum_split_kernel(rows, *refs):
+    total = functools.reduce(
+        jnp.add, [ref[...].astype(jnp.float32) for ref in refs[:INNER]]
+    ).astype(jnp.bfloat16)
+    for k in range(INNER):
+        refs[INNER + k][...] = total[k * rows : (k + 1) * rows]
+
+
+def sum_join_kernel(first, *refs):
+    out_ref = refs[-1]
+    for at, part in ((0, refs[:INNER]), (first, refs[INNER : 2 * INNER])):
+        total = functools.reduce(jnp.add, [ref[...].astype(jnp.float32) for ref in part])
+        out_ref[:, at : at + total.shape[1]] = total.astype(out_ref.dtype)
+
+
+def params(mib):
+    return pltpu.CompilerParams(vmem_limit_bytes=mib << 20)
+
+
+def up_call(kernel, where, pieces, gate_weight, up_weight, far, sums, out_shapes, scratch, name):
+    half = gate_weight.shape[0] // 2
+    units = gate_weight.shape[1]
+    tile = min(256, units)
+    tokens = INNER * pieces[0].shape[0]
+    whole = [pl.BlockSpec(p.shape, lambda n, w: (0, 0)) for p in pieces]
+    weight = pl.BlockSpec(
+        (1, half, tile), (lambda n, w: (1 - w[0], 0, n)) if far else (lambda n, w: (w[0], 0, n))
+    )
+    columns = pl.BlockSpec((tokens, tile), lambda n, w: (0, n))
+    flops = 2 * 2 * tokens * half * units
+    return pl.pallas_call(
+        kernel,
+        out_shape=out_shapes,
+        grid_spec=pltpu.PrefetchScalarGridSpec(
+            num_scalar_prefetch=1,
+            grid=(units // tile,),
+            in_specs=whole + [weight, weight] + [columns] * len(sums),
+            out_specs=[columns] * len(out_shapes),
+            scratch_shapes=scratch,
+        ),
+        compiler_params=params(32),
+        cost_estimate=pl.CostEstimate(
+            flops=flops, bytes_accessed=4 * half * units, transcendentals=0
+        ),
+        name=name,
+    )(
+        where,
+        *pieces,
+        gate_weight.reshape(2, half, units),
+        up_weight.reshape(2, half, units),
+        *sums,
+    )
+
+
+def down_call(kernel, where, hidden, weight, far, start, width, tile, received, out_shapes, name):
+    tokens, units = hidden.shape
+    per_half = weight.shape[1] // 2 // tile
+    base = start // tile
+    if far:
+        pick = lambda n, w: (0, (1 - w[0]) * per_half + base + n)
+    else:
+        pick = lambda n, w: (0, w[0] * per_half + base + n)
+    extra = [pl.BlockSpec((tokens, tile), lambda n, w: (0, n))] * len(received)
+    return pl.pallas_call(
+        kernel,
+        out_shape=out_shapes,
+        grid_spec=pltpu.PrefetchScalarGridSpec(
+            num_scalar_prefetch=1,
+            grid=(width // tile,),
+            in_specs=[
+                pl.BlockSpec((tokens, units), lambda n, w: (0, 0)),
+                pl.BlockSpec((units, tile), pick),
+            ]
+            + extra,
+            out_specs=[pl.BlockSpec((s.shape[0], tile), lambda n, w: (0, n)) for s in out_shapes],
+        ),
+        compiler_params=params(24),
+        cost_estimate=pl.CostEstimate(
+            flops=2 * tokens * units * width, bytes_accessed=2 * units * width, transcendentals=0
+        ),
+        name=name,
+    )(where, hidden, weight, *received)
+
+
+def local_single(tokens, routes, route_weights, gate_weight, up_weight, down_weight):
+    rows, width = tokens.shape
+    owners = lax.axis_size("expert")
+    units = gate_weight.shape[2]
+    half = width // 2
+    tile = 512
+    first = half * 5 // 7 // tile * tile
+    second = half - first
+    total_rows = owners * rows
+    core = lax.axis_index("hsplit")
+    where = jnp.stack([core, lax.axis_index("expert")]).astype(jnp.int32)
+    gate_weight, up_weight, down_weight = gate_weight[0], up_weight[0], down_weight[0]
+    by_inner = [inner_route(owners, k) for k in range(1, INNER)]
+    by_outer = [outer_route(owners, k) for k in range(1, INNER)]
+
+    named = routes[:, :, None] == jnp.arange(EXPERTS, dtype=jnp.int32)[None, None, :]
+    table = jnp.sum(jnp.where(named, route_weights[:, :, None], 0.0), axis=1)
+    high = table.astype(jnp.bfloat16)
+    low = (table - high.astype(jnp.float32)).astype(jnp.bfloat16)
+    extra = jnp.pad(jnp.concatenate([high, low], axis=1), ((0, 0), (0, LANES - 2 * EXPERTS)))
+
+    mine = lax.dynamic_slice_in_dim(tokens, core * half, half, 1)
+    a_block = mine[:, :first]
+    b_block = jnp.concatenate([mine[:, first:], extra], axis=1)
+
+    z_blocks = spread(a_block, by_outer)
+    p_blocks = spread(b_block, by_inner)
+    a_pieces = spread(jnp.concatenate(z_blocks, axis=0), by_inner)
+    b_pieces = spread(jnp.concatenate(p_blocks, axis=0), by_outer)
+    pieces = a_pieces + b_pieces
+    far_pieces = [other_core(p) for p in pieces]
+
+    f32 = functools.partial(jax.ShapeDtypeStruct, dtype=jnp.float32)
+    b16 = functools.partial(jax.ShapeDtypeStruct, dtype=jnp.bfloat16)
+    x_scratch = pltpu.VMEM((total_rows, half), jnp.bfloat16)
+    sums = up_call(
+        functools.partial(own_kernel, rows, first),
+        where,
+        pieces,
+        gate_weight,
+        up_weight,
+        False,
+        [],
+        [f32((total_rows, units))] * 2,
+        [x_scratch],
+        "own_columns",
+    )
+    (hidden,) = up_call(
+        functools.partial(rest_kernel, rows, first, second),
+        where,
+        far_pieces,
+        gate_weight,
+        up_weight,
+        True,
+        sums,
+        [b16((total_rows, units))],
+        [x_scratch, pltpu.VMEM((total_rows, LANES), jnp.float32)],
+        "other_columns",
+    )
+
+    def partial_out(start, span, name):
+        (out,) = down_call(
+            down_kernel, where, hidden, down_weight, True, start, span, tile, [],
+            [b16((total_rows, span))], name,
+        )
+        return other_core(out)
+
+    def summed_out(kernel, start, span, received, name):
+        return down_call(
+            functools.partial(kernel, rows), where, hidden, down_weight, False, start, span, tile,
+            [received], [b16((INNER * rows, span))] * INNER, name,
+        )
+
+    b_far = partial_out(first, second, "down_far_b")
+    a_far = partial_out(0, first, "down_far_a")
+    b_out = summed_out(down_outer_kernel, first, second, b_far, "down_own_b")
+    a_out = summed_out(down_inner_kernel, 0, first, a_far, "down_own_a")
+
+    def back(parts, routes_out):
+        return [parts[0]] + [send(p, r) for p, r in zip(parts[1:], routes_out)]
+
+    def sum_split(parts, span, name):
+        return pl.pallas_call(
+            functools.partial(sum_split_kernel, rows),
+            out_shape=[b16((rows, span))] * INNER,
+            compiler_params=params(16),
+            name=name,
+        )(*parts)
+
+    b_mid = sum_split(back(b_out, by_outer), second, "sum_b")
+    a_mid = sum_split(back(a_out, by_inner), first, "sum_a")
+    b_end = back(b_mid, by_inner)
+    a_end = back(a_mid, by_outer)
+    return pl.pallas_call(
+        functools.partial(sum_join_kernel, first),
+        out_shape=b16((rows, half)),
+        compiler_params=params(16),
+        name="sum_out",
+    )(*a_end, *b_end)
 
 
 def as_sent(array):
@@ -32,7 +311,7 @@
     return lax.optimization_barrier(partial_value.astype(jnp.bfloat16))
 
 
-def local(tokens, routes, route_weights, gate_weight, up_weight, down_weight):
+def local_grouped(tokens, routes, route_weights, gate_weight, up_weight, down_weight):
     tok_dev, model_width = tokens.shape
     top_k = routes.shape[1]
     owners = lax.axis_size("expert")
@@ -106,6 +385,11 @@
         P("expert", None, "hsplit"),
         P("expert", "hsplit", None),
     )
+    single = mesh.shape["expert"] == EXPERTS and mesh.shape["hsplit"] == 2
     return jax.shard_map(
-        local, mesh=mesh, in_specs=placed, out_specs=P("expert", "hsplit"), check_vma=False
-    )
+        local_single if single else local_grouped,
+        mesh=mesh,
+        in_specs=placed,
+        out_specs=P("expert", "hsplit"),
+        check_vma=False,
+    )

time: 197 us -> 108 us (0.55); the launches traced: 194 us -> 107 us
  blocking collectives: 90.7 us -> 0 us
  starting transfers between devices: 6.75 us -> 38.8 us
  matrix products: 28.5 us -> 0 us
  Pallas kernels: 0 us -> 27 us
  waiting for transfers between devices: 48.6 us -> 23.7 us
  between operations: 13.5 us -> 0.2 us
  local copies, waits for them, and re-layouts: 4.08 us -> 17.1 us
    all_to_all x1 -> x0, blocking collectives: 90.7 us -> none  [local(): lax.all_to_all(outgoing, 'expert', split_axis=0, concat_axis=0, tiled=True)]
    ppermute x0 -> x34, starting transfers between devices: none -> 38.8 us  [the longest x24 36.5 us: send(): return lax.ppermute(block, 'expert', route)]
    all_to_all x1 -> x0, waiting for transfers between devices: 38.6 us -> none  [local(): lax.all_to_all(results, 'expert', split_axis=0, concat_axis=0, tiled=True)]
    dot_general x3 -> x0, matrix products: 28.5 us -> none  [the longest x1 20.1 us: expert_rows(): jnp.dot(hidden, full_down, preferred_element_type=jnp.float32)]
    pallas_call x0 -> x9, Pallas kernels: none -> 27 us  [the longest x2 15.9 us: up_call(): pl.pallas_call(kernel, out_shape=out_shapes, grid_spec=pltpu.PrefetchScal...]
    ppermute x0 -> x34, waiting for transfers between devices: none -> 23.7 us  [the longest x24 22 us: send(): return lax.ppermute(block, 'expert', route)]
    unnamed x8 -> x10, local copies, waits for them, and re-layouts: 2.71 us -> 17.1 us
    reduce_scatter x1 -> x0, waiting for transfers between devices: 9.98 us -> none  [local(): lax.psum_scatter(partials.astype(jnp.float32).astype(jnp.bfloat16), 'hspl...]
  transfers between devices with their start and end apart: 2 -> 34, of which waited for: 2 -> 14; matrix products, arithmetic and copies ran while one was open for 0% -> 0% of each run, Pallas kernels for 0% -> 14%
where the time goes in v1:
time: 108 us; the launch traced here: 107 us
  starting transfers between devices  38.8 us (36%)
  Pallas kernels  27 us (25%)
  waiting for transfers between devices  23.7 us (22%)
  local copies, waits for them, and re-layouts  17.1 us (16%)
    ppermute x24, starting transfers between devices, send(): return lax.ppermute(block, 'expert', route)  36.5 us
    ppermute x24, waiting for transfers between devices, send(): return lax.ppermute(block, 'expert', route)  22 us
    unnamed x10, local copies, waits for them, and re-layouts  17.1 us
    pallas_call x2, Pallas kernels, up_call(): pl.pallas_call(kernel, out_shape=out_shapes, grid_spec=pltpu.PrefetchScal...  15.9 us
    pallas_call x4, Pallas kernels, down_call(): pl.pallas_call(kernel, out_shape=out_shapes, grid_spec=pltpu.PrefetchScal...  10.1 us
    ppermute x10, starting transfers between devices, other_core(): return lax.ppermute(block, 'hsplit', [(0, 1), (1, 0)])  2.3 us
  transfers between devices with their start and end apart: 34, of which 14 were waited for; matrix products, arithmetic and copies ran while one was open for 0% of the time, Pallas kernels for 14%

profile of v1, /device:TPU:0, one launch (start us, length us, event | category | flops | bytes accessed | tf_op | source)
XLA Modules:
  0.0 107.1 jit_solution(6431333976771534761)
XLA Ops:
  0.0 0.8 copy.10
  0.8 0.8 copy.9
  1.8 2.9 %collective-permute-start.10 = (bf16[16,1152]{1,0:T(8,128)(2,1)S(1)}, bf16[16,1152]{1,0:T(8,128)(2,1)S(1)}, u32[]{:S(2)}, u32[]{:S(2)}) collective-permute-start(bf16[16,1152]{1,0:T(8,128)(2,1)S(1)} %pad_maximum_fusion.2), channel_id=1, source_target_pairs={{0,2},{2,0},{4,6},{6,4},{8,10},{10,8},{12,14},{14,12},{16,18},{18,... | collective-permute-start | bytes 110600 | tf_op jit(solution)/shard_map/ppermute | solution.py:24
  4.8 1.5 %collective-permute-start.11 = (bf16[16,1152]{1,0:T(8,128)(2,1)S(1)}, bf16[16,1152]{1,0:T(8,128)(2,1)S(1)}, u32[]{:S(2)}, u32[]{:S(2)}) collective-permute-start(bf16[16,1152]{1,0:T(8,128)(2,1)S(1)} %pad_maximum_fusion.2), channel_id=1, source_target_pairs={{0,4},{2,6},{4,0},{6,2},{8,12},{10,14},{12,8},{14,10},{16,20},{18,... | collective-permute-start | bytes 110600 | tf_op jit(solution)/shard_map/ppermute | solution.py:24
  6.3 2.0 %collective-permute-start = (bf16[16,2560]{1,0:T(8,128)(2,1)S(1)}, bf16[16,2560]{1,0:T(8,128)(2,1)S(1)}, u32[]{:S(2)}, u32[]{:S(2)}) collective-permute-start(bf16[16,2560]{1,0:T(8,128)(2,1)S(1)} %constant_dynamic-slice_fusion), channel_id=1, source_target_pairs={{0,8},{2,10},{4,12},{6,14},{8,0},{10,2},{12,4},{14,6},{16,24},{18,... | collective-permute-start | bytes 245768 | tf_op jit(solution)/shard_map/ppermute | solution.py:24
  8.3 2.6 %collective-permute-start.1 = (bf16[16,2560]{1,0:T(8,128)(2,1)S(1)}, bf16[16,2560]{1,0:T(8,128)(2,1)S(1)}, u32[]{:S(2)}, u32[]{:S(2)}) collective-permute-start(bf16[16,2560]{1,0:T(8,128)(2,1)S(1)} %constant_dynamic-slice_fusion), channel_id=1, source_target_pairs={{0,16},{2,18},{4,20},{6,22},{8,24},{10,26},{12,28},{14,30},{16,0},... | collective-permute-start | bytes 245768 | tf_op jit(solution)/shard_map/ppermute | solution.py:24
  11.1 1.6 %collective-permute-start.14 = (bf16[64,1152]{1,0:T(8,128)(2,1)S(1)}, bf16[64,1152]{1,0:T(8,128)(2,1)S(1)}, u32[]{:S(2)}, u32[]{:S(2)}) collective-permute-start(bf16[64,1152]{1,0:T(8,128)(2,1)S(1)} %pad_maximum_fusion.1.refs_4_), channel_id=1, source_target_pairs={{0,8},{2,10},{4,12},{6,14},{8,0},{10,2},{12,4},{14,6},{16,24},{18,... | collective-permute-start | bytes 442376 | tf_op jit(solution)/shard_map/ppermute | solution.py:24
  12.8 2.6 %collective-permute-start.16 = (bf16[64,1152]{1,0:T(8,128)(2,1)S(1)}, bf16[64,1152]{1,0:T(8,128)(2,1)S(1)}, u32[]{:S(2)}, u32[]{:S(2)}) collective-permute-start(bf16[64,1152]{1,0:T(8,128)(2,1)S(1)} %pad_maximum_fusion.1.refs_4_), channel_id=1, source_target_pairs={{0,16},{2,18},{4,20},{6,22},{8,24},{10,26},{12,28},{14,30},{16,0},... | collective-permute-start | bytes 442376 | tf_op jit(solution)/shard_map/ppermute | solution.py:24
  15.4 1.0 collective-permute-done.1
  16.4 1.8 %collective-permute-done.2 = bf16[16,2560]{1,0:T(8,128)(2,1)S(1)} collective-permute-done((bf16[16,2560]{1,0:T(8,128)(2,1)S(1)}, bf16[16,2560]{1,0:T(8,128)(2,1)S(1)}, u32[]{:S(2)}, u32[]{:S(2)}) %collective-permute-start.2) | collective-permute-done | bytes 81952 | tf_op jit(solution)/shard_map/ppermute | solution.py:24
  18.2 1.6 %collective-permute-start.4 = (bf16[64,2560]{1,0:T(8,128)(2,1)S(1)}, bf16[64,2560]{1,0:T(8,128)(2,1)S(1)}, u32[]{:S(2)}, u32[]{:S(2)}) collective-permute-start(bf16[64,2560]{1,0:T(8,128)(2,1)S(1)} %pad_maximum_fusion.refs_0_), channel_id=1, source_target_pairs={{0,2},{2,0},{4,6},{6,4},{8,10},{10,8},{12,14},{14,12},{16,18},{18,... | collective-permute-start | bytes 983048 | tf_op jit(solution)/shard_map/ppermute | solution.py:24
  19.8 1.5 %collective-permute-start.6 = (bf16[64,2560]{1,0:T(8,128)(2,1)S(1)}, bf16[64,2560]{1,0:T(8,128)(2,1)S(1)}, u32[]{:S(2)}, u32[]{:S(2)}) collective-permute-start(bf16[64,2560]{1,0:T(8,128)(2,1)S(1)} %pad_maximum_fusion.refs_0_), channel_id=1, source_target_pairs={{0,4},{2,6},{4,0},{6,2},{8,12},{10,14},{12,8},{14,10},{16,20},{18,... | collective-permute-start | bytes 983048 | tf_op jit(solution)/shard_map/ppermute | solution.py:24
  21.8 2.2 %collective-permute-start.18 = (bf16[64,1152]{1,0:T(8,128)(2,1)S(1)}, bf16[64,1152]{1,0:T(8,128)(2,1)S(1)}, u32[]{:S(2)}, u32[]{:S(2)}) collective-permute-start(bf16[64,1152]{1,0:T(8,128)(2,1)S(1)} %pad_maximum_fusion.1.refs_4_), channel_id=1, source_target_pairs={{0,24},{2,26},{4,28},{6,30},{8,16},{10,18},{12,20},{14,22},{16,8},... | collective-permute-start | bytes 442376 | tf_op jit(solution)/shard_map/ppermute | solution.py:24
  24.0 2.9 %collective-permute-done.16.refs_6_ = bf16[64,1152]{1,0:T(8,128)(2,1)S(1)} collective-permute-done((bf16[64,1152]{1,0:T(8,128)(2,1)S(1)}, bf16[64,1152]{1,0:T(8,128)(2,1)S(1)}, u32[]{:S(2)}, u32[]{:S(2)}) %collective-permute-start.16) | collective-permute-done | bytes 147488 | tf_op jit(solution)/shard_map/ppermute | solution.py:24
  26.9 1.8 %collective-permute-done.18.refs_7_ = bf16[64,1152]{1,0:T(8,128)(2,1)S(1)} collective-permute-done((bf16[64,1152]{1,0:T(8,128)(2,1)S(1)}, bf16[64,1152]{1,0:T(8,128)(2,1)S(1)}, u32[]{:S(2)}, u32[]{:S(2)}) %collective-permute-start.18) | collective-permute-done | bytes 147488 | tf_op jit(solution)/shard_map/ppermute | solution.py:24
  28.7 0.5 collective-permute-start.17
  29.3 0.8 collective-permute-done.15.refs_5_
  30.8 2.0 %collective-permute-done.6.refs_2_ = bf16[64,2560]{1,0:T(8,128)(2,1)S(1)} collective-permute-done((bf16[64,2560]{1,0:T(8,128)(2,1)S(1)}, bf16[64,2560]{1,0:T(8,128)(2,1)S(1)}, u32[]{:S(2)}, u32[]{:S(2)}) %collective-permute-start.6) | collective-permute-done | bytes 327712 | tf_op jit(solution)/shard_map/ppermute | solution.py:24
  32.9 0.5 collective-permute-start.9
  33.4 5.2 %copy-done.2 = bf16[1,7168,1024]{2,1,0:T(8,128)(2,1)S(1)} copy-done((bf16[1,7168,1024]{2,1,0:T(8,128)(2,1)S(1)}, bf16[1,7168,1024]{2,1,0:T(8,128)(2,1)}, u32[]{:S(2)}) %copy-start.2) | copy-done | bytes 14680088
  38.6 7.9 %own_columns.1 = (f32[256,1024]{1,0:T(8,128)S(1)}, f32[256,1024]{1,0:T(8,128)S(1)}) custom-call(s32[2]{0:T(128)S(1)} %pad_add_fusion.where, bf16[64,2560]{1,0:T(8,128)(2,1)S(1)} %pad_maximum_fusion.refs_0_, bf16[64,2560]{1,0:T(8,128)(2,1)S(1)} %collective-permute-done.4.refs_1_, bf16[64,2560]{1,0:T(8,128)(2,1)S(1)} %collective-permute-done.6.refs_2_, ...), custom_call_target="tpu_custom_call" | custom-call | flops 3758096384 | bytes 14680064 | tf_op jit(solution)/shard_map/own_columns/pallas_call | solution.py:133
  46.6 5.2 %copy-done.3 = bf16[1,7168,1024]{2,1,0:T(8,128)(2,1)S(1)} copy-done((bf16[1,7168,1024]{2,1,0:T(8,128)(2,1)S(1)}, bf16[1,7168,1024]{2,1,0:T(8,128)(2,1)}, u32[]{:S(2)}) %copy-start.3) | copy-done | bytes 14680088
  51.7 8.0 %other_columns.1.hid_ref = bf16[256,1024]{1,0:T(8,128)(2,1)S(1)} custom-call(s32[2]{0:T(128)S(1)} %pad_add_fusion.where, bf16[64,2560]{1,0:T(8,128)(2,1)S(1)} %collective-permute-done.3.refs_0_, bf16[64,2560]{1,0:T(8,128)(2,1)S(1)} %collective-permute-done.5.refs_1_, bf16[64,2560]{1,0:T(8,128)(2,1)S(1)} %collective-permute-done.7.refs_2_, ...), custom_call_target="tpu_custom_call" | custom-call | flops 3758096384 | bytes 14680064 | tf_op jit(solution)/shard_map/other_columns/pallas_call | solution.py:133
  59.7 5.2 %copy-done.1 = bf16[1,1024,7168]{2,1,0:T(8,128)(2,1)S(1)} copy-done((bf16[1,1024,7168]{2,1,0:T(8,128)(2,1)S(1)}, bf16[1,1024,7168]{2,1,0:T(8,128)(2,1)}, u32[]{:S(2)}) %copy-start.1) | copy-done | bytes 14680088
  64.9 3.3 %down_far_a.1 = bf16[256,2560]{1,0:T(8,128)(2,1)S(1)} custom-call(s32[2]{0:T(128)S(1)} %pad_add_fusion.where, bf16[256,1024]{1,0:T(8,128)(2,1)S(1)} %other_columns.1.hid_ref, bf16[1024,7168]{1,0:T(8,128)(2,1)S(1)} %bitcast.5), custom_call_target="tpu_custom_call" | custom-call | flops 1342177280 | bytes 5242880 | tf_op jit(solution)/shard_map/down_far_a/pallas_call | solution.py:166
  68.3 1.7 %down_far_b.1 = bf16[256,1024]{1,0:T(8,128)(2,1)S(1)} custom-call(s32[2]{0:T(128)S(1)} %pad_add_fusion.where, bf16[256,1024]{1,0:T(8,128)(2,1)S(1)} %other_columns.1.hid_ref, bf16[1024,7168]{1,0:T(8,128)(2,1)S(1)} %bitcast.6), custom_call_target="tpu_custom_call" | custom-call | flops 536870912 | bytes 2097152 | tf_op jit(solution)/shard_map/down_far_b/pallas_call | solution.py:166
  70.0 0.6 collective-permute-start.27
  70.5 0.8 collective-permute-done.20.far_ref
  71.3 3.4 %down_own_a.1 = (bf16[64,2560]{1,0:T(8,128)(2,1)S(1)}, bf16[64,2560]{1,0:T(8,128)(2,1)S(1)}, bf16[64,2560]{1,0:T(8,128)(2,1)S(1)}, bf16[64,2560]{1,0:T(8,128)(2,1)S(1)}) custom-call(s32[2]{0:T(128)S(1)} %pad_add_fusion.where, bf16[256,1024]{1,0:T(8,128)(2,1)S(1)} %other_columns.1.hid_ref, bf16[1024,7168]{1,0:T(8,128)(2,1)S(1)} %bitcast.7, ...), custom_call_target="tpu_custom_call" | custom-call | flops 1342177280 | bytes 5242880 | tf_op jit(solution)/shard_map/down_own_a/pallas_call | solution.py:166
  74.8 0.9 collective-permute-start.21
  75.7 1.2 %collective-permute-start.22 = (bf16[64,2560]{1,0:T(8,128)(2,1)S(1)}, bf16[64,2560]{1,0:T(8,128)(2,1)S(1)}, u32[]{:S(2)}, u32[]{:S(2)}) collective-permute-start(bf16[64,2560]{1,0:T(8,128)(2,1)S(1)} %get-tuple-element.27), channel_id=1, source_target_pairs={{0,4},{2,6},{4,0},{6,2},{8,12},{10,14},{12,8},{14,10},{16,20},{18,... | collective-permute-start | bytes 983048 | tf_op jit(solution)/shard_map/ppermute | solution.py:24
  76.9 1.4 %collective-permute-start.23 = (bf16[64,2560]{1,0:T(8,128)(2,1)S(1)}, bf16[64,2560]{1,0:T(8,128)(2,1)S(1)}, u32[]{:S(2)}, u32[]{:S(2)}) collective-permute-start(bf16[64,2560]{1,0:T(8,128)(2,1)S(1)} %get-tuple-element.28), channel_id=1, source_target_pairs={{0,6},{2,4},{4,2},{6,0},{8,14},{10,12},{12,10},{14,8},{16,22},{18,... | collective-permute-start | bytes 983048 | tf_op jit(solution)/shard_map/ppermute | solution.py:24
  78.3 1.7 %down_own_b.1 = (bf16[64,1024]{1,0:T(8,128)(2,1)S(1)}, bf16[64,1024]{1,0:T(8,128)(2,1)S(1)}, bf16[64,1024]{1,0:T(8,128)(2,1)S(1)}, bf16[64,1024]{1,0:T(8,128)(2,1)S(1)}) custom-call(s32[2]{0:T(128)S(1)} %pad_add_fusion.where, bf16[256,1024]{1,0:T(8,128)(2,1)S(1)} %other_columns.1.hid_ref, bf16[1024,7168]{1,0:T(8,128)(2,1)S(1)} %bitcast.8, ...), custom_call_target="tpu_custom_call" | custom-call | flops 536870912 | bytes 2097152 | tf_op jit(solution)/shard_map/down_own_b/pallas_call | solution.py:166
  80.1 1.3 %collective-permute-start.28 = (bf16[64,1024]{1,0:T(8,128)(2,1)S(1)}, bf16[64,1024]{1,0:T(8,128)(2,1)S(1)}, u32[]{:S(2)}, u32[]{:S(2)}) collective-permute-start(bf16[64,1024]{1,0:T(8,128)(2,1)S(1)} %get-tuple-element.34), channel_id=1, source_target_pairs={{0,8},{2,10},{4,12},{6,14},{8,0},{10,2},{12,4},{14,6},{16,24},{18,... | collective-permute-start | bytes 393224 | tf_op jit(solution)/shard_map/ppermute | solution.py:24
  81.4 2.1 %collective-permute-start.29 = (bf16[64,1024]{1,0:T(8,128)(2,1)S(1)}, bf16[64,1024]{1,0:T(8,128)(2,1)S(1)}, u32[]{:S(2)}, u32[]{:S(2)}) collective-permute-start(bf16[64,1024]{1,0:T(8,128)(2,1)S(1)} %get-tuple-element.35), channel_id=1, source_target_pairs={{0,16},{2,18},{4,20},{6,22},{8,24},{10,26},{12,28},{14,30},{16,0},... | collective-permute-start | bytes 393224 | tf_op jit(solution)/shard_map/ppermute | solution.py:24
  83.5 1.9 %collective-permute-done.21.refs_1_ = bf16[64,2560]{1,0:T(8,128)(2,1)S(1)} collective-permute-done((bf16[64,2560]{1,0:T(8,128)(2,1)S(1)}, bf16[64,2560]{1,0:T(8,128)(2,1)S(1)}, u32[]{:S(2)}, u32[]{:S(2)}) %collective-permute-start.21) | collective-permute-done | bytes 327712 | tf_op jit(solution)/shard_map/ppermute | solution.py:24
  85.4 1.5 %collective-permute-start.30 = (bf16[64,1024]{1,0:T(8,128)(2,1)S(1)}, bf16[64,1024]{1,0:T(8,128)(2,1)S(1)}, u32[]{:S(2)}, u32[]{:S(2)}) collective-permute-start(bf16[64,1024]{1,0:T(8,128)(2,1)S(1)} %get-tuple-element.36), channel_id=1, source_target_pairs={{0,24},{2,26},{4,28},{6,30},{8,16},{10,18},{12,20},{14,22},{16,8},... | collective-permute-start | bytes 393224 | tf_op jit(solution)/shard_map/ppermute | solution.py:24
  86.8 4.1 %collective-permute-done.22.refs_2_ = bf16[64,2560]{1,0:T(8,128)(2,1)S(1)} collective-permute-done((bf16[64,2560]{1,0:T(8,128)(2,1)S(1)}, bf16[64,2560]{1,0:T(8,128)(2,1)S(1)}, u32[]{:S(2)}, u32[]{:S(2)}) %collective-permute-start.22) | collective-permute-done | bytes 327712 | tf_op jit(solution)/shard_map/ppermute | solution.py:24
  90.9 1.6 %collective-permute-done.23.refs_3_ = bf16[64,2560]{1,0:T(8,128)(2,1)S(1)} collective-permute-done((bf16[64,2560]{1,0:T(8,128)(2,1)S(1)}, bf16[64,2560]{1,0:T(8,128)(2,1)S(1)}, u32[]{:S(2)}, u32[]{:S(2)}) %collective-permute-start.23) | collective-permute-done | bytes 327712 | tf_op jit(solution)/shard_map/ppermute | solution.py:24
  92.7 1.3 %collective-permute-start.24 = (bf16[16,2560]{1,0:T(8,128)(2,1)S(1)}, bf16[16,2560]{1,0:T(8,128)(2,1)S(1)}, u32[]{:S(2)}, u32[]{:S(2)}) collective-permute-start(bf16[16,2560]{1,0:T(8,128)(2,1)S(1)} %get-tuple-element.30), channel_id=1, source_target_pairs={{0,8},{2,10},{4,12},{6,14},{8,0},{10,2},{12,4},{14,6},{16,24},{18,... | collective-permute-start | bytes 245768 | tf_op jit(solution)/shard_map/ppermute | solution.py:24
  94.0 2.1 %collective-permute-start.25 = (bf16[16,2560]{1,0:T(8,128)(2,1)S(1)}, bf16[16,2560]{1,0:T(8,128)(2,1)S(1)}, u32[]{:S(2)}, u32[]{:S(2)}) collective-permute-start(bf16[16,2560]{1,0:T(8,128)(2,1)S(1)} %get-tuple-element.31), channel_id=1, source_target_pairs={{0,16},{2,18},{4,20},{6,22},{8,24},{10,26},{12,28},{14,30},{16,0},... | collective-permute-start | bytes 245768 | tf_op jit(solution)/shard_map/ppermute | solution.py:24
  96.1 1.4 %collective-permute-start.26 = (bf16[16,2560]{1,0:T(8,128)(2,1)S(1)}, bf16[16,2560]{1,0:T(8,128)(2,1)S(1)}, u32[]{:S(2)}, u32[]{:S(2)}) collective-permute-start(bf16[16,2560]{1,0:T(8,128)(2,1)S(1)} %get-tuple-element.32), channel_id=1, source_target_pairs={{0,24},{2,26},{4,28},{6,30},{8,16},{10,18},{12,20},{14,22},{16,8},... | collective-permute-start | bytes 245768 | tf_op jit(solution)/shard_map/ppermute | solution.py:24
  97.6 0.9 collective-permute-start.31
  98.5 1.5 %collective-permute-start.32 = (bf16[16,1024]{1,0:T(8,128)(2,1)S(1)}, bf16[16,1024]{1,0:T(8,128)(2,1)S(1)}, u32[]{:S(2)}, u32[]{:S(2)}) collective-permute-start(bf16[16,1024]{1,0:T(8,128)(2,1)S(1)} %get-tuple-element.39), channel_id=1, source_target_pairs={{0,4},{2,6},{4,0},{6,2},{8,12},{10,14},{12,8},{14,10},{16,20},{18,... | collective-permute-start | bytes 98312 | tf_op jit(solution)/shard_map/ppermute | solution.py:24
  100.0 1.6 %collective-permute-done.31.refs_5_ = bf16[16,1024]{1,0:T(8,128)(2,1)S(1)} collective-permute-done((bf16[16,1024]{1,0:T(8,128)(2,1)S(1)}, bf16[16,1024]{1,0:T(8,128)(2,1)S(1)}, u32[]{:S(2)}, u32[]{:S(2)}) %collective-permute-start.31) | collective-permute-done | bytes 32800 | tf_op jit(solution)/shard_map/ppermute | solution.py:24
  101.6 1.8 %collective-permute-start.33 = (bf16[16,1024]{1,0:T(8,128)(2,1)S(1)}, bf16[16,1024]{1,0:T(8,128)(2,1)S(1)}, u32[]{:S(2)}, u32[]{:S(2)}) collective-permute-start(bf16[16,1024]{1,0:T(8,128)(2,1)S(1)} %get-tuple-element.40), channel_id=1, source_target_pairs={{0,6},{2,4},{4,2},{6,0},{8,14},{10,12},{12,10},{14,8},{16,22},{18,... | collective-permute-start | bytes 98312 | tf_op jit(solution)/shard_map/ppermute | solution.py:24
  103.3 3.1 %collective-permute-done.33.refs_7_ = bf16[16,1024]{1,0:T(8,128)(2,1)S(1)} collective-permute-done((bf16[16,1024]{1,0:T(8,128)(2,1)S(1)}, bf16[16,1024]{1,0:T(8,128)(2,1)S(1)}, u32[]{:S(2)}, u32[]{:S(2)}) %collective-permute-start.33) | collective-permute-done | bytes 32800 | tf_op jit(solution)/shard_map/ppermute | solution.py:24
  106.4 0.7 sum_out.1
  (48 shorter events, 2.1 us)
Async XLA Ops:
  0.0 1.7 %copy-start = (bf16[16,7168]{1,0:T(8,128)(2,1)S(1)}, bf16[16,7168]{1,0:T(8,128)(2,1)}, u32[]{:S(2)}) copy-start(bf16[16,7168]{1,0:T(8,128)(2,1)} %param.6) | copy-start | bytes 688132
  1.8 9.1 %collective-permute-start.10 = (bf16[16,1152]{1,0:T(8,128)(2,1)S(1)}, bf16[16,1152]{1,0:T(8,128)(2,1)S(1)}, u32[]{:S(2)}, u32[]{:S(2)}) collective-permute-start(bf16[16,1152]{1,0:T(8,128)(2,1)S(1)} %pad_maximum_fusion.2), channel_id=1, source_target_pairs={{0,2},{2,0},{4,6},{6,4},{8,10},{10,8},{12,14},{14,12},{16,18},{18,... | collective-permute-start | bytes 110600 | tf_op jit(solution)/shard_map/ppermute | solution.py:24
  4.8 6.2 %collective-permute-start.11 = (bf16[16,1152]{1,0:T(8,128)(2,1)S(1)}, bf16[16,1152]{1,0:T(8,128)(2,1)S(1)}, u32[]{:S(2)}, u32[]{:S(2)}) collective-permute-start(bf16[16,1152]{1,0:T(8,128)(2,1)S(1)} %pad_maximum_fusion.2), channel_id=1, source_target_pairs={{0,4},{2,6},{4,0},{6,2},{8,12},{10,14},{12,8},{14,10},{16,20},{18,... | collective-permute-start | bytes 110600 | tf_op jit(solution)/shard_map/ppermute | solution.py:24
  6.3 4.9 %collective-permute-start.12 = (bf16[16,1152]{1,0:T(8,128)(2,1)S(1)}, bf16[16,1152]{1,0:T(8,128)(2,1)S(1)}, u32[]{:S(2)}, u32[]{:S(2)}) collective-permute-start(bf16[16,1152]{1,0:T(8,128)(2,1)S(1)} %pad_maximum_fusion.2), channel_id=1, source_target_pairs={{0,6},{2,4},{4,2},{6,0},{8,14},{10,12},{12,10},{14,8},{16,22},{18,... | collective-permute-start | bytes 110600 | tf_op jit(solution)/shard_map/ppermute | solution.py:24
  6.3 9.1 %collective-permute-start = (bf16[16,2560]{1,0:T(8,128)(2,1)S(1)}, bf16[16,2560]{1,0:T(8,128)(2,1)S(1)}, u32[]{:S(2)}, u32[]{:S(2)}) collective-permute-start(bf16[16,2560]{1,0:T(8,128)(2,1)S(1)} %constant_dynamic-slice_fusion), channel_id=1, source_target_pairs={{0,8},{2,10},{4,12},{6,14},{8,0},{10,2},{12,4},{14,6},{16,24},{18,... | collective-permute-start | bytes 245768 | tf_op jit(solution)/shard_map/ppermute | solution.py:24
  8.3 8.1 %collective-permute-start.1 = (bf16[16,2560]{1,0:T(8,128)(2,1)S(1)}, bf16[16,2560]{1,0:T(8,128)(2,1)S(1)}, u32[]{:S(2)}, u32[]{:S(2)}) collective-permute-start(bf16[16,2560]{1,0:T(8,128)(2,1)S(1)} %constant_dynamic-slice_fusion), channel_id=1, source_target_pairs={{0,16},{2,18},{4,20},{6,22},{8,24},{10,26},{12,28},{14,30},{16,0},... | collective-permute-start | bytes 245768 | tf_op jit(solution)/shard_map/ppermute | solution.py:24
  10.9 7.3 %collective-permute-start.2 = (bf16[16,2560]{1,0:T(8,128)(2,1)S(1)}, bf16[16,2560]{1,0:T(8,128)(2,1)S(1)}, u32[]{:S(2)}, u32[]{:S(2)}) collective-permute-start(bf16[16,2560]{1,0:T(8,128)(2,1)S(1)} %constant_dynamic-slice_fusion), channel_id=1, source_target_pairs={{0,24},{2,26},{4,28},{6,30},{8,16},{10,18},{12,20},{14,22},{16,8},... | collective-permute-start | bytes 245768 | tf_op jit(solution)/shard_map/ppermute | solution.py:24
  11.1 10.6 %collective-permute-start.14 = (bf16[64,1152]{1,0:T(8,128)(2,1)S(1)}, bf16[64,1152]{1,0:T(8,128)(2,1)S(1)}, u32[]{:S(2)}, u32[]{:S(2)}) collective-permute-start(bf16[64,1152]{1,0:T(8,128)(2,1)S(1)} %pad_maximum_fusion.1.refs_4_), channel_id=1, source_target_pairs={{0,8},{2,10},{4,12},{6,14},{8,0},{10,2},{12,4},{14,6},{16,24},{18,... | collective-permute-start | bytes 442376 | tf_op jit(solution)/shard_map/ppermute | solution.py:24
  12.8 14.1 %collective-permute-start.16 = (bf16[64,1152]{1,0:T(8,128)(2,1)S(1)}, bf16[64,1152]{1,0:T(8,128)(2,1)S(1)}, u32[]{:S(2)}, u32[]{:S(2)}) collective-permute-start(bf16[64,1152]{1,0:T(8,128)(2,1)S(1)} %pad_maximum_fusion.1.refs_4_), channel_id=1, source_target_pairs={{0,16},{2,18},{4,20},{6,22},{8,24},{10,26},{12,28},{14,30},{16,0},... | collective-permute-start | bytes 442376 | tf_op jit(solution)/shard_map/ppermute | solution.py:24
  18.2 12.4 %collective-permute-start.4 = (bf16[64,2560]{1,0:T(8,128)(2,1)S(1)}, bf16[64,2560]{1,0:T(8,128)(2,1)S(1)}, u32[]{:S(2)}, u32[]{:S(2)}) collective-permute-start(bf16[64,2560]{1,0:T(8,128)(2,1)S(1)} %pad_maximum_fusion.refs_0_), channel_id=1, source_target_pairs={{0,2},{2,0},{4,6},{6,4},{8,10},{10,8},{12,14},{14,12},{16,18},{18,... | collective-permute-start | bytes 983048 | tf_op jit(solution)/shard_map/ppermute | solution.py:24
  19.8 13.1 %collective-permute-start.6 = (bf16[64,2560]{1,0:T(8,128)(2,1)S(1)}, bf16[64,2560]{1,0:T(8,128)(2,1)S(1)}, u32[]{:S(2)}, u32[]{:S(2)}) collective-permute-start(bf16[64,2560]{1,0:T(8,128)(2,1)S(1)} %pad_maximum_fusion.refs_0_), channel_id=1, source_target_pairs={{0,4},{2,6},{4,0},{6,2},{8,12},{10,14},{12,8},{14,10},{16,20},{18,... | collective-permute-start | bytes 983048 | tf_op jit(solution)/shard_map/ppermute | solution.py:24
  21.3 11.6 %collective-permute-start.8 = (bf16[64,2560]{1,0:T(8,128)(2,1)S(1)}, bf16[64,2560]{1,0:T(8,128)(2,1)S(1)}, u32[]{:S(2)}, u32[]{:S(2)}) collective-permute-start(bf16[64,2560]{1,0:T(8,128)(2,1)S(1)} %pad_maximum_fusion.refs_0_), channel_id=1, source_target_pairs={{0,6},{2,4},{4,2},{6,0},{8,14},{10,12},{12,10},{14,8},{16,22},{18,... | collective-permute-start | bytes 983048 | tf_op jit(solution)/shard_map/ppermute | solution.py:24
  21.8 6.9 %collective-permute-start.18 = (bf16[64,1152]{1,0:T(8,128)(2,1)S(1)}, bf16[64,1152]{1,0:T(8,128)(2,1)S(1)}, u32[]{:S(2)}, u32[]{:S(2)}) collective-permute-start(bf16[64,1152]{1,0:T(8,128)(2,1)S(1)} %pad_maximum_fusion.1.refs_4_), channel_id=1, source_target_pairs={{0,24},{2,26},{4,28},{6,30},{8,16},{10,18},{12,20},{14,22},{16,8},... | collective-permute-start | bytes 442376 | tf_op jit(solution)/shard_map/ppermute | solution.py:24
  26.9 1.8 %collective-permute-start.13 = (bf16[64,1152]{1,0:T(8,128)(2,1)S(1)}, bf16[64,1152]{1,0:T(8,128)(2,1)S(1)}, u32[]{:S(2)}, u32[]{:S(2)}) collective-permute-start(bf16[64,1152]{1,0:T(8,128)(2,1)S(1)} %pad_maximum_fusion.1.refs_4_), channel_id=1, source_target_pairs={{0,1},{1,0},{2,3},{3,2},{4,5},{5,4},{6,7},{7,6},{8,9},{9,8},{10,11... | collective-permute-start | bytes 442376 | tf_op jit(solution)/shard_map/ppermute | solution.py:28
  28.7 1.4 %collective-permute-start.15 = (bf16[64,1152]{1,0:T(8,128)(2,1)S(1)}, bf16[64,1152]{1,0:T(8,128)(2,1)S(1)}, u32[]{:S(2)}, u32[]{:S(2)}) collective-permute-start(bf16[64,1152]{1,0:T(8,128)(2,1)S(1)} %collective-permute-done.14.refs_5_), channel_id=1, source_target_pairs={{0,1},{1,0},{2,3},{3,2},{4,5},{5,4},{6,7},{7,6},{8,9},{9,8},{10,11... | collective-permute-start | bytes 442376 | tf_op jit(solution)/shard_map/ppermute | solution.py:28
  28.7 1.6 %collective-permute-start.17 = (bf16[64,1152]{1,0:T(8,128)(2,1)S(1)}, bf16[64,1152]{1,0:T(8,128)(2,1)S(1)}, u32[]{:S(2)}, u32[]{:S(2)}) collective-permute-start(bf16[64,1152]{1,0:T(8,128)(2,1)S(1)} %collective-permute-done.16.refs_6_), channel_id=1, source_target_pairs={{0,1},{1,0},{2,3},{3,2},{4,5},{5,4},{6,7},{7,6},{8,9},{9,8},{10,11... | collective-permute-start | bytes 442376 | tf_op jit(solution)/shard_map/ppermute | solution.py:28
  30.1 16.4 %collective-permute-start.3 = (bf16[64,2560]{1,0:T(8,128)(2,1)S(1)}, bf16[64,2560]{1,0:T(8,128)(2,1)S(1)}, u32[]{:S(2)}, u32[]{:S(2)}) collective-permute-start(bf16[64,2560]{1,0:T(8,128)(2,1)S(1)} %pad_maximum_fusion.refs_0_), channel_id=1, source_target_pairs={{0,1},{1,0},{2,3},{3,2},{4,5},{5,4},{6,7},{7,6},{8,9},{9,8},{10,11... | collective-permute-start | bytes 983048 | tf_op jit(solution)/shard_map/ppermute | solution.py:28
  30.3 16.2 %collective-permute-start.19 = (bf16[64,1152]{1,0:T(8,128)(2,1)S(1)}, bf16[64,1152]{1,0:T(8,128)(2,1)S(1)}, u32[]{:S(2)}, u32[]{:S(2)}) collective-permute-start(bf16[64,1152]{1,0:T(8,128)(2,1)S(1)} %collective-permute-done.18.refs_7_), channel_id=1, source_target_pairs={{0,1},{1,0},{2,3},{3,2},{4,5},{5,4},{6,7},{7,6},{8,9},{9,8},{10,11... | collective-permute-start | bytes 442376 | tf_op jit(solution)/shard_map/ppermute | solution.py:28
  30.6 15.9 %collective-permute-start.5 = (bf16[64,2560]{1,0:T(8,128)(2,1)S(1)}, bf16[64,2560]{1,0:T(8,128)(2,1)S(1)}, u32[]{:S(2)}, u32[]{:S(2)}) collective-permute-start(bf16[64,2560]{1,0:T(8,128)(2,1)S(1)} %collective-permute-done.4.refs_1_), channel_id=1, source_target_pairs={{0,1},{1,0},{2,3},{3,2},{4,5},{5,4},{6,7},{7,6},{8,9},{9,8},{10,11... | collective-permute-start | bytes 983048 | tf_op jit(solution)/shard_map/ppermute | solution.py:28
  32.9 13.7 %collective-permute-start.7 = (bf16[64,2560]{1,0:T(8,128)(2,1)S(1)}, bf16[64,2560]{1,0:T(8,128)(2,1)S(1)}, u32[]{:S(2)}, u32[]{:S(2)}) collective-permute-start(bf16[64,2560]{1,0:T(8,128)(2,1)S(1)} %collective-permute-done.6.refs_2_), channel_id=1, source_target_pairs={{0,1},{1,0},{2,3},{3,2},{4,5},{5,4},{6,7},{7,6},{8,9},{9,8},{10,11... | collective-permute-start | bytes 983048 | tf_op jit(solution)/shard_map/ppermute | solution.py:28
  32.9 13.7 %collective-permute-start.9 = (bf16[64,2560]{1,0:T(8,128)(2,1)S(1)}, bf16[64,2560]{1,0:T(8,128)(2,1)S(1)}, u32[]{:S(2)}, u32[]{:S(2)}) collective-permute-start(bf16[64,2560]{1,0:T(8,128)(2,1)S(1)} %collective-permute-done.8.refs_3_), channel_id=1, source_target_pairs={{0,1},{1,0},{2,3},{3,2},{4,5},{5,4},{6,7},{7,6},{8,9},{9,8},{10,11... | collective-permute-start | bytes 983048 | tf_op jit(solution)/shard_map/ppermute | solution.py:28
  33.4 5.2 %copy-start.2 = (bf16[1,7168,1024]{2,1,0:T(8,128)(2,1)S(1)}, bf16[1,7168,1024]{2,1,0:T(8,128)(2,1)}, u32[]{:S(2)}) copy-start(bf16[1,7168,1024]{2,1,0:T(8,128)(2,1)} %param.9) | copy-start | bytes 44040196
  46.5 5.2 %copy-start.3 = (bf16[1,7168,1024]{2,1,0:T(8,128)(2,1)S(1)}, bf16[1,7168,1024]{2,1,0:T(8,128)(2,1)}, u32[]{:S(2)}) copy-start(bf16[1,7168,1024]{2,1,0:T(8,128)(2,1)} %param.9) | copy-start | bytes 44040196
  59.7 5.2 %copy-start.1 = (bf16[1,1024,7168]{2,1,0:T(8,128)(2,1)S(1)}, bf16[1,1024,7168]{2,1,0:T(8,128)(2,1)}, u32[]{:S(2)}) copy-start(bf16[1,1024,7168]{2,1,0:T(8,128)(2,1)} %param.11) | copy-start | bytes 44040196
  68.2 3.1 %collective-permute-start.20 = (bf16[256,2560]{1,0:T(8,128)(2,1)S(1)}, bf16[256,2560]{1,0:T(8,128)(2,1)S(1)}, u32[]{:S(2)}, u32[]{:S(2)}) collective-permute-start(bf16[256,2560]{1,0:T(8,128)(2,1)S(1)} %down_far_a.1), channel_id=1, source_target_pairs={{0,1},{1,0},{2,3},{3,2},{4,5},{5,4},{6,7},{7,6},{8,9},{9,8},{10,11... | collective-permute-start | bytes 3932168 | tf_op jit(solution)/shard_map/ppermute | solution.py:28
  70.0 8.4 %collective-permute-start.27 = (bf16[256,1024]{1,0:T(8,128)(2,1)S(1)}, bf16[256,1024]{1,0:T(8,128)(2,1)S(1)}, u32[]{:S(2)}, u32[]{:S(2)}) collective-permute-start(bf16[256,1024]{1,0:T(8,128)(2,1)S(1)} %down_far_b.1), channel_id=1, source_target_pairs={{0,1},{1,0},{2,3},{3,2},{4,5},{5,4},{6,7},{7,6},{8,9},{9,8},{10,11... | collective-permute-start | bytes 1572872 | tf_op jit(solution)/shard_map/ppermute | solution.py:28
  74.8 10.6 %collective-permute-start.21 = (bf16[64,2560]{1,0:T(8,128)(2,1)S(1)}, bf16[64,2560]{1,0:T(8,128)(2,1)S(1)}, u32[]{:S(2)}, u32[]{:S(2)}) collective-permute-start(bf16[64,2560]{1,0:T(8,128)(2,1)S(1)} %get-tuple-element.26), channel_id=1, source_target_pairs={{0,2},{2,0},{4,6},{6,4},{8,10},{10,8},{12,14},{14,12},{16,18},{18,... | collective-permute-start | bytes 983048 | tf_op jit(solution)/shard_map/ppermute | solution.py:24
  75.7 15.2 %collective-permute-start.22 = (bf16[64,2560]{1,0:T(8,128)(2,1)S(1)}, bf16[64,2560]{1,0:T(8,128)(2,1)S(1)}, u32[]{:S(2)}, u32[]{:S(2)}) collective-permute-start(bf16[64,2560]{1,0:T(8,128)(2,1)S(1)} %get-tuple-element.27), channel_id=1, source_target_pairs={{0,4},{2,6},{4,0},{6,2},{8,12},{10,14},{12,8},{14,10},{16,20},{18,... | collective-permute-start | bytes 983048 | tf_op jit(solution)/shard_map/ppermute | solution.py:24
  76.9 15.7 %collective-permute-start.23 = (bf16[64,2560]{1,0:T(8,128)(2,1)S(1)}, bf16[64,2560]{1,0:T(8,128)(2,1)S(1)}, u32[]{:S(2)}, u32[]{:S(2)}) collective-permute-start(bf16[64,2560]{1,0:T(8,128)(2,1)S(1)} %get-tuple-element.28), channel_id=1, source_target_pairs={{0,6},{2,4},{4,2},{6,0},{8,14},{10,12},{12,10},{14,8},{16,22},{18,... | collective-permute-start | bytes 983048 | tf_op jit(solution)/shard_map/ppermute | solution.py:24
  80.1 16.1 %collective-permute-start.28 = (bf16[64,1024]{1,0:T(8,128)(2,1)S(1)}, bf16[64,1024]{1,0:T(8,128)(2,1)S(1)}, u32[]{:S(2)}, u32[]{:S(2)}) collective-permute-start(bf16[64,1024]{1,0:T(8,128)(2,1)S(1)} %get-tuple-element.34), channel_id=1, source_target_pairs={{0,8},{2,10},{4,12},{6,14},{8,0},{10,2},{12,4},{14,6},{16,24},{18,... | collective-permute-start | bytes 393224 | tf_op jit(solution)/shard_map/ppermute | solution.py:24
  81.4 16.1 %collective-permute-start.29 = (bf16[64,1024]{1,0:T(8,128)(2,1)S(1)}, bf16[64,1024]{1,0:T(8,128)(2,1)S(1)}, u32[]{:S(2)}, u32[]{:S(2)}) collective-permute-start(bf16[64,1024]{1,0:T(8,128)(2,1)S(1)} %get-tuple-element.35), channel_id=1, source_target_pairs={{0,16},{2,18},{4,20},{6,22},{8,24},{10,26},{12,28},{14,30},{16,0},... | collective-permute-start | bytes 393224 | tf_op jit(solution)/shard_map/ppermute | solution.py:24
  85.4 12.1 %collective-permute-start.30 = (bf16[64,1024]{1,0:T(8,128)(2,1)S(1)}, bf16[64,1024]{1,0:T(8,128)(2,1)S(1)}, u32[]{:S(2)}, u32[]{:S(2)}) collective-permute-start(bf16[64,1024]{1,0:T(8,128)(2,1)S(1)} %get-tuple-element.36), channel_id=1, source_target_pairs={{0,24},{2,26},{4,28},{6,30},{8,16},{10,18},{12,20},{14,22},{16,8},... | collective-permute-start | bytes 393224 | tf_op jit(solution)/shard_map/ppermute | solution.py:24
  92.7 13.7 %collective-permute-start.24 = (bf16[16,2560]{1,0:T(8,128)(2,1)S(1)}, bf16[16,2560]{1,0:T(8,128)(2,1)S(1)}, u32[]{:S(2)}, u32[]{:S(2)}) collective-permute-start(bf16[16,2560]{1,0:T(8,128)(2,1)S(1)} %get-tuple-element.30), channel_id=1, source_target_pairs={{0,8},{2,10},{4,12},{6,14},{8,0},{10,2},{12,4},{14,6},{16,24},{18,... | collective-permute-start | bytes 245768 | tf_op jit(solution)/shard_map/ppermute | solution.py:24
  94.0 12.4 %collective-permute-start.25 = (bf16[16,2560]{1,0:T(8,128)(2,1)S(1)}, bf16[16,2560]{1,0:T(8,128)(2,1)S(1)}, u32[]{:S(2)}, u32[]{:S(2)}) collective-permute-start(bf16[16,2560]{1,0:T(8,128)(2,1)S(1)} %get-tuple-element.31), channel_id=1, source_target_pairs={{0,16},{2,18},{4,20},{6,22},{8,24},{10,26},{12,28},{14,30},{16,0},... | collective-permute-start | bytes 245768 | tf_op jit(solution)/shard_map/ppermute | solution.py:24
  96.1 10.3 %collective-permute-start.26 = (bf16[16,2560]{1,0:T(8,128)(2,1)S(1)}, bf16[16,2560]{1,0:T(8,128)(2,1)S(1)}, u32[]{:S(2)}, u32[]{:S(2)}) collective-permute-start(bf16[16,2560]{1,0:T(8,128)(2,1)S(1)} %get-tuple-element.32), channel_id=1, source_target_pairs={{0,24},{2,26},{4,28},{6,30},{8,16},{10,18},{12,20},{14,22},{16,8},... | collective-permute-start | bytes 245768 | tf_op jit(solution)/shard_map/ppermute | solution.py:24
  97.6 4.0 %collective-permute-start.31 = (bf16[16,1024]{1,0:T(8,128)(2,1)S(1)}, bf16[16,1024]{1,0:T(8,128)(2,1)S(1)}, u32[]{:S(2)}, u32[]{:S(2)}) collective-permute-start(bf16[16,1024]{1,0:T(8,128)(2,1)S(1)} %get-tuple-element.38), channel_id=1, source_target_pairs={{0,2},{2,0},{4,6},{6,4},{8,10},{10,8},{12,14},{14,12},{16,18},{18,... | collective-permute-start | bytes 98312 | tf_op jit(solution)/shard_map/ppermute | solution.py:24
  98.5 4.8 %collective-permute-start.32 = (bf16[16,1024]{1,0:T(8,128)(2,1)S(1)}, bf16[16,1024]{1,0:T(8,128)(2,1)S(1)}, u32[]{:S(2)}, u32[]{:S(2)}) collective-permute-start(bf16[16,1024]{1,0:T(8,128)(2,1)S(1)} %get-tuple-element.39), channel_id=1, source_target_pairs={{0,4},{2,6},{4,0},{6,2},{8,12},{10,14},{12,8},{14,10},{16,20},{18,... | collective-permute-start | bytes 98312 | tf_op jit(solution)/shard_map/ppermute | solution.py:24
  101.6 4.8 %collective-permute-start.33 = (bf16[16,1024]{1,0:T(8,128)(2,1)S(1)}, bf16[16,1024]{1,0:T(8,128)(2,1)S(1)}, u32[]{:S(2)}, u32[]{:S(2)}) collective-permute-start(bf16[16,1024]{1,0:T(8,128)(2,1)S(1)} %get-tuple-element.40), channel_id=1, source_target_pairs={{0,6},{2,4},{4,2},{6,0},{8,14},{10,12},{12,10},{14,8},{16,22},{18,... | collective-permute-start | bytes 98312 | tf_op jit(solution)/shard_map/ppermute | solution.py:24

commit v2 on v0

--- a/solution.py
+++ b/solution.py
@@ -1,9 +1,380 @@
+import functools
+
 import jax
 import jax.numpy as jnp
 from jax import lax
+from jax.experimental import pallas as pl
+from jax.experimental.pallas import tpu as pltpu
 from jax.sharding import PartitionSpec as P
 
 EXPERTS = 16
+LANES = 128
+INNER = 4
+
+
+def exchanged(array, even, odd):
+    owners = lax.axis_size("expert")
+    route = []
+    for core, apart in enumerate((even, odd)):
+        route += [(2 * i + core, 2 * (i ^ apart) + core) for i in range(owners)]
+    return lax.ppermute(array, ("expert", "hsplit"), route)
+
+
+def first_hop(array, k):
+    return exchanged(array, INNER * k, k)
+
+
+def second_hop(array, k):
+    return exchanged(array, k, INNER * k)
+
+
+def other_core(array):
+    return lax.ppermute(array, "hsplit", [(0, 1), (1, 0)])
+
+
+VMEM = pl.BlockSpec(memory_space=pltpu.VMEM)
+HBM = pl.BlockSpec(memory_space=pltpu.HBM)
+TILE = 256
+
+
+def kept(rows, columns, dtype=jnp.bfloat16):
+    return pltpu.VMEM((rows, columns), dtype)
+
+
+def call(kernel, out_shape, args, name, flops=0, moved=0, specs=None, scratch=(), mib=4):
+    return pl.pallas_call(
+        kernel,
+        out_shape=out_shape,
+        in_specs=specs or [VMEM] * len(args),
+        out_specs=jax.tree.map(lambda _: VMEM, out_shape),
+        scratch_shapes=scratch,
+        compiler_params=pltpu.CompilerParams(vmem_limit_bytes=mib << 20),
+        cost_estimate=pl.CostEstimate(flops=flops, bytes_accessed=moved, transcendentals=0),
+        name=name,
+    )(*args)
+
+
+def fetches(wanted):
+    args = [pltpu.with_memory_space_constraint(w[0], pltpu.HBM) for w in wanted]
+    specs = [HBM] * len(wanted)
+    outs = []
+    for weight, axis, _, _, span in wanted:
+        shape = list(weight.shape)
+        shape[axis] = span
+        outs.append(kept(*shape))
+
+    def copies(in_refs, out_refs, sems):
+        found = []
+        for n, (weight, axis, own, start, span) in enumerate(wanted):
+            core = lax.axis_index("hsplit")
+            core_at = core if own else 1 - core
+            at = pl.multiple_of(core_at * (weight.shape[axis] // 2) + start, LANES)
+            ref = in_refs[n]
+            part = ref.at[:, pl.ds(at, span)] if axis else ref.at[pl.ds(at, span)]
+            found.append(pltpu.make_async_copy(part, out_refs[n], sems.at[n]))
+        return found
+
+    scratch = [pltpu.SemaphoreType.DMA((len(wanted),))] if wanted else []
+    moved = sum(2 * 2 * o.shape[0] * o.shape[1] for o in outs)
+    return args, specs, outs, scratch, moved, copies
+
+
+def fetch(wanted, name):
+    args, specs, outs, scratch, moved, copies = fetches(wanted)
+
+    def kernel(*refs):
+        found = copies(refs[: len(args)], refs[len(args) : -2], refs[-1])
+        for copy in found:
+            copy.start()
+        refs[-2][...] = jnp.zeros(refs[-2].shape, refs[-2].dtype)
+        for copy in found:
+            copy.wait()
+
+    results = call(
+        kernel, outs + [kept(8, LANES, jnp.float32)], args, name, moved=moved,
+        specs=specs, scratch=scratch, mib=2,
+    )
+    return results[:-1], results[-1]
+
+
+def beside(copies, compute):
+    for copy in copies:
+        copy.start()
+    if copies:
+        pl.when(lax.axis_index("hsplit") >= 0)(compute)
+    else:
+        compute()
+    for copy in copies:
+        copy.wait()
+
+
+def first_piece(tokens, routes, route_weights):
+    rows, width = tokens.shape
+    half = width // 2
+
+    def kernel(tok_ref, routes_ref, weights_ref, out_ref):
+        at = pl.multiple_of(lax.axis_index("hsplit") * half, LANES)
+        out_ref[:, :half] = tok_ref[:, pl.ds(at, half)]
+        expert = lax.broadcasted_iota(jnp.int32, (EXPERTS, rows), 0)
+        table = jnp.zeros((EXPERTS, rows), jnp.float32)
+        for k in range(routes_ref.shape[0]):
+            named = routes_ref[k : k + 1, :] == expert
+            table += jnp.where(named, weights_ref[k : k + 1, :], 0.0)
+        high = table.astype(jnp.bfloat16)
+        low = (table - high.astype(jnp.float32)).astype(jnp.bfloat16)
+        both = jnp.concatenate([high, low], axis=0)
+        shape = (2 * EXPERTS, LANES)
+        lane = lax.broadcasted_iota(jnp.int32, shape, 1)
+        place = (lax.broadcasted_iota(jnp.int32, shape, 0) == lane).astype(jnp.bfloat16)
+        out_ref[:, half:] = lax.dot_general(
+            both, place, (((0,), (0,)), ((), ())), preferred_element_type=jnp.float32
+        ).astype(out_ref.dtype)
+
+    return call(
+        kernel, kept(rows, half + LANES), (tokens, routes.T, route_weights.T), "first_piece"
+    )
+
+
+def joined(parts, done, name):
+    rows, width = parts[0].shape
+
+    def kernel(*refs):
+        for k in range(len(parts)):
+            refs[-1][k * rows : (k + 1) * rows] = refs[k][...]
+
+    return call(kernel, kept(len(parts) * rows, width), (*parts, done), name)
+
+
+def up_own(pieces, weights, wanted, name):
+    units = weights[0].shape[1]
+    depth = weights[0].shape[0]
+    rows = sum(p.shape[0] for p in pieces)
+    more, more_specs, fetched, scratch, moved, copies = fetches(wanted)
+    fixed = list(pieces) + list(weights)
+    args = fixed + more
+    shapes = [kept(rows, units, jnp.float32) for _ in range(2)]
+
+    def kernel(*refs):
+        outs = refs[len(args) : len(args) + 2]
+        found = []
+        if wanted:
+            found = copies(refs[len(fixed) : len(args)], refs[len(args) + 2 : -1], refs[-1])
+
+        def compute():
+            for n in range(units // TILE):
+                columns = slice(n * TILE, (n + 1) * TILE)
+                x = jnp.concatenate([refs[p][:, :depth] for p in range(len(pieces))], axis=0)
+                for which in range(2):
+                    outs[which][:, columns] = jnp.dot(
+                        x, refs[len(pieces) + which][:, columns], preferred_element_type=jnp.float32
+                    )
+
+        beside(found, compute)
+
+    results = call(
+        kernel, shapes + fetched, args, name, flops=4 * rows * units * depth, moved=moved,
+        specs=[VMEM] * len(fixed) + more_specs, scratch=scratch, mib=8,
+    )
+    return results[:2], results[2:]
+
+
+def hidden_call(pieces, last, weights, own_sums, far_sums, extras, wanted):
+    units = weights[0].shape[1]
+    depth = weights[0].shape[0]
+    rows = pieces[0].shape[0]
+    block_rows = rows // INNER
+    more, more_specs, fetched, scratch, moved, copies = fetches(wanted)
+    fixed = list(pieces) + list(weights)
+    sums_at = len(fixed)
+    for _, gate, up in own_sums + far_sums:
+        fixed += [gate, up]
+    extras_at = len(fixed)
+    fixed += list(extras)
+    args = fixed + more
+    out_shape = kept(INNER * rows, units)
+
+    def kernel(*refs):
+        out_ref = refs[len(args)]
+        scale_ref = refs[-1]
+        found = copies(refs[len(fixed) : len(args)], refs[len(args) + 1 : -2], refs[-2])
+        def compute():
+            extra = jnp.concatenate(
+                [refs[extras_at + k][:, depth:] for k in range(INNER)], axis=0
+            ).astype(jnp.float32)
+            lane = lax.broadcasted_iota(jnp.int32, extra.shape, 1)
+            expert = lax.axis_index("expert")
+            mine = (lane == expert) | (lane == expert + EXPERTS)
+            total = jnp.sum(jnp.where(mine, extra, 0.0), axis=1, keepdims=True)
+            scale_ref[...] = jnp.broadcast_to(total, scale_ref.shape)
+
+            for n in range(units // TILE):
+                columns = slice(n * TILE, (n + 1) * TILE)
+                x = jnp.concatenate([refs[p][:, :depth] for p in range(len(pieces))], axis=0)
+                both = []
+                for which in range(2):
+                    product = jnp.dot(
+                        x, refs[len(pieces) + which][:, columns], preferred_element_type=jnp.float32
+                    )
+                    own, far = {}, {}
+                    for n_sum, (held, _, _) in enumerate(own_sums):
+                        for at, k in enumerate(held):
+                            own[k] = (refs[sums_at + 2 * n_sum + which], at)
+                    for n_sum, (held, _, _) in enumerate(far_sums):
+                        for at, k in enumerate(held):
+                            far[k] = (refs[sums_at + 2 * (len(own_sums) + n_sum) + which], at)
+                    parts = []
+                    for jj in range(INNER):
+                        for ii in range(INNER):
+                            ref, at = own[jj]
+                            at = at * rows + ii * block_rows
+                            mine_part = ref[at : at + block_rows, columns]
+                            if ii in far:
+                                ref, at = far[ii]
+                                at = at * rows + jj * block_rows
+                                other = ref[at : at + block_rows, columns]
+                            else:
+                                at = last.index(ii) * rows + jj * block_rows
+                                other = product[at : at + block_rows]
+                            parts.append(mine_part + other)
+                    both.append(jnp.concatenate(parts, axis=0))
+                gate, up = both
+                scale = jnp.concatenate([scale_ref[...]] * (TILE // LANES), axis=1)
+                hidden = gate / (1.0 + jnp.exp(-gate)) * up * scale
+                out_ref[:, columns] = hidden.astype(out_ref.dtype)
+
+        beside(found, compute)
+
+    results = call(
+        kernel, [out_shape] + fetched, args, "hidden",
+        flops=4 * len(pieces) * rows * units * depth, moved=moved,
+        specs=[VMEM] * len(fixed) + more_specs,
+        scratch=scratch + [pltpu.VMEM((INNER * rows, LANES), jnp.float32)], mib=8,
+    )
+    return results[0], results[1:]
+
+
+def down_far(hidden, weight, held, name, before=()):
+    tokens, units = hidden.shape
+    rows = tokens // INNER
+    block_rows = rows // INNER
+    span = weight.shape[1]
+
+    def kernel(hid_ref, w_ref, *rest):
+        out_ref = rest[-1]
+        at = [jj * rows + k * block_rows for k in held for jj in range(INNER)]
+        x = jnp.concatenate([hid_ref[a : a + block_rows] for a in at], axis=0)
+        for at in range(0, span, TILE):
+            out_ref[:, at : at + TILE] = jnp.dot(
+                x, w_ref[:, at : at + TILE], preferred_element_type=jnp.float32
+            ).astype(out_ref.dtype)
+
+    out_rows = len(held) * rows
+    return call(
+        kernel, kept(out_rows, span), (hidden, weight, *before), name, flops=2 * out_rows * units * span
+    )
+
+
+def down_own(hidden, weight, received, held, name, before=()):
+    tokens, units = hidden.shape
+    rows = tokens // INNER
+    span = weight.shape[1]
+
+    def kernel(hid_ref, w_ref, far_ref, *rest):
+        out_refs = rest[len(before) :]
+        x = jnp.concatenate([hid_ref[k * rows : (k + 1) * rows] for k in held], axis=0)
+        for at in range(0, span, TILE):
+            columns = slice(at, at + TILE)
+            total = jnp.dot(x, w_ref[:, columns], preferred_element_type=jnp.float32)
+            total = (total + far_ref[:, columns].astype(jnp.float32)).astype(jnp.bfloat16)
+            for n in range(len(held)):
+                out_refs[n][:, columns] = total[n * rows : (n + 1) * rows]
+
+    return call(
+        kernel,
+        [kept(rows, span) for _ in held],
+        (hidden, weight, received, *before),
+        name,
+        flops=2 * len(held) * rows * units * span,
+    )
+
+
+def summed(refs):
+    return functools.reduce(jnp.add, [ref[...].astype(jnp.float32) for ref in refs]).astype(
+        jnp.bfloat16
+    )
+
+
+def sum_split(parts, name):
+    rows, span = parts[0].shape
+    rows //= INNER
+
+    def kernel(*refs):
+        total = summed(refs[:INNER])
+        for k in range(INNER):
+            refs[INNER + k][...] = total[k * rows : (k + 1) * rows]
+
+    return call(kernel, [kept(rows, span) for _ in range(INNER)], parts, name)
+
+
+def sum_out(parts):
+    def kernel(*refs):
+        refs[INNER][...] = summed(refs[:INNER])
+
+    return call(kernel, jax.ShapeDtypeStruct(parts[0].shape, jnp.bfloat16), parts, "sum_out")
+
+
+def local_single(tokens, routes, route_weights, gate_weight, up_weight, down_weight):
+    rows, width = tokens.shape
+    half = width // 2
+    gate_weight, up_weight, down_weight = gate_weight[0], up_weight[0], down_weight[0]
+    first = first_piece(tokens, routes, route_weights)
+
+    def wanted(mine_too):
+        return [(weight, 0, mine_too, 0, half) for weight in (gate_weight, up_weight)]
+
+    firsts = {0: first}
+    for k in (3, 2, 1):
+        firsts[k] = first_hop(first, k)
+    own_weights, done = fetch(wanted(True), "fetch_own")
+    second = joined([firsts[k] for k in range(INNER)], done, "second")
+    pieces = {0: second}
+    for k in (3, 2, 1):
+        pieces[k] = second_hop(second, k)
+    far = {k: other_core(pieces[k]) for k in (0, 3, 2, 1)}
+
+    far_weights, _ = fetch(wanted(False), "fetch_far")
+    early, late = (0, 3), (2, 1)
+    own_early, _ = up_own([pieces[k] for k in early], own_weights, [], "up_own_early")
+    far_early, _ = up_own([far[k] for k in early], far_weights, [], "up_far_early")
+    own_late, (down_other,) = up_own(
+        [pieces[k] for k in late], own_weights, [(down_weight, 1, False, 0, half)],
+        "up_own_late",
+    )
+    hidden, (down_mine,) = hidden_call(
+        [far[k] for k in late],
+        late,
+        far_weights,
+        [(early, *own_early), (late, *own_late)],
+        [(early, *far_early)],
+        [pieces[k] for k in range(INNER)],
+        [(down_weight, 1, True, 0, half)],
+    )
+
+    middle, received, before = {}, {}, ()
+    halves = (((3, 2), "a"), ((1, 0), "b"))
+    for held, name in halves:
+        sums = down_far(hidden, down_other, held, "down_far_" + name, before)
+        received[held] = other_core(sums)
+        before = (sums,)
+    before = ()
+    for held, name in halves:
+        sums = down_own(hidden, down_mine, received[held], held, "down_own_" + name, before)
+        before = (sums[0],)
+        for k, part in zip(held, sums):
+            middle[k] = second_hop(part, k) if k else part
+    split = sum_split([middle[k] for k in range(INNER)], "sum_split")
+    ended = [split[0]] + [first_hop(split[k], k) for k in (3, 2, 1)]
+    return sum_out(ended)
 
 
 def as_sent(array):
@@ -32,7 +403,7 @@
     return lax.optimization_barrier(partial_value.astype(jnp.bfloat16))
 
 
-def local(tokens, routes, route_weights, gate_weight, up_weight, down_weight):
+def local_grouped(tokens, routes, route_weights, gate_weight, up_weight, down_weight):
     tok_dev, model_width = tokens.shape
     top_k = routes.shape[1]
     owners = lax.axis_size("expert")
@@ -106,6 +477,11 @@
         P("expert", None, "hsplit"),
         P("expert", "hsplit", None),
     )
+    single = mesh.shape["expert"] == EXPERTS and mesh.shape["hsplit"] == 2
     return jax.shard_map(
-        local, mesh=mesh, in_specs=placed, out_specs=P("expert", "hsplit"), check_vma=False
-    )
+        local_single if single else local_grouped,
+        mesh=mesh,
+        in_specs=placed,
+        out_specs=P("expert", "hsplit"),
+        check_vma=False,
+    )

time: 197 us -> 86.1 us (0.44)
  the two profiles are of different devices: /device:TPU:0 before, /device:TPU:13 now
where the time goes in v2:
time: 86.1 us; the launch traced here: 85.8 us
  waiting for transfers between devices  40.4 us (47%)
  Pallas kernels  27.4 us (32%)
  starting transfers between devices  15.6 us (18%)
  local copies, waits for them, and re-layouts  2.31 us (3%)
    ppermute x12, waiting for transfers between devices, exchanged(): return lax.ppermute(array, ('expert', 'hsplit'), route)  39.1 us
    pallas_call x14, Pallas kernels, call(): pl.pallas_call(kernel, out_shape=out_shape, in_specs=specs or [VMEM] * le...  27.4 us
    ppermute x12, starting transfers between devices, exchanged(): return lax.ppermute(array, ('expert', 'hsplit'), route)  12.1 us
    ppermute x6, starting transfers between devices, other_core(): return lax.ppermute(array, 'hsplit', [(0, 1), (1, 0)])  3.47 us
    unnamed x6, local copies, waits for them, and re-layouts  2.31 us
  transfers between devices with their start and end apart: 18, of which 10 were waited for; matrix products, arithmetic and copies ran while one was open for 0% of the time, Pallas kernels for 24%

profile of v2, /device:TPU:13, one launch (start us, length us, event | category | flops | bytes accessed | tf_op | source)
XLA Modules:
  0.0 85.8 jit_solution(934285826107577580)
XLA Ops:
  0.0 0.9 %copy-done = bf16[16,7168]{1,0:T(8,128)(2,1)S(1)} copy-done((bf16[16,7168]{1,0:T(8,128)(2,1)S(1)}, bf16[16,7168]{1,0:T(8,128)(2,1)}, u32[]{:S(2)}) %copy-start) | copy-done | bytes 229400
  0.9 0.7 copy-done.1
  1.6 0.7 copy-done.2
  2.3 0.2 first_piece.1.refs_0_
  2.5 1.2 %collective-permute-start.2 = (bf16[16,3712]{1,0:T(8,128)(2,1)S(1)}, bf16[16,3712]{1,0:T(8,128)(2,1)S(1)}, u32[]{:S(2)}, u32[]{:S(2)}) collective-permute-start(bf16[16,3712]{1,0:T(8,128)(2,1)S(1)} %first_piece.1.refs_0_), channel_id=1, source_target_pairs={{0,24},{2,26},{4,28},{6,30},{8,16},{10,18},{12,20},{14,22},{16,8},... | collective-permute-start | bytes 356360 | tf_op jit(solution)/shard_map/ppermute | solution.py:20
  3.7 1.2 %collective-permute-start.1 = (bf16[16,3712]{1,0:T(8,128)(2,1)S(1)}, bf16[16,3712]{1,0:T(8,128)(2,1)S(1)}, u32[]{:S(2)}, u32[]{:S(2)}) collective-permute-start(bf16[16,3712]{1,0:T(8,128)(2,1)S(1)} %first_piece.1.refs_0_), channel_id=1, source_target_pairs={{0,16},{2,18},{4,20},{6,22},{8,24},{10,26},{12,28},{14,30},{16,0},... | collective-permute-start | bytes 356360 | tf_op jit(solution)/shard_map/ppermute | solution.py:20
  4.9 0.3 collective-permute-start
  5.1 5.4 %fetch_own.1 = (bf16[3584,1024]{1,0:T(8,128)(2,1)S(1)}, bf16[3584,1024]{1,0:T(8,128)(2,1)S(1)}, f32[8,128]{1,0:T(8,128)S(1)}) custom-call(bf16[7168,1024]{1,0:T(8,128)(2,1)} %bitcast.7, bf16[7168,1024]{1,0:T(8,128)(2,1)} %bitcast.9), custom_call_target="tpu_custom_call" | custom-call | bytes 29360128 | tf_op jit(solution)/shard_map/fetch_own/pallas_call | solution.py:45
  10.6 0.0 collective-permute-done.2.refs_3_
  10.6 0.0 collective-permute-done.1.refs_2_
  10.6 0.0 collective-permute-done.refs_1_
  10.6 1.4 %collective-permute-start.7 = (bf16[64,3712]{1,0:T(8,128)(2,1)S(1)}, bf16[64,3712]{1,0:T(8,128)(2,1)S(1)}, u32[]{:S(2)}, u32[]{:S(2)}) collective-permute-start(bf16[64,3712]{1,0:T(8,128)(2,1)S(1)} %second.1.refs_0_.refs_10_), channel_id=1, source_target_pairs={{0,6},{2,4},{4,2},{6,0},{8,14},{10,12},{12,10},{14,8},{16,22},{18,... | collective-permute-start | bytes 1425416 | tf_op jit(solution)/shard_map/ppermute | solution.py:20
  12.0 2.2 %collective-permute-start.5 = (bf16[64,3712]{1,0:T(8,128)(2,1)S(1)}, bf16[64,3712]{1,0:T(8,128)(2,1)S(1)}, u32[]{:S(2)}, u32[]{:S(2)}) collective-permute-start(bf16[64,3712]{1,0:T(8,128)(2,1)S(1)} %second.1.refs_0_.refs_10_), channel_id=1, source_target_pairs={{0,2},{2,0},{4,6},{6,4},{8,10},{10,8},{12,14},{14,12},{16,18},{18,... | collective-permute-start | bytes 1425416 | tf_op jit(solution)/shard_map/ppermute | solution.py:20
  14.2 0.0 collective-permute-start.3
  14.2 2.0 %collective-permute-start.8 = (bf16[64,3712]{1,0:T(8,128)(2,1)S(1)}, bf16[64,3712]{1,0:T(8,128)(2,1)S(1)}, u32[]{:S(2)}, u32[]{:S(2)}) collective-permute-start(bf16[64,3712]{1,0:T(8,128)(2,1)S(1)} %second.1.refs_0_.refs_10_), channel_id=1, source_target_pairs={{0,1},{1,0},{2,3},{3,2},{4,5},{5,4},{6,7},{7,6},{8,9},{9,8},{10,11... | collective-permute-start | bytes 1425416 | tf_op jit(solution)/shard_map/ppermute | solution.py:32
  16.2 7.4 %collective-permute-done.7.refs_1_.refs_13_ = bf16[64,3712]{1,0:T(8,128)(2,1)S(1)} collective-permute-done((bf16[64,3712]{1,0:T(8,128)(2,1)S(1)}, bf16[64,3712]{1,0:T(8,128)(2,1)S(1)}, u32[]{:S(2)}, u32[]{:S(2)}) %collective-permute-start.7) | collective-permute-done | bytes 475168 | tf_op jit(solution)/shard_map/ppermute | solution.py:20
  23.6 0.0 collective-permute-start.9
  23.6 5.8 %fetch_far.1 = (bf16[3584,1024]{1,0:T(8,128)(2,1)S(1)}, bf16[3584,1024]{1,0:T(8,128)(2,1)S(1)}, f32[8,128]{1,0:T(8,128)}) custom-call(bf16[7168,1024]{1,0:T(8,128)(2,1)} %bitcast.8, bf16[7168,1024]{1,0:T(8,128)(2,1)} %bitcast.10), custom_call_target="tpu_custom_call" | custom-call | bytes 29360128 | tf_op jit(solution)/shard_map/fetch_far/pallas_call | solution.py:45
  29.4 0.0 collective-permute-done.5.refs_1_.refs_11_
  29.4 0.8 collective-permute-start.6
  30.2 2.7 %collective-permute-done.3.refs_0_.refs_12_ = bf16[64,3712]{1,0:T(8,128)(2,1)S(1)} collective-permute-done((bf16[64,3712]{1,0:T(8,128)(2,1)S(1)}, bf16[64,3712]{1,0:T(8,128)(2,1)S(1)}, u32[]{:S(2)}, u32[]{:S(2)}) %collective-permute-start.3) | collective-permute-done | bytes 475168 | tf_op jit(solution)/shard_map/ppermute | solution.py:20
  32.9 0.0 collective-permute-start.4
  32.9 2.2 %up_own_early.1 = (f32[128,1024]{1,0:T(8,128)S(1)}, f32[128,1024]{1,0:T(8,128)S(1)}) custom-call(bf16[64,3712]{1,0:T(8,128)(2,1)S(1)} %second.1.refs_0_.refs_10_, bf16[64,3712]{1,0:T(8,128)(2,1)S(1)} %collective-permute-done.7.refs_1_.refs_13_, bf16[3584,1024]{1,0:T(8,128)(2,1)S(1)} %get-tuple-element.30.refs_2_, ...), custom_call_target="tpu_custom_call" | custom-call | flops 1879048192 | tf_op jit(solution)/shard_map/up_own_early/pallas_call | solution.py:45
  35.1 3.1 %up_own_late.1 = (f32[128,1024]{1,0:T(8,128)S(1)}, f32[128,1024]{1,0:T(8,128)S(1)}, bf16[1024,3584]{1,0:T(8,128)(2,1)S(1)}) custom-call(bf16[64,3712]{1,0:T(8,128)(2,1)S(1)} %collective-permute-done.3.refs_0_.refs_12_, bf16[64,3712]{1,0:T(8,128)(2,1)S(1)} %collective-permute-done.5.refs_1_.refs_11_, bf16[3584,1024]{1,0:T(8,128)(2,1)S(1)} %get-tuple-element.30.refs_2_, ...), custom_call_target="tpu_custom_call" | custom-call | flops 1879048192 | bytes 14680064 | tf_op jit(solution)/shard_map/up_own_late/pallas_call | solution.py:45
  38.2 2.1 %up_far_early.1 = (f32[128,1024]{1,0:T(8,128)S(1)}, f32[128,1024]{1,0:T(8,128)S(1)}) custom-call(bf16[64,3712]{1,0:T(8,128)(2,1)S(1)} %collective-permute-done.8.refs_0_, bf16[64,3712]{1,0:T(8,128)(2,1)S(1)} %collective-permute-done.9.refs_1_, bf16[3584,1024]{1,0:T(8,128)(2,1)S(1)} %get-tuple-element.28.refs_2_, bf16[3584,1024]{1,0:T(8,128)(2,1)S(1)} %get-tuple-element.29.refs_3_), custom_call_target="tpu_custom_call" | custom-call | flops 1879048192 | tf_op jit(solution)/shard_map/up_far_early/pallas_call | solution.py:45
  40.4 3.1 %hidden.1 = (bf16[256,1024]{1,0:T(8,128)(2,1)S(1)}, bf16[1024,3584]{1,0:T(8,128)(2,1)S(1)}) custom-call(bf16[64,3712]{1,0:T(8,128)(2,1)S(1)} %collective-permute-done.4.refs_0_, bf16[64,3712]{1,0:T(8,128)(2,1)S(1)} %collective-permute-done.6.refs_1_, bf16[3584,1024]{1,0:T(8,128)(2,1)S(1)} %get-tuple-element.28.refs_2_, ...), custom_call_target="tpu_custom_call" | custom-call | flops 1879048192 | bytes 14680064 | tf_op jit(solution)/shard_map/hidden/pallas_call | solution.py:45
  43.5 1.1 %down_far_a.1.rest_0_ = bf16[128,3584]{1,0:T(8,128)(2,1)S(1)} custom-call(bf16[256,1024]{1,0:T(8,128)(2,1)S(1)} %get-tuple-element.38.hid_ref, bf16[1024,3584]{1,0:T(8,128)(2,1)S(1)} %get-tuple-element.40.w_ref), custom_call_target="tpu_custom_call" | custom-call | flops 939524096 | tf_op jit(solution)/shard_map/down_far_a/pallas_call | solution.py:45
  44.6 0.6 collective-permute-start.11
  45.2 1.1 %down_far_b.1 = bf16[128,3584]{1,0:T(8,128)(2,1)S(1)} custom-call(bf16[256,1024]{1,0:T(8,128)(2,1)S(1)} %get-tuple-element.38.hid_ref, bf16[1024,3584]{1,0:T(8,128)(2,1)S(1)} %get-tuple-element.40.w_ref, bf16[128,3584]{1,0:T(8,128)(2,1)S(1)} %down_far_a.1.rest_0_), custom_call_target="tpu_custom_call" | custom-call | flops 939524096 | tf_op jit(solution)/shard_map/down_far_b/pallas_call | solution.py:45
  46.3 0.1 collective-permute-start.10
  46.4 0.9 %collective-permute-done.11.far_ref = bf16[128,3584]{1,0:T(8,128)(2,1)S(1)} collective-permute-done((bf16[128,3584]{1,0:T(8,128)(2,1)S(1)}, bf16[128,3584]{1,0:T(8,128)(2,1)S(1)}, u32[]{:S(2)}, u32[]{:S(2)}) %collective-permute-start.11) | collective-permute-done | bytes 917536 | tf_op jit(solution)/shard_map/ppermute | solution.py:32
  47.3 1.1 %down_own_a.1 = (bf16[64,3584]{1,0:T(8,128)(2,1)S(1)}, bf16[64,3584]{1,0:T(8,128)(2,1)S(1)}) custom-call(bf16[256,1024]{1,0:T(8,128)(2,1)S(1)} %get-tuple-element.38.hid_ref, bf16[1024,3584]{1,0:T(8,128)(2,1)S(1)} %get-tuple-element.39.w_ref, bf16[128,3584]{1,0:T(8,128)(2,1)S(1)} %collective-permute-done.11.far_ref), custom_call_target="tpu_custom_call" | custom-call | flops 939524096 | tf_op jit(solution)/shard_map/down_own_a/pallas_call | solution.py:45
  48.4 0.4 collective-permute-done.10.far_ref
  48.9 1.1 %down_own_b.1 = (bf16[64,3584]{1,0:T(8,128)(2,1)S(1)}, bf16[64,3584]{1,0:T(8,128)(2,1)S(1)}) custom-call(bf16[256,1024]{1,0:T(8,128)(2,1)S(1)} %get-tuple-element.38.hid_ref, bf16[1024,3584]{1,0:T(8,128)(2,1)S(1)} %get-tuple-element.39.w_ref, bf16[128,3584]{1,0:T(8,128)(2,1)S(1)} %collective-permute-done.10.far_ref, ...), custom_call_target="tpu_custom_call" | custom-call | flops 939524096 | tf_op jit(solution)/shard_map/down_own_b/pallas_call | solution.py:45
  50.0 1.8 %collective-permute-start.12 = (bf16[64,3584]{1,0:T(8,128)(2,1)S(1)}, bf16[64,3584]{1,0:T(8,128)(2,1)S(1)}, u32[]{:S(2)}, u32[]{:S(2)}) collective-permute-start(bf16[64,3584]{1,0:T(8,128)(2,1)S(1)} %get-tuple-element.43), channel_id=1, source_target_pairs={{0,2},{2,0},{4,6},{6,4},{8,10},{10,8},{12,14},{14,12},{16,18},{18,... | collective-permute-start | bytes 1376264 | tf_op jit(solution)/shard_map/ppermute | solution.py:20
  51.8 1.1 %collective-permute-start.13 = (bf16[64,3584]{1,0:T(8,128)(2,1)S(1)}, bf16[64,3584]{1,0:T(8,128)(2,1)S(1)}, u32[]{:S(2)}, u32[]{:S(2)}) collective-permute-start(bf16[64,3584]{1,0:T(8,128)(2,1)S(1)} %get-tuple-element.44), channel_id=1, source_target_pairs={{0,4},{2,6},{4,0},{6,2},{8,12},{10,14},{12,8},{14,10},{16,20},{18,... | collective-permute-start | bytes 1376264 | tf_op jit(solution)/shard_map/ppermute | solution.py:20
  53.0 0.2 collective-permute-start.14
  53.2 8.8 %collective-permute-done.12.refs_1_ = bf16[64,3584]{1,0:T(8,128)(2,1)S(1)} collective-permute-done((bf16[64,3584]{1,0:T(8,128)(2,1)S(1)}, bf16[64,3584]{1,0:T(8,128)(2,1)S(1)}, u32[]{:S(2)}, u32[]{:S(2)}) %collective-permute-start.12) | collective-permute-done | bytes 458784 | tf_op jit(solution)/shard_map/ppermute | solution.py:20
  61.9 7.6 %collective-permute-done.13.refs_2_ = bf16[64,3584]{1,0:T(8,128)(2,1)S(1)} collective-permute-done((bf16[64,3584]{1,0:T(8,128)(2,1)S(1)}, bf16[64,3584]{1,0:T(8,128)(2,1)S(1)}, u32[]{:S(2)}, u32[]{:S(2)}) %collective-permute-start.13) | collective-permute-done | bytes 458784 | tf_op jit(solution)/shard_map/ppermute | solution.py:20
  69.6 9.2 %collective-permute-done.14.refs_3_ = bf16[64,3584]{1,0:T(8,128)(2,1)S(1)} collective-permute-done((bf16[64,3584]{1,0:T(8,128)(2,1)S(1)}, bf16[64,3584]{1,0:T(8,128)(2,1)S(1)}, u32[]{:S(2)}, u32[]{:S(2)}) %collective-permute-start.14) | collective-permute-done | bytes 458784 | tf_op jit(solution)/shard_map/ppermute | solution.py:20
  78.8 0.2 sum_split.1
  79.0 1.2 %collective-permute-start.15 = (bf16[16,3584]{1,0:T(8,128)(2,1)S(1)}, bf16[16,3584]{1,0:T(8,128)(2,1)S(1)}, u32[]{:S(2)}, u32[]{:S(2)}) collective-permute-start(bf16[16,3584]{1,0:T(8,128)(2,1)S(1)} %get-tuple-element.46), channel_id=1, source_target_pairs={{0,24},{2,26},{4,28},{6,30},{8,16},{10,18},{12,20},{14,22},{16,8},... | collective-permute-start | bytes 344072 | tf_op jit(solution)/shard_map/ppermute | solution.py:20
  80.2 1.3 %collective-permute-start.16 = (bf16[16,3584]{1,0:T(8,128)(2,1)S(1)}, bf16[16,3584]{1,0:T(8,128)(2,1)S(1)}, u32[]{:S(2)}, u32[]{:S(2)}) collective-permute-start(bf16[16,3584]{1,0:T(8,128)(2,1)S(1)} %get-tuple-element.47), channel_id=1, source_target_pairs={{0,16},{2,18},{4,20},{6,22},{8,24},{10,26},{12,28},{14,30},{16,0},... | collective-permute-start | bytes 344072 | tf_op jit(solution)/shard_map/ppermute | solution.py:20
  81.4 0.3 collective-permute-start.17
  81.7 2.0 %collective-permute-done.15.refs_1_ = bf16[16,3584]{1,0:T(8,128)(2,1)S(1)} collective-permute-done((bf16[16,3584]{1,0:T(8,128)(2,1)S(1)}, bf16[16,3584]{1,0:T(8,128)(2,1)S(1)}, u32[]{:S(2)}, u32[]{:S(2)}) %collective-permute-start.15) | collective-permute-done | bytes 114720 | tf_op jit(solution)/shard_map/ppermute | solution.py:20
  83.7 1.1 %collective-permute-done.16.refs_2_ = bf16[16,3584]{1,0:T(8,128)(2,1)S(1)} collective-permute-done((bf16[16,3584]{1,0:T(8,128)(2,1)S(1)}, bf16[16,3584]{1,0:T(8,128)(2,1)S(1)}, u32[]{:S(2)}, u32[]{:S(2)}) %collective-permute-start.16) | collective-permute-done | bytes 114720 | tf_op jit(solution)/shard_map/ppermute | solution.py:20
  84.8 0.3 collective-permute-done.17.refs_3_
  85.1 0.7 sum_out.1
  (8 shorter events, 0.1 us)
Async XLA Ops:
  0.0 0.9 %copy-start = (bf16[16,7168]{1,0:T(8,128)(2,1)S(1)}, bf16[16,7168]{1,0:T(8,128)(2,1)}, u32[]{:S(2)}) copy-start(bf16[16,7168]{1,0:T(8,128)(2,1)} %tok_ref.1) | copy-start | bytes 688132
  0.9 0.7 copy-start.1
  1.6 0.7 copy-start.2
  2.5 8.1 %collective-permute-start.2 = (bf16[16,3712]{1,0:T(8,128)(2,1)S(1)}, bf16[16,3712]{1,0:T(8,128)(2,1)S(1)}, u32[]{:S(2)}, u32[]{:S(2)}) collective-permute-start(bf16[16,3712]{1,0:T(8,128)(2,1)S(1)} %first_piece.1.refs_0_), channel_id=1, source_target_pairs={{0,24},{2,26},{4,28},{6,30},{8,16},{10,18},{12,20},{14,22},{16,8},... | collective-permute-start | bytes 356360 | tf_op jit(solution)/shard_map/ppermute | solution.py:20
  3.7 6.9 %collective-permute-start.1 = (bf16[16,3712]{1,0:T(8,128)(2,1)S(1)}, bf16[16,3712]{1,0:T(8,128)(2,1)S(1)}, u32[]{:S(2)}, u32[]{:S(2)}) collective-permute-start(bf16[16,3712]{1,0:T(8,128)(2,1)S(1)} %first_piece.1.refs_0_), channel_id=1, source_target_pairs={{0,16},{2,18},{4,20},{6,22},{8,24},{10,26},{12,28},{14,30},{16,0},... | collective-permute-start | bytes 356360 | tf_op jit(solution)/shard_map/ppermute | solution.py:20
  4.9 5.7 %collective-permute-start = (bf16[16,3712]{1,0:T(8,128)(2,1)S(1)}, bf16[16,3712]{1,0:T(8,128)(2,1)S(1)}, u32[]{:S(2)}, u32[]{:S(2)}) collective-permute-start(bf16[16,3712]{1,0:T(8,128)(2,1)S(1)} %first_piece.1.refs_0_), channel_id=1, source_target_pairs={{0,8},{2,10},{4,12},{6,14},{8,0},{10,2},{12,4},{14,6},{16,24},{18,... | collective-permute-start | bytes 356360 | tf_op jit(solution)/shard_map/ppermute | solution.py:20
  10.6 13.0 %collective-permute-start.7 = (bf16[64,3712]{1,0:T(8,128)(2,1)S(1)}, bf16[64,3712]{1,0:T(8,128)(2,1)S(1)}, u32[]{:S(2)}, u32[]{:S(2)}) collective-permute-start(bf16[64,3712]{1,0:T(8,128)(2,1)S(1)} %second.1.refs_0_.refs_10_), channel_id=1, source_target_pairs={{0,6},{2,4},{4,2},{6,0},{8,14},{10,12},{12,10},{14,8},{16,22},{18,... | collective-permute-start | bytes 1425416 | tf_op jit(solution)/shard_map/ppermute | solution.py:20
  12.0 17.4 %collective-permute-start.5 = (bf16[64,3712]{1,0:T(8,128)(2,1)S(1)}, bf16[64,3712]{1,0:T(8,128)(2,1)S(1)}, u32[]{:S(2)}, u32[]{:S(2)}) collective-permute-start(bf16[64,3712]{1,0:T(8,128)(2,1)S(1)} %second.1.refs_0_.refs_10_), channel_id=1, source_target_pairs={{0,2},{2,0},{4,6},{6,4},{8,10},{10,8},{12,14},{14,12},{16,18},{18,... | collective-permute-start | bytes 1425416 | tf_op jit(solution)/shard_map/ppermute | solution.py:20
  14.2 18.7 %collective-permute-start.3 = (bf16[64,3712]{1,0:T(8,128)(2,1)S(1)}, bf16[64,3712]{1,0:T(8,128)(2,1)S(1)}, u32[]{:S(2)}, u32[]{:S(2)}) collective-permute-start(bf16[64,3712]{1,0:T(8,128)(2,1)S(1)} %second.1.refs_0_.refs_10_), channel_id=1, source_target_pairs={{0,4},{2,6},{4,0},{6,2},{8,12},{10,14},{12,8},{14,10},{16,20},{18,... | collective-permute-start | bytes 1425416 | tf_op jit(solution)/shard_map/ppermute | solution.py:20
  14.2 24.0 %collective-permute-start.8 = (bf16[64,3712]{1,0:T(8,128)(2,1)S(1)}, bf16[64,3712]{1,0:T(8,128)(2,1)S(1)}, u32[]{:S(2)}, u32[]{:S(2)}) collective-permute-start(bf16[64,3712]{1,0:T(8,128)(2,1)S(1)} %second.1.refs_0_.refs_10_), channel_id=1, source_target_pairs={{0,1},{1,0},{2,3},{3,2},{4,5},{5,4},{6,7},{7,6},{8,9},{9,8},{10,11... | collective-permute-start | bytes 1425416 | tf_op jit(solution)/shard_map/ppermute | solution.py:32
  23.6 14.6 %collective-permute-start.9 = (bf16[64,3712]{1,0:T(8,128)(2,1)S(1)}, bf16[64,3712]{1,0:T(8,128)(2,1)S(1)}, u32[]{:S(2)}, u32[]{:S(2)}) collective-permute-start(bf16[64,3712]{1,0:T(8,128)(2,1)S(1)} %collective-permute-done.7.refs_1_.refs_13_), channel_id=1, source_target_pairs={{0,1},{1,0},{2,3},{3,2},{4,5},{5,4},{6,7},{7,6},{8,9},{9,8},{10,11... | collective-permute-start | bytes 1425416 | tf_op jit(solution)/shard_map/ppermute | solution.py:32
  29.4 11.0 %collective-permute-start.6 = (bf16[64,3712]{1,0:T(8,128)(2,1)S(1)}, bf16[64,3712]{1,0:T(8,128)(2,1)S(1)}, u32[]{:S(2)}, u32[]{:S(2)}) collective-permute-start(bf16[64,3712]{1,0:T(8,128)(2,1)S(1)} %collective-permute-done.5.refs_1_.refs_11_), channel_id=1, source_target_pairs={{0,1},{1,0},{2,3},{3,2},{4,5},{5,4},{6,7},{7,6},{8,9},{9,8},{10,11... | collective-permute-start | bytes 1425416 | tf_op jit(solution)/shard_map/ppermute | solution.py:32
  32.9 7.5 %collective-permute-start.4 = (bf16[64,3712]{1,0:T(8,128)(2,1)S(1)}, bf16[64,3712]{1,0:T(8,128)(2,1)S(1)}, u32[]{:S(2)}, u32[]{:S(2)}) collective-permute-start(bf16[64,3712]{1,0:T(8,128)(2,1)S(1)} %collective-permute-done.3.refs_0_.refs_12_), channel_id=1, source_target_pairs={{0,1},{1,0},{2,3},{3,2},{4,5},{5,4},{6,7},{7,6},{8,9},{9,8},{10,11... | collective-permute-start | bytes 1425416 | tf_op jit(solution)/shard_map/ppermute | solution.py:32
  44.6 2.7 %collective-permute-start.11 = (bf16[128,3584]{1,0:T(8,128)(2,1)S(1)}, bf16[128,3584]{1,0:T(8,128)(2,1)S(1)}, u32[]{:S(2)}, u32[]{:S(2)}) collective-permute-start(bf16[128,3584]{1,0:T(8,128)(2,1)S(1)} %down_far_a.1.rest_0_), channel_id=1, source_target_pairs={{0,1},{1,0},{2,3},{3,2},{4,5},{5,4},{6,7},{7,6},{8,9},{9,8},{10,11... | collective-permute-start | bytes 2752520 | tf_op jit(solution)/shard_map/ppermute | solution.py:32
  46.3 2.5 %collective-permute-start.10 = (bf16[128,3584]{1,0:T(8,128)(2,1)S(1)}, bf16[128,3584]{1,0:T(8,128)(2,1)S(1)}, u32[]{:S(2)}, u32[]{:S(2)}) collective-permute-start(bf16[128,3584]{1,0:T(8,128)(2,1)S(1)} %down_far_b.1), channel_id=1, source_target_pairs={{0,1},{1,0},{2,3},{3,2},{4,5},{5,4},{6,7},{7,6},{8,9},{9,8},{10,11... | collective-permute-start | bytes 2752520 | tf_op jit(solution)/shard_map/ppermute | solution.py:32
  50.0 11.9 %collective-permute-start.12 = (bf16[64,3584]{1,0:T(8,128)(2,1)S(1)}, bf16[64,3584]{1,0:T(8,128)(2,1)S(1)}, u32[]{:S(2)}, u32[]{:S(2)}) collective-permute-start(bf16[64,3584]{1,0:T(8,128)(2,1)S(1)} %get-tuple-element.43), channel_id=1, source_target_pairs={{0,2},{2,0},{4,6},{6,4},{8,10},{10,8},{12,14},{14,12},{16,18},{18,... | collective-permute-start | bytes 1376264 | tf_op jit(solution)/shard_map/ppermute | solution.py:20
  51.8 17.7 %collective-permute-start.13 = (bf16[64,3584]{1,0:T(8,128)(2,1)S(1)}, bf16[64,3584]{1,0:T(8,128)(2,1)S(1)}, u32[]{:S(2)}, u32[]{:S(2)}) collective-permute-start(bf16[64,3584]{1,0:T(8,128)(2,1)S(1)} %get-tuple-element.44), channel_id=1, source_target_pairs={{0,4},{2,6},{4,0},{6,2},{8,12},{10,14},{12,8},{14,10},{16,20},{18,... | collective-permute-start | bytes 1376264 | tf_op jit(solution)/shard_map/ppermute | solution.py:20
  53.0 25.8 %collective-permute-start.14 = (bf16[64,3584]{1,0:T(8,128)(2,1)S(1)}, bf16[64,3584]{1,0:T(8,128)(2,1)S(1)}, u32[]{:S(2)}, u32[]{:S(2)}) collective-permute-start(bf16[64,3584]{1,0:T(8,128)(2,1)S(1)} %get-tuple-element.41.rest_0_), channel_id=1, source_target_pairs={{0,6},{2,4},{4,2},{6,0},{8,14},{10,12},{12,10},{14,8},{16,22},{18,... | collective-permute-start | bytes 1376264 | tf_op jit(solution)/shard_map/ppermute | solution.py:20
  79.0 4.7 %collective-permute-start.15 = (bf16[16,3584]{1,0:T(8,128)(2,1)S(1)}, bf16[16,3584]{1,0:T(8,128)(2,1)S(1)}, u32[]{:S(2)}, u32[]{:S(2)}) collective-permute-start(bf16[16,3584]{1,0:T(8,128)(2,1)S(1)} %get-tuple-element.46), channel_id=1, source_target_pairs={{0,24},{2,26},{4,28},{6,30},{8,16},{10,18},{12,20},{14,22},{16,8},... | collective-permute-start | bytes 344072 | tf_op jit(solution)/shard_map/ppermute | solution.py:20
  80.2 4.6 %collective-permute-start.16 = (bf16[16,3584]{1,0:T(8,128)(2,1)S(1)}, bf16[16,3584]{1,0:T(8,128)(2,1)S(1)}, u32[]{:S(2)}, u32[]{:S(2)}) collective-permute-start(bf16[16,3584]{1,0:T(8,128)(2,1)S(1)} %get-tuple-element.47), channel_id=1, source_target_pairs={{0,16},{2,18},{4,20},{6,22},{8,24},{10,26},{12,28},{14,30},{16,0},... | collective-permute-start | bytes 344072 | tf_op jit(solution)/shard_map/ppermute | solution.py:20
  81.4 3.6 %collective-permute-start.17 = (bf16[16,3584]{1,0:T(8,128)(2,1)S(1)}, bf16[16,3584]{1,0:T(8,128)(2,1)S(1)}, u32[]{:S(2)}, u32[]{:S(2)}) collective-permute-start(bf16[16,3584]{1,0:T(8,128)(2,1)S(1)} %get-tuple-element.48), channel_id=1, source_target_pairs={{0,8},{2,10},{4,12},{6,14},{8,0},{10,2},{12,4},{14,6},{16,24},{18,... | collective-permute-start | bytes 344072 | tf_op jit(solution)/shard_map/ppermute | solution.py:20

commit v3 on v2

--- a/solution.py
+++ b/solution.py
@@ -35,21 +35,27 @@
 VMEM = pl.BlockSpec(memory_space=pltpu.VMEM)
 HBM = pl.BlockSpec(memory_space=pltpu.HBM)
 TILE = 256
+WEIGHT = 3
 
 
 def kept(rows, columns, dtype=jnp.bfloat16):
     return pltpu.VMEM((rows, columns), dtype)
 
 
-def call(kernel, out_shape, args, name, flops=0, moved=0, specs=None, scratch=(), mib=4):
+def call(
+    kernel, out_shape, args, name, flops=0, moved=0, specs=None, scratch=(), mib=4, aliases=None
+):
     return pl.pallas_call(
         kernel,
         out_shape=out_shape,
         in_specs=specs or [VMEM] * len(args),
         out_specs=jax.tree.map(lambda _: VMEM, out_shape),
         scratch_shapes=scratch,
+        input_output_aliases=aliases or {},
         compiler_params=pltpu.CompilerParams(vmem_limit_bytes=mib << 20),
-        cost_estimate=pl.CostEstimate(flops=flops, bytes_accessed=moved, transcendentals=0),
+        cost_estimate=pl.CostEstimate(
+            flops=WEIGHT * flops, bytes_accessed=WEIGHT * moved, transcendentals=0
+        ),
         name=name,
     )(*args)
 
@@ -108,13 +114,30 @@
         copy.wait()
 
 
+def tied(array, done, name):
+    def kernel(*refs):
+        del refs
+
+    return call(kernel, kept(*array.shape), (array, *done), name, aliases={0: 0})
+
+
 def first_piece(tokens, routes, route_weights):
     rows, width = tokens.shape
     half = width // 2
 
-    def kernel(tok_ref, routes_ref, weights_ref, out_ref):
+    def kernel(tok_in, routes_in, weights_in, out_ref, routes_ref, weights_ref, sems):
         at = pl.multiple_of(lax.axis_index("hsplit") * half, LANES)
-        out_ref[:, :half] = tok_ref[:, pl.ds(at, half)]
+        copies = [
+            pltpu.make_async_copy(routes_in, routes_ref, sems.at[0]),
+            pltpu.make_async_copy(weights_in, weights_ref, sems.at[1]),
+            pltpu.make_async_copy(
+                tok_in.at[:, pl.ds(at, half)], out_ref.at[:, pl.ds(0, half)], sems.at[2]
+            ),
+        ]
+        for copy in copies:
+            copy.start()
+        copies[0].wait()
+        copies[1].wait()
         expert = lax.broadcasted_iota(jnp.int32, (EXPERTS, rows), 0)
         table = jnp.zeros((EXPERTS, rows), jnp.float32)
         for k in range(routes_ref.shape[0]):
@@ -129,9 +152,20 @@
         out_ref[:, half:] = lax.dot_general(
             both, place, (((0,), (0,)), ((), ())), preferred_element_type=jnp.float32
         ).astype(out_ref.dtype)
-
+        copies[2].wait()
+
+    args = (tokens, routes.T, route_weights.T)
     return call(
-        kernel, kept(rows, half + LANES), (tokens, routes.T, route_weights.T), "first_piece"
+        kernel,
+        kept(rows, half + LANES),
+        [pltpu.with_memory_space_constraint(a, pltpu.HBM) for a in args],
+        "first_piece",
+        specs=[HBM] * 3,
+        scratch=[
+            pltpu.VMEM(args[1].shape, jnp.int32),
+            pltpu.VMEM(args[2].shape, jnp.float32),
+            pltpu.SemaphoreType.DMA((3,)),
+        ],
     )
 
 
@@ -145,12 +179,12 @@
     return call(kernel, kept(len(parts) * rows, width), (*parts, done), name)
 
 
-def up_own(pieces, weights, wanted, name):
+def up_own(pieces, weights, wanted, before, name):
     units = weights[0].shape[1]
     depth = weights[0].shape[0]
     rows = sum(p.shape[0] for p in pieces)
     more, more_specs, fetched, scratch, moved, copies = fetches(wanted)
-    fixed = list(pieces) + list(weights)
+    fixed = list(pieces) + list(weights) + list(before)
     args = fixed + more
     shapes = [kept(rows, units, jnp.float32) for _ in range(2)]
 
@@ -173,7 +207,7 @@
 
     results = call(
         kernel, shapes + fetched, args, name, flops=4 * rows * units * depth, moved=moved,
-        specs=[VMEM] * len(fixed) + more_specs, scratch=scratch, mib=8,
+        specs=[VMEM] * len(fixed) + more_specs, scratch=scratch,
     )
     return results[:2], results[2:]
 
@@ -248,7 +282,7 @@
         kernel, [out_shape] + fetched, args, "hidden",
         flops=4 * len(pieces) * rows * units * depth, moved=moved,
         specs=[VMEM] * len(fixed) + more_specs,
-        scratch=scratch + [pltpu.VMEM((INNER * rows, LANES), jnp.float32)], mib=8,
+        scratch=scratch + [pltpu.VMEM((INNER * rows, LANES), jnp.float32)],
     )
     return results[0], results[1:]
 
@@ -304,14 +338,21 @@
     )
 
 
+def add(*parts):
+    def kernel(*refs):
+        refs[-1][...] = summed(refs[:-1])
+
+    return call(kernel, kept(*parts[0].shape), parts, "add")
+
+
 def sum_split(parts, name):
     rows, span = parts[0].shape
     rows //= INNER
 
     def kernel(*refs):
-        total = summed(refs[:INNER])
+        total = summed(refs[: len(parts)])
         for k in range(INNER):
-            refs[INNER + k][...] = total[k * rows : (k + 1) * rows]
+            refs[len(parts) + k][...] = total[k * rows : (k + 1) * rows]
 
     return call(kernel, [kept(rows, span) for _ in range(INNER)], parts, name)
 
@@ -329,50 +370,54 @@
     gate_weight, up_weight, down_weight = gate_weight[0], up_weight[0], down_weight[0]
     first = first_piece(tokens, routes, route_weights)
 
-    def wanted(mine_too):
-        return [(weight, 0, mine_too, 0, half) for weight in (gate_weight, up_weight)]
-
     firsts = {0: first}
     for k in (3, 2, 1):
         firsts[k] = first_hop(first, k)
-    own_weights, done = fetch(wanted(True), "fetch_own")
+    (gate_mine,), done = fetch([(gate_weight, 0, True, 0, half)], "fetch_1")
     second = joined([firsts[k] for k in range(INNER)], done, "second")
-    pieces = {0: second}
-    for k in (3, 2, 1):
-        pieces[k] = second_hop(second, k)
-    far = {k: other_core(pieces[k]) for k in (0, 3, 2, 1)}
-
-    far_weights, _ = fetch(wanted(False), "fetch_far")
-    early, late = (0, 3), (2, 1)
-    own_early, _ = up_own([pieces[k] for k in early], own_weights, [], "up_own_early")
-    far_early, _ = up_own([far[k] for k in early], far_weights, [], "up_far_early")
+    pieces = {0: second, 2: second_hop(second, 2), 1: second_hop(second, 1)}
+    (up_mine, gate_other), done = fetch(
+        [(up_weight, 0, True, 0, half), (gate_weight, 0, False, 0, half)], "fetch_2"
+    )
+    pieces[2] = tied(pieces[2], (pieces[1], done), "piece_2")
+    pieces[3] = second_hop(pieces[2], 1)
+    far = {k: other_core(pieces[k]) for k in (0, 2, 1)}
+
+    early, late = (0, 2), (1, 3)
+    own_early, (up_other,) = up_own(
+        [pieces[k] for k in early], (gate_mine, up_mine), [(up_weight, 0, False, 0, half)], (),
+        "up_own_early",
+    )
+    far_early, _ = up_own([far[k] for k in early], (gate_other, up_other), [], (), "up_far_early")
+    pieces[3] = tied(pieces[3], far_early[:1], "piece_3")
+    far[3] = other_core(pieces[3])
     own_late, (down_other,) = up_own(
-        [pieces[k] for k in late], own_weights, [(down_weight, 1, False, 0, half)],
-        "up_own_late",
+        [pieces[k] for k in late], (gate_mine, up_mine), [(down_weight, 1, False, 0, half)],
+        (), "up_own_late",
     )
     hidden, (down_mine,) = hidden_call(
         [far[k] for k in late],
         late,
-        far_weights,
+        (gate_other, up_other),
         [(early, *own_early), (late, *own_late)],
         [(early, *far_early)],
         [pieces[k] for k in range(INNER)],
         [(down_weight, 1, True, 0, half)],
     )
 
-    middle, received, before = {}, {}, ()
-    halves = (((3, 2), "a"), ((1, 0), "b"))
+    received, sums, before = {}, {}, ()
+    halves = (((3, 1), "a"), ((2, 0), "b"))
     for held, name in halves:
-        sums = down_far(hidden, down_other, held, "down_far_" + name, before)
-        received[held] = other_core(sums)
-        before = (sums,)
+        partial = down_far(hidden, down_other, held, "down_far_" + name, before)
+        received[held] = other_core(partial)
+        before = (partial,)
     before = ()
     for held, name in halves:
-        sums = down_own(hidden, down_mine, received[held], held, "down_own_" + name, before)
-        before = (sums[0],)
-        for k, part in zip(held, sums):
-            middle[k] = second_hop(part, k) if k else part
-    split = sum_split([middle[k] for k in range(INNER)], "sum_split")
+        parts = down_own(hidden, down_mine, received[held], held, "down_own_" + name, before)
+        before = (parts[0],)
+        sums.update(zip(held, parts))
+    passed = add(sums[2], second_hop(sums[3], 1))
+    split = sum_split([sums[0], second_hop(sums[1], 1), second_hop(passed, 2)], "sum_split")
     ended = [split[0]] + [first_hop(split[k], k) for k in (3, 2, 1)]
     return sum_out(ended)
 

time: 86.1 us -> 73 us (0.85)
  the two profiles are of different devices: /device:TPU:13 before, /device:TPU:0 now
where the time goes in v3:
time: 73 us; the launch traced here: 71.7 us
  waiting for transfers between devices  26.5 us (36%)
  Pallas kernels  26.3 us (36%)
  starting transfers between devices  18.7 us (26%)
    pallas_call x17, Pallas kernels, call(): pl.pallas_call(kernel, out_shape=out_shape, in_specs=specs or [VMEM] * le...  26.3 us
    ppermute x12, waiting for transfers between devices, exchanged(): return lax.ppermute(array, ('expert', 'hsplit'), route)  25.6 us
    ppermute x12, starting transfers between devices, exchanged(): return lax.ppermute(array, ('expert', 'hsplit'), route)  17.1 us
    ppermute x6, starting transfers between devices, other_core(): return lax.ppermute(array, 'hsplit', [(0, 1), (1, 0)])  1.63 us
  transfers between devices with their start and end apart: 18, of which 11 were waited for; matrix products, arithmetic and copies ran while one was open for 0% of the time, Pallas kernels for 28%

profile of v3, /device:TPU:0, one launch (start us, length us, event | category | flops | bytes accessed | tf_op | source)
XLA Modules:
  0.0 71.7 jit_solution(9463980827800373276)
XLA Ops:
  0.0 1.0 %first_piece.1.refs_0_ = bf16[16,3712]{1,0:T(8,128)(2,1)S(1)} custom-call(bf16[16,7168]{1,0:T(8,128)(2,1)} %tok_in.1, s32[8,16]{1,0:T(8,128)} %bitcast.11, f32[8,16]{1,0:T(8,128)} %bitcast.12), custom_call_target="tpu_custom_call" | custom-call | tf_op jit(solution)/shard_map/first_piece/pallas_call | solution.py:48
  1.0 3.1 %collective-permute-start = (bf16[16,3712]{1,0:T(8,128)(2,1)S(1)}, bf16[16,3712]{1,0:T(8,128)(2,1)S(1)}, u32[]{:S(2)}, u32[]{:S(2)}) collective-permute-start(bf16[16,3712]{1,0:T(8,128)(2,1)S(1)} %first_piece.1.refs_0_), channel_id=1, source_target_pairs={{0,8},{2,10},{4,12},{6,14},{8,0},{10,2},{12,4},{14,6},{16,24},{18,... | collective-permute-start | bytes 356360 | tf_op jit(solution)/shard_map/ppermute | solution.py:20
  4.1 2.6 %collective-permute-start.1 = (bf16[16,3712]{1,0:T(8,128)(2,1)S(1)}, bf16[16,3712]{1,0:T(8,128)(2,1)S(1)}, u32[]{:S(2)}, u32[]{:S(2)}) collective-permute-start(bf16[16,3712]{1,0:T(8,128)(2,1)S(1)} %first_piece.1.refs_0_), channel_id=1, source_target_pairs={{0,16},{2,18},{4,20},{6,22},{8,24},{10,26},{12,28},{14,30},{16,0},... | collective-permute-start | bytes 356360 | tf_op jit(solution)/shard_map/ppermute | solution.py:20
  6.6 0.0 collective-permute-start.2
  6.6 3.1 %fetch_1.1 = (bf16[3584,1024]{1,0:T(8,128)(2,1)S(1)}, f32[8,128]{1,0:T(8,128)S(1)}) custom-call(bf16[7168,1024]{1,0:T(8,128)(2,1)} %bitcast.5), custom_call_target="tpu_custom_call" | custom-call | bytes 44040192 | tf_op jit(solution)/shard_map/fetch_1/pallas_call | solution.py:48
  9.7 0.0 collective-permute-done.refs_1_
  9.8 1.3 %collective-permute-done.1.refs_2_ = bf16[16,3712]{1,0:T(8,128)(2,1)S(1)} collective-permute-done((bf16[16,3712]{1,0:T(8,128)(2,1)S(1)}, bf16[16,3712]{1,0:T(8,128)(2,1)S(1)}, u32[]{:S(2)}, u32[]{:S(2)}) %collective-permute-start.1) | collective-permute-done | bytes 118816 | tf_op jit(solution)/shard_map/ppermute | solution.py:20
  11.1 2.4 %collective-permute-done.2.refs_3_ = bf16[16,3712]{1,0:T(8,128)(2,1)S(1)} collective-permute-done((bf16[16,3712]{1,0:T(8,128)(2,1)S(1)}, bf16[16,3712]{1,0:T(8,128)(2,1)S(1)}, u32[]{:S(2)}, u32[]{:S(2)}) %collective-permute-start.2) | collective-permute-done | bytes 118816 | tf_op jit(solution)/shard_map/ppermute | solution.py:20
  13.5 1.5 %collective-permute-start.3 = (bf16[64,3712]{1,0:T(8,128)(2,1)S(1)}, bf16[64,3712]{1,0:T(8,128)(2,1)S(1)}, u32[]{:S(2)}, u32[]{:S(2)}) collective-permute-start(bf16[64,3712]{1,0:T(8,128)(2,1)S(1)} %second.1.refs_0_.refs_10_), channel_id=1, source_target_pairs={{0,2},{2,0},{4,6},{6,4},{8,10},{10,8},{12,14},{14,12},{16,18},{18,... | collective-permute-start | bytes 1425416 | tf_op jit(solution)/shard_map/ppermute | solution.py:20
  15.0 1.8 %collective-permute-start.5 = (bf16[64,3712]{1,0:T(8,128)(2,1)S(1)}, bf16[64,3712]{1,0:T(8,128)(2,1)S(1)}, u32[]{:S(2)}, u32[]{:S(2)}) collective-permute-start(bf16[64,3712]{1,0:T(8,128)(2,1)S(1)} %second.1.refs_0_.refs_10_), channel_id=1, source_target_pairs={{0,4},{2,6},{4,0},{6,2},{8,12},{10,14},{12,8},{14,10},{16,20},{18,... | collective-permute-start | bytes 1425416 | tf_op jit(solution)/shard_map/ppermute | solution.py:20
  16.9 5.2 %fetch_2.1 = (bf16[3584,1024]{1,0:T(8,128)(2,1)S(1)}, bf16[3584,1024]{1,0:T(8,128)(2,1)S(1)}, f32[8,128]{1,0:T(8,128)S(1)}) custom-call(bf16[7168,1024]{1,0:T(8,128)(2,1)} %bitcast.7, bf16[7168,1024]{1,0:T(8,128)(2,1)} %bitcast.6), custom_call_target="tpu_custom_call" | custom-call | bytes 88080384 | tf_op jit(solution)/shard_map/fetch_2/pallas_call | solution.py:48
  22.1 0.1 collective-permute-start.7
  22.1 0.1 collective-permute-done.3.refs_1_.refs_0_.refs_11_
  22.2 1.4 %collective-permute-done.5.refs_0_ = bf16[64,3712]{1,0:T(8,128)(2,1)S(1)} collective-permute-done((bf16[64,3712]{1,0:T(8,128)(2,1)S(1)}, bf16[64,3712]{1,0:T(8,128)(2,1)S(1)}, u32[]{:S(2)}, u32[]{:S(2)}) %collective-permute-start.5) | collective-permute-done | bytes 475168 | tf_op jit(solution)/shard_map/ppermute | solution.py:20
  23.7 0.9 %collective-permute-start.8 = (bf16[64,3712]{1,0:T(8,128)(2,1)S(1)}, bf16[64,3712]{1,0:T(8,128)(2,1)S(1)}, u32[]{:S(2)}, u32[]{:S(2)}) collective-permute-start(bf16[64,3712]{1,0:T(8,128)(2,1)S(1)} %piece_2.1.refs_1_.refs_12_), channel_id=1, source_target_pairs={{0,1},{1,0},{2,3},{3,2},{4,5},{5,4},{6,7},{7,6},{8,9},{9,8},{10,11... | collective-permute-start | bytes 1425416 | tf_op jit(solution)/shard_map/ppermute | solution.py:32
  24.6 0.5 collective-permute-start.6
  25.1 0.0 collective-permute-start.4
  25.1 3.1 %up_own_early.1 = (f32[128,1024]{1,0:T(8,128)S(1)}, f32[128,1024]{1,0:T(8,128)S(1)}, bf16[3584,1024]{1,0:T(8,128)(2,1)S(1)}) custom-call(bf16[64,3712]{1,0:T(8,128)(2,1)S(1)} %second.1.refs_0_.refs_10_, bf16[64,3712]{1,0:T(8,128)(2,1)S(1)} %piece_2.1.refs_1_.refs_12_, bf16[3584,1024]{1,0:T(8,128)(2,1)S(1)} %get-tuple-element.31.refs_2_, ...), custom_call_target="tpu_custom_call" | custom-call | flops 5637144576 | bytes 44040192 | tf_op jit(solution)/shard_map/up_own_early/pallas_call | solution.py:48
  28.2 0.0 collective-permute-done.7.refs_0_
  28.2 0.0 collective-permute-done.8.refs_1_
  28.2 2.2 %up_far_early.1 = (f32[128,1024]{1,0:T(8,128)S(1)}, f32[128,1024]{1,0:T(8,128)S(1)}) custom-call(bf16[64,3712]{1,0:T(8,128)(2,1)S(1)} %collective-permute-done.7.refs_0_, bf16[64,3712]{1,0:T(8,128)(2,1)S(1)} %collective-permute-done.8.refs_1_, bf16[3584,1024]{1,0:T(8,128)(2,1)S(1)} %get-tuple-element.30.refs_2_, bf16[3584,1024]{1,0:T(8,128)(2,1)S(1)} %get-tuple-element.33.refs_3_), custom_call_target="tpu_custom_call" | custom-call | flops 5637144576 | tf_op jit(solution)/shard_map/up_far_early/pallas_call | solution.py:48
  30.5 2.8 %collective-permute-done.6.refs_0_ = bf16[64,3712]{1,0:T(8,128)(2,1)S(1)} collective-permute-done((bf16[64,3712]{1,0:T(8,128)(2,1)S(1)}, bf16[64,3712]{1,0:T(8,128)(2,1)S(1)}, u32[]{:S(2)}, u32[]{:S(2)}) %collective-permute-start.6) | collective-permute-done | bytes 475168 | tf_op jit(solution)/shard_map/ppermute | solution.py:20
  33.2 0.0 collective-permute-start.9
  33.2 3.1 %up_own_late.1 = (f32[128,1024]{1,0:T(8,128)S(1)}, f32[128,1024]{1,0:T(8,128)S(1)}, bf16[1024,3584]{1,0:T(8,128)(2,1)S(1)}) custom-call(bf16[64,3712]{1,0:T(8,128)(2,1)S(1)} %collective-permute-done.3.refs_1_.refs_0_.refs_11_, bf16[64,3712]{1,0:T(8,128)(2,1)S(1)} %piece_3.1.refs_1_.refs_13_, bf16[3584,1024]{1,0:T(8,128)(2,1)S(1)} %get-tuple-element.31.refs_2_, ...), custom_call_target="tpu_custom_call" | custom-call | flops 5637144576 | bytes 44040192 | tf_op jit(solution)/shard_map/up_own_late/pallas_call | solution.py:48
  36.4 0.0 collective-permute-done.9.refs_1_
  36.4 3.1 %hidden.1 = (bf16[256,1024]{1,0:T(8,128)(2,1)S(1)}, bf16[1024,3584]{1,0:T(8,128)(2,1)S(1)}) custom-call(bf16[64,3712]{1,0:T(8,128)(2,1)S(1)} %collective-permute-done.4.refs_0_, bf16[64,3712]{1,0:T(8,128)(2,1)S(1)} %collective-permute-done.9.refs_1_, bf16[3584,1024]{1,0:T(8,128)(2,1)S(1)} %get-tuple-element.30.refs_2_, ...), custom_call_target="tpu_custom_call" | custom-call | flops 5637144576 | bytes 44040192 | tf_op jit(solution)/shard_map/hidden/pallas_call | solution.py:48
  39.5 1.1 %down_far_a.1.rest_0_ = bf16[128,3584]{1,0:T(8,128)(2,1)S(1)} custom-call(bf16[256,1024]{1,0:T(8,128)(2,1)S(1)} %get-tuple-element.40.hid_ref, bf16[1024,3584]{1,0:T(8,128)(2,1)S(1)} %get-tuple-element.42.w_ref), custom_call_target="tpu_custom_call" | custom-call | flops 2818572288 | tf_op jit(solution)/shard_map/down_far_a/pallas_call | solution.py:48
  40.6 0.6 collective-permute-start.11
  41.2 1.1 %down_far_b.1 = bf16[128,3584]{1,0:T(8,128)(2,1)S(1)} custom-call(bf16[256,1024]{1,0:T(8,128)(2,1)S(1)} %get-tuple-element.40.hid_ref, bf16[1024,3584]{1,0:T(8,128)(2,1)S(1)} %get-tuple-element.42.w_ref, bf16[128,3584]{1,0:T(8,128)(2,1)S(1)} %down_far_a.1.rest_0_), custom_call_target="tpu_custom_call" | custom-call | flops 2818572288 | tf_op jit(solution)/shard_map/down_far_b/pallas_call | solution.py:48
  42.3 0.1 collective-permute-start.10
  42.4 0.9 %collective-permute-done.11.far_ref = bf16[128,3584]{1,0:T(8,128)(2,1)S(1)} collective-permute-done((bf16[128,3584]{1,0:T(8,128)(2,1)S(1)}, bf16[128,3584]{1,0:T(8,128)(2,1)S(1)}, u32[]{:S(2)}, u32[]{:S(2)}) %collective-permute-start.11) | collective-permute-done | bytes 917536 | tf_op jit(solution)/shard_map/ppermute | solution.py:32
  43.3 1.1 %down_own_a.1 = (bf16[64,3584]{1,0:T(8,128)(2,1)S(1)}, bf16[64,3584]{1,0:T(8,128)(2,1)S(1)}) custom-call(bf16[256,1024]{1,0:T(8,128)(2,1)S(1)} %get-tuple-element.40.hid_ref, bf16[1024,3584]{1,0:T(8,128)(2,1)S(1)} %get-tuple-element.41.w_ref, bf16[128,3584]{1,0:T(8,128)(2,1)S(1)} %collective-permute-done.11.far_ref), custom_call_target="tpu_custom_call" | custom-call | flops 2818572288 | tf_op jit(solution)/shard_map/down_own_a/pallas_call | solution.py:48
  44.4 0.6 collective-permute-start.13
  45.0 1.5 %collective-permute-start.12 = (bf16[64,3584]{1,0:T(8,128)(2,1)S(1)}, bf16[64,3584]{1,0:T(8,128)(2,1)S(1)}, u32[]{:S(2)}, u32[]{:S(2)}) collective-permute-start(bf16[64,3584]{1,0:T(8,128)(2,1)S(1)} %get-tuple-element.45), channel_id=1, source_target_pairs={{0,2},{2,0},{4,6},{6,4},{8,10},{10,8},{12,14},{14,12},{16,18},{18,... | collective-permute-start | bytes 1376264 | tf_op jit(solution)/shard_map/ppermute | solution.py:20
  46.5 0.0 collective-permute-done.10.far_ref
  46.5 1.1 %down_own_b.1 = (bf16[64,3584]{1,0:T(8,128)(2,1)S(1)}, bf16[64,3584]{1,0:T(8,128)(2,1)S(1)}) custom-call(bf16[256,1024]{1,0:T(8,128)(2,1)S(1)} %get-tuple-element.40.hid_ref, bf16[1024,3584]{1,0:T(8,128)(2,1)S(1)} %get-tuple-element.41.w_ref, bf16[128,3584]{1,0:T(8,128)(2,1)S(1)} %collective-permute-done.10.far_ref, ...), custom_call_target="tpu_custom_call" | custom-call | flops 2818572288 | tf_op jit(solution)/shard_map/down_own_b/pallas_call | solution.py:48
  47.7 5.3 %collective-permute-done.13.refs_1_ = bf16[64,3584]{1,0:T(8,128)(2,1)S(1)} collective-permute-done((bf16[64,3584]{1,0:T(8,128)(2,1)S(1)}, bf16[64,3584]{1,0:T(8,128)(2,1)S(1)}, u32[]{:S(2)}, u32[]{:S(2)}) %collective-permute-start.13) | collective-permute-done | bytes 458784 | tf_op jit(solution)/shard_map/ppermute | solution.py:20
  53.0 0.1 add.1
  53.1 1.0 %collective-permute-start.14 = (bf16[64,3584]{1,0:T(8,128)(2,1)S(1)}, bf16[64,3584]{1,0:T(8,128)(2,1)S(1)}, u32[]{:S(2)}, u32[]{:S(2)}) collective-permute-start(bf16[64,3584]{1,0:T(8,128)(2,1)S(1)} %add.1), channel_id=1, source_target_pairs={{0,4},{2,6},{4,0},{6,2},{8,12},{10,14},{12,8},{14,10},{16,20},{18,... | collective-permute-start | bytes 1376264 | tf_op jit(solution)/shard_map/ppermute | solution.py:20
  54.1 3.8 %collective-permute-done.12.refs_1_ = bf16[64,3584]{1,0:T(8,128)(2,1)S(1)} collective-permute-done((bf16[64,3584]{1,0:T(8,128)(2,1)S(1)}, bf16[64,3584]{1,0:T(8,128)(2,1)S(1)}, u32[]{:S(2)}, u32[]{:S(2)}) %collective-permute-start.12) | collective-permute-done | bytes 458784 | tf_op jit(solution)/shard_map/ppermute | solution.py:20
  57.9 3.7 %collective-permute-done.14.refs_2_ = bf16[64,3584]{1,0:T(8,128)(2,1)S(1)} collective-permute-done((bf16[64,3584]{1,0:T(8,128)(2,1)S(1)}, bf16[64,3584]{1,0:T(8,128)(2,1)S(1)}, u32[]{:S(2)}, u32[]{:S(2)}) %collective-permute-start.14) | collective-permute-done | bytes 458784 | tf_op jit(solution)/shard_map/ppermute | solution.py:20
  61.6 0.2 sum_split.1
  61.8 2.5 %collective-permute-start.15 = (bf16[16,3584]{1,0:T(8,128)(2,1)S(1)}, bf16[16,3584]{1,0:T(8,128)(2,1)S(1)}, u32[]{:S(2)}, u32[]{:S(2)}) collective-permute-start(bf16[16,3584]{1,0:T(8,128)(2,1)S(1)} %get-tuple-element.48), channel_id=1, source_target_pairs={{0,24},{2,26},{4,28},{6,30},{8,16},{10,18},{12,20},{14,22},{16,8},... | collective-permute-start | bytes 344072 | tf_op jit(solution)/shard_map/ppermute | solution.py:20
  64.3 0.0 collective-permute-start.16
  64.3 1.9 %collective-permute-start.17 = (bf16[16,3584]{1,0:T(8,128)(2,1)S(1)}, bf16[16,3584]{1,0:T(8,128)(2,1)S(1)}, u32[]{:S(2)}, u32[]{:S(2)}) collective-permute-start(bf16[16,3584]{1,0:T(8,128)(2,1)S(1)} %get-tuple-element.50), channel_id=1, source_target_pairs={{0,8},{2,10},{4,12},{6,14},{8,0},{10,2},{12,4},{14,6},{16,24},{18,... | collective-permute-start | bytes 344072 | tf_op jit(solution)/shard_map/ppermute | solution.py:20
  66.3 2.3 %collective-permute-done.15.refs_1_ = bf16[16,3584]{1,0:T(8,128)(2,1)S(1)} collective-permute-done((bf16[16,3584]{1,0:T(8,128)(2,1)S(1)}, bf16[16,3584]{1,0:T(8,128)(2,1)S(1)}, u32[]{:S(2)}, u32[]{:S(2)}) %collective-permute-start.15) | collective-permute-done | bytes 114720 | tf_op jit(solution)/shard_map/ppermute | solution.py:20
  68.6 2.4 %collective-permute-done.16.refs_2_ = bf16[16,3584]{1,0:T(8,128)(2,1)S(1)} collective-permute-done((bf16[16,3584]{1,0:T(8,128)(2,1)S(1)}, bf16[16,3584]{1,0:T(8,128)(2,1)S(1)}, u32[]{:S(2)}, u32[]{:S(2)}) %collective-permute-start.16) | collective-permute-done | bytes 114720 | tf_op jit(solution)/shard_map/ppermute | solution.py:20
  71.0 0.7 sum_out.1
  (5 shorter events, 0.0 us)
Async XLA Ops:
  1.0 8.8 %collective-permute-start = (bf16[16,3712]{1,0:T(8,128)(2,1)S(1)}, bf16[16,3712]{1,0:T(8,128)(2,1)S(1)}, u32[]{:S(2)}, u32[]{:S(2)}) collective-permute-start(bf16[16,3712]{1,0:T(8,128)(2,1)S(1)} %first_piece.1.refs_0_), channel_id=1, source_target_pairs={{0,8},{2,10},{4,12},{6,14},{8,0},{10,2},{12,4},{14,6},{16,24},{18,... | collective-permute-start | bytes 356360 | tf_op jit(solution)/shard_map/ppermute | solution.py:20
  4.1 7.0 %collective-permute-start.1 = (bf16[16,3712]{1,0:T(8,128)(2,1)S(1)}, bf16[16,3712]{1,0:T(8,128)(2,1)S(1)}, u32[]{:S(2)}, u32[]{:S(2)}) collective-permute-start(bf16[16,3712]{1,0:T(8,128)(2,1)S(1)} %first_piece.1.refs_0_), channel_id=1, source_target_pairs={{0,16},{2,18},{4,20},{6,22},{8,24},{10,26},{12,28},{14,30},{16,0},... | collective-permute-start | bytes 356360 | tf_op jit(solution)/shard_map/ppermute | solution.py:20
  6.6 6.8 %collective-permute-start.2 = (bf16[16,3712]{1,0:T(8,128)(2,1)S(1)}, bf16[16,3712]{1,0:T(8,128)(2,1)S(1)}, u32[]{:S(2)}, u32[]{:S(2)}) collective-permute-start(bf16[16,3712]{1,0:T(8,128)(2,1)S(1)} %first_piece.1.refs_0_), channel_id=1, source_target_pairs={{0,24},{2,26},{4,28},{6,30},{8,16},{10,18},{12,20},{14,22},{16,8},... | collective-permute-start | bytes 356360 | tf_op jit(solution)/shard_map/ppermute | solution.py:20
  13.5 8.7 %collective-permute-start.3 = (bf16[64,3712]{1,0:T(8,128)(2,1)S(1)}, bf16[64,3712]{1,0:T(8,128)(2,1)S(1)}, u32[]{:S(2)}, u32[]{:S(2)}) collective-permute-start(bf16[64,3712]{1,0:T(8,128)(2,1)S(1)} %second.1.refs_0_.refs_10_), channel_id=1, source_target_pairs={{0,2},{2,0},{4,6},{6,4},{8,10},{10,8},{12,14},{14,12},{16,18},{18,... | collective-permute-start | bytes 1425416 | tf_op jit(solution)/shard_map/ppermute | solution.py:20
  15.0 8.7 %collective-permute-start.5 = (bf16[64,3712]{1,0:T(8,128)(2,1)S(1)}, bf16[64,3712]{1,0:T(8,128)(2,1)S(1)}, u32[]{:S(2)}, u32[]{:S(2)}) collective-permute-start(bf16[64,3712]{1,0:T(8,128)(2,1)S(1)} %second.1.refs_0_.refs_10_), channel_id=1, source_target_pairs={{0,4},{2,6},{4,0},{6,2},{8,12},{10,14},{12,8},{14,10},{16,20},{18,... | collective-permute-start | bytes 1425416 | tf_op jit(solution)/shard_map/ppermute | solution.py:20
  22.1 6.1 %collective-permute-start.7 = (bf16[64,3712]{1,0:T(8,128)(2,1)S(1)}, bf16[64,3712]{1,0:T(8,128)(2,1)S(1)}, u32[]{:S(2)}, u32[]{:S(2)}) collective-permute-start(bf16[64,3712]{1,0:T(8,128)(2,1)S(1)} %second.1.refs_0_.refs_10_), channel_id=1, source_target_pairs={{0,1},{1,0},{2,3},{3,2},{4,5},{5,4},{6,7},{7,6},{8,9},{9,8},{10,11... | collective-permute-start | bytes 1425416 | tf_op jit(solution)/shard_map/ppermute | solution.py:32
  23.7 4.5 %collective-permute-start.8 = (bf16[64,3712]{1,0:T(8,128)(2,1)S(1)}, bf16[64,3712]{1,0:T(8,128)(2,1)S(1)}, u32[]{:S(2)}, u32[]{:S(2)}) collective-permute-start(bf16[64,3712]{1,0:T(8,128)(2,1)S(1)} %piece_2.1.refs_1_.refs_12_), channel_id=1, source_target_pairs={{0,1},{1,0},{2,3},{3,2},{4,5},{5,4},{6,7},{7,6},{8,9},{9,8},{10,11... | collective-permute-start | bytes 1425416 | tf_op jit(solution)/shard_map/ppermute | solution.py:32
  24.6 8.7 %collective-permute-start.6 = (bf16[64,3712]{1,0:T(8,128)(2,1)S(1)}, bf16[64,3712]{1,0:T(8,128)(2,1)S(1)}, u32[]{:S(2)}, u32[]{:S(2)}) collective-permute-start(bf16[64,3712]{1,0:T(8,128)(2,1)S(1)} %piece_2.1.refs_1_.refs_12_), channel_id=1, source_target_pairs={{0,2},{2,0},{4,6},{6,4},{8,10},{10,8},{12,14},{14,12},{16,18},{18,... | collective-permute-start | bytes 1425416 | tf_op jit(solution)/shard_map/ppermute | solution.py:20
  25.1 11.2 %collective-permute-start.4 = (bf16[64,3712]{1,0:T(8,128)(2,1)S(1)}, bf16[64,3712]{1,0:T(8,128)(2,1)S(1)}, u32[]{:S(2)}, u32[]{:S(2)}) collective-permute-start(bf16[64,3712]{1,0:T(8,128)(2,1)S(1)} %collective-permute-done.3.refs_1_.refs_0_.refs_11_), channel_id=1, source_target_pairs={{0,1},{1,0},{2,3},{3,2},{4,5},{5,4},{6,7},{7,6},{8,9},{9,8},{10,11... | collective-permute-start | bytes 1425416 | tf_op jit(solution)/shard_map/ppermute | solution.py:32
  33.2 3.1 %collective-permute-start.9 = (bf16[64,3712]{1,0:T(8,128)(2,1)S(1)}, bf16[64,3712]{1,0:T(8,128)(2,1)S(1)}, u32[]{:S(2)}, u32[]{:S(2)}) collective-permute-start(bf16[64,3712]{1,0:T(8,128)(2,1)S(1)} %piece_3.1.refs_1_.refs_13_), channel_id=1, source_target_pairs={{0,1},{1,0},{2,3},{3,2},{4,5},{5,4},{6,7},{7,6},{8,9},{9,8},{10,11... | collective-permute-start | bytes 1425416 | tf_op jit(solution)/shard_map/ppermute | solution.py:32
  40.6 2.7 %collective-permute-start.11 = (bf16[128,3584]{1,0:T(8,128)(2,1)S(1)}, bf16[128,3584]{1,0:T(8,128)(2,1)S(1)}, u32[]{:S(2)}, u32[]{:S(2)}) collective-permute-start(bf16[128,3584]{1,0:T(8,128)(2,1)S(1)} %down_far_a.1.rest_0_), channel_id=1, source_target_pairs={{0,1},{1,0},{2,3},{3,2},{4,5},{5,4},{6,7},{7,6},{8,9},{9,8},{10,11... | collective-permute-start | bytes 2752520 | tf_op jit(solution)/shard_map/ppermute | solution.py:32
  42.3 4.2 %collective-permute-start.10 = (bf16[128,3584]{1,0:T(8,128)(2,1)S(1)}, bf16[128,3584]{1,0:T(8,128)(2,1)S(1)}, u32[]{:S(2)}, u32[]{:S(2)}) collective-permute-start(bf16[128,3584]{1,0:T(8,128)(2,1)S(1)} %down_far_b.1), channel_id=1, source_target_pairs={{0,1},{1,0},{2,3},{3,2},{4,5},{5,4},{6,7},{7,6},{8,9},{9,8},{10,11... | collective-permute-start | bytes 2752520 | tf_op jit(solution)/shard_map/ppermute | solution.py:32
  44.4 8.5 %collective-permute-start.13 = (bf16[64,3584]{1,0:T(8,128)(2,1)S(1)}, bf16[64,3584]{1,0:T(8,128)(2,1)S(1)}, u32[]{:S(2)}, u32[]{:S(2)}) collective-permute-start(bf16[64,3584]{1,0:T(8,128)(2,1)S(1)} %get-tuple-element.43.rest_0_), channel_id=1, source_target_pairs={{0,2},{2,0},{4,6},{6,4},{8,10},{10,8},{12,14},{14,12},{16,18},{18,... | collective-permute-start | bytes 1376264 | tf_op jit(solution)/shard_map/ppermute | solution.py:20
  45.0 12.9 %collective-permute-start.12 = (bf16[64,3584]{1,0:T(8,128)(2,1)S(1)}, bf16[64,3584]{1,0:T(8,128)(2,1)S(1)}, u32[]{:S(2)}, u32[]{:S(2)}) collective-permute-start(bf16[64,3584]{1,0:T(8,128)(2,1)S(1)} %get-tuple-element.45), channel_id=1, source_target_pairs={{0,2},{2,0},{4,6},{6,4},{8,10},{10,8},{12,14},{14,12},{16,18},{18,... | collective-permute-start | bytes 1376264 | tf_op jit(solution)/shard_map/ppermute | solution.py:20
  53.1 8.5 %collective-permute-start.14 = (bf16[64,3584]{1,0:T(8,128)(2,1)S(1)}, bf16[64,3584]{1,0:T(8,128)(2,1)S(1)}, u32[]{:S(2)}, u32[]{:S(2)}) collective-permute-start(bf16[64,3584]{1,0:T(8,128)(2,1)S(1)} %add.1), channel_id=1, source_target_pairs={{0,4},{2,6},{4,0},{6,2},{8,12},{10,14},{12,8},{14,10},{16,20},{18,... | collective-permute-start | bytes 1376264 | tf_op jit(solution)/shard_map/ppermute | solution.py:20
  61.8 6.8 %collective-permute-start.15 = (bf16[16,3584]{1,0:T(8,128)(2,1)S(1)}, bf16[16,3584]{1,0:T(8,128)(2,1)S(1)}, u32[]{:S(2)}, u32[]{:S(2)}) collective-permute-start(bf16[16,3584]{1,0:T(8,128)(2,1)S(1)} %get-tuple-element.48), channel_id=1, source_target_pairs={{0,24},{2,26},{4,28},{6,30},{8,16},{10,18},{12,20},{14,22},{16,8},... | collective-permute-start | bytes 344072 | tf_op jit(solution)/shard_map/ppermute | solution.py:20
  64.3 6.6 %collective-permute-start.16 = (bf16[16,3584]{1,0:T(8,128)(2,1)S(1)}, bf16[16,3584]{1,0:T(8,128)(2,1)S(1)}, u32[]{:S(2)}, u32[]{:S(2)}) collective-permute-start(bf16[16,3584]{1,0:T(8,128)(2,1)S(1)} %get-tuple-element.49), channel_id=1, source_target_pairs={{0,16},{2,18},{4,20},{6,22},{8,24},{10,26},{12,28},{14,30},{16,0},... | collective-permute-start | bytes 344072 | tf_op jit(solution)/shard_map/ppermute | solution.py:20
  64.3 6.6 %collective-permute-start.17 = (bf16[16,3584]{1,0:T(8,128)(2,1)S(1)}, bf16[16,3584]{1,0:T(8,128)(2,1)S(1)}, u32[]{:S(2)}, u32[]{:S(2)}) collective-permute-start(bf16[16,3584]{1,0:T(8,128)(2,1)S(1)} %get-tuple-element.50), channel_id=1, source_target_pairs={{0,8},{2,10},{4,12},{6,14},{8,0},{10,2},{12,4},{14,6},{16,24},{18,... | collective-permute-start | bytes 344072 | tf_op jit(solution)/shard_map/ppermute | solution.py:20

commit v4 on v3

--- a/solution.py
+++ b/solution.py
@@ -287,6 +287,13 @@
     return results[0], results[1:]
 
 
+def product(x, weights, at):
+    for weight in weights:
+        if at < weight.shape[1]:
+            return jnp.dot(x, weight[:, at : at + TILE], preferred_element_type=jnp.float32)
+        at -= weight.shape[1]
+
+
 def down_far(hidden, weight, held, name, before=()):
     tokens, units = hidden.shape
     rows = tokens // INNER
@@ -294,40 +301,42 @@
     span = weight.shape[1]
 
     def kernel(hid_ref, w_ref, *rest):
-        out_ref = rest[-1]
         at = [jj * rows + k * block_rows for k in held for jj in range(INNER)]
         x = jnp.concatenate([hid_ref[a : a + block_rows] for a in at], axis=0)
         for at in range(0, span, TILE):
-            out_ref[:, at : at + TILE] = jnp.dot(
-                x, w_ref[:, at : at + TILE], preferred_element_type=jnp.float32
-            ).astype(out_ref.dtype)
-
-    out_rows = len(held) * rows
+            total = product(x, [w_ref], at).astype(jnp.bfloat16)
+            for n in range(len(held)):
+                rest[len(before) + n][:, at : at + TILE] = total[n * rows : (n + 1) * rows]
+
     return call(
-        kernel, kept(out_rows, span), (hidden, weight, *before), name, flops=2 * out_rows * units * span
-    )
-
-
-def down_own(hidden, weight, received, held, name, before=()):
+        kernel, [kept(rows, span) for _ in held], (hidden, weight, *before), name,
+        flops=2 * len(held) * rows * units * span,
+    )
+
+
+def down_own(hidden, weights, received, held, name, before=()):
     tokens, units = hidden.shape
     rows = tokens // INNER
-    span = weight.shape[1]
-
-    def kernel(hid_ref, w_ref, far_ref, *rest):
-        out_refs = rest[len(before) :]
-        x = jnp.concatenate([hid_ref[k * rows : (k + 1) * rows] for k in held], axis=0)
+    span = sum(weight.shape[1] for weight in weights)
+    args = (hidden, *weights, *received, *before)
+    dtype = jnp.bfloat16 if received else jnp.float32
+
+    def kernel(*refs):
+        weight_refs = refs[1 : 1 + len(weights)]
+        far_refs = refs[1 + len(weights) : 1 + len(weights) + len(received)]
+        out_refs = refs[len(args) :]
+        x = jnp.concatenate([refs[0][k * rows : (k + 1) * rows] for k in held], axis=0)
         for at in range(0, span, TILE):
             columns = slice(at, at + TILE)
-            total = jnp.dot(x, w_ref[:, columns], preferred_element_type=jnp.float32)
-            total = (total + far_ref[:, columns].astype(jnp.float32)).astype(jnp.bfloat16)
+            total = product(x, weight_refs, at)
             for n in range(len(held)):
-                out_refs[n][:, columns] = total[n * rows : (n + 1) * rows]
+                part = total[n * rows : (n + 1) * rows]
+                if far_refs:
+                    part = part + far_refs[n][:, columns].astype(jnp.float32)
+                out_refs[n][:, columns] = part.astype(dtype)
 
     return call(
-        kernel,
-        [kept(rows, span) for _ in held],
-        (hidden, weight, received, *before),
-        name,
+        kernel, [kept(rows, span, dtype) for _ in held], args, name,
         flops=2 * len(held) * rows * units * span,
     )
 
@@ -338,23 +347,45 @@
     )
 
 
-def add(*parts):
-    def kernel(*refs):
-        refs[-1][...] = summed(refs[:-1])
-
-    return call(kernel, kept(*parts[0].shape), parts, "add")
-
-
-def sum_split(parts, name):
+def add(parts, name, cuts=None, before=()):
+    rows, width = parts[0].shape
+    cuts = cuts or [width]
+    args = (*parts, *before)
+
+    def kernel(*refs):
+        at = 0
+        for n, cut in enumerate(cuts):
+            refs[len(args) + n][...] = summed([ref.at[:, pl.ds(at, cut)] for ref in refs[: len(parts)]])
+            at += cut
+
+    return call(kernel, [kept(rows, cut) for cut in cuts], args, name)
+
+
+def add_side(whole, at, part, name):
+    rows, width = part.shape
+
+    def kernel(whole_ref, part_ref, out_ref):
+        out_ref[...] = summed([whole_ref.at[:, pl.ds(at, width)], part_ref])
+
+    return call(kernel, [kept(rows, width)], (whole, part), name)
+
+
+def sum_split(parts, sides, name):
     rows, span = parts[0].shape
     rows //= INNER
-
-    def kernel(*refs):
-        total = summed(refs[: len(parts)])
-        for k in range(INNER):
-            refs[len(parts) + k][...] = total[k * rows : (k + 1) * rows]
-
-    return call(kernel, [kept(rows, span) for _ in range(INNER)], parts, name)
+    args = (*parts, *sides)
+
+    def kernel(*refs):
+        at = 0
+        for n, side in enumerate(sides):
+            width = side.shape[1]
+            columns = pl.ds(at, width)
+            total = summed([ref.at[:, columns] for ref in refs[: len(parts)]] + [refs[len(parts) + n]])
+            for k in range(INNER):
+                refs[len(args) + k][:, columns] = total[k * rows : (k + 1) * rows]
+            at += width
+
+    return call(kernel, [kept(rows, span) for _ in range(INNER)], args, name)
 
 
 def sum_out(parts):
@@ -388,36 +419,46 @@
         [pieces[k] for k in early], (gate_mine, up_mine), [(up_weight, 0, False, 0, half)], (),
         "up_own_early",
     )
-    far_early, _ = up_own([far[k] for k in early], (gate_other, up_other), [], (), "up_far_early")
+    far_early, (down_other,) = up_own(
+        [far[k] for k in early], (gate_other, up_other), [(down_weight, 1, False, 0, half)], (),
+        "up_far_early",
+    )
     pieces[3] = tied(pieces[3], far_early[:1], "piece_3")
     far[3] = other_core(pieces[3])
-    own_late, (down_other,) = up_own(
-        [pieces[k] for k in late], (gate_mine, up_mine), [(down_weight, 1, False, 0, half)],
+    side = half // 2
+    own_late, (down_left,) = up_own(
+        [pieces[k] for k in late], (gate_mine, up_mine), [(down_weight, 1, True, 0, side)],
         (), "up_own_late",
     )
-    hidden, (down_mine,) = hidden_call(
+    hidden, (down_right,) = hidden_call(
         [far[k] for k in late],
         late,
         (gate_other, up_other),
         [(early, *own_early), (late, *own_late)],
         [(early, *far_early)],
         [pieces[k] for k in range(INNER)],
-        [(down_weight, 1, True, 0, half)],
-    )
-
-    received, sums, before = {}, {}, ()
-    halves = (((3, 1), "a"), ((2, 0), "b"))
-    for held, name in halves:
+        [(down_weight, 1, True, side, side)],
+    )
+
+    down_mine = (down_left, down_right)
+    received, before = {}, ()
+    for held, name in (((3, 1), "a"), ((2, 0), "b")):
         partial = down_far(hidden, down_other, held, "down_far_" + name, before)
-        received[held] = other_core(partial)
-        before = (partial,)
-    before = ()
-    for held, name in halves:
-        parts = down_own(hidden, down_mine, received[held], held, "down_own_" + name, before)
-        before = (parts[0],)
-        sums.update(zip(held, parts))
-    passed = add(sums[2], second_hop(sums[3], 1))
-    split = sum_split([sums[0], second_hop(sums[1], 1), second_hop(passed, 2)], "sum_split")
+        for k, part in zip(held, partial):
+            received[k] = other_core(part)
+        before = (partial[0],)
+    mine_3, mine_1 = down_own(hidden, down_mine, (), (3, 1), "down_own_a", before)
+    sides_3 = add((mine_3, received[3]), "sum_3", [side, half - side])
+    passed = [second_hop(part, 1) for part in sides_3]
+    (sum_1,) = add((mine_1, received[1]), "sum_1", before=sides_3)
+    sum_2, sum_0 = down_own(hidden, down_mine, (received[2], received[0]), (2, 0), "down_own_b", (sum_1,))
+    sum_1 = second_hop(sum_1, 1)
+    sides_2, at = [], 0
+    for n, part in enumerate(passed):
+        (total,) = add_side(sum_2, at, part, "sum_2_%d" % n)
+        sides_2.append(second_hop(total, 2))
+        at += part.shape[1]
+    split = sum_split([sum_0, sum_1], sides_2, "sum_split")
     ended = [split[0]] + [first_hop(split[k], k) for k in (3, 2, 1)]
     return sum_out(ended)
 

time: 73 us -> 69.2 us (0.948)
  waiting for transfers between devices: 26.5 us -> 20.5 us
  starting transfers between devices: 18.7 us -> 20.9 us
    ppermute x12 -> x14, waiting for transfers between devices: 25.6 us -> 20.5 us  [exchanged(): return lax.ppermute(array, ('expert', 'hsplit'), route)]
    ppermute x12 -> x14, starting transfers between devices: 17.1 us -> 18.7 us  [exchanged(): return lax.ppermute(array, ('expert', 'hsplit'), route)]
    ppermute x6 -> x8, waiting for transfers between devices: 0.9 us -> 0.02 us  [other_core(): return lax.ppermute(array, 'hsplit', [(0, 1), (1, 0)])]
    ppermute x6 -> x8, starting transfers between devices: 1.63 us -> 2.21 us  [other_core(): return lax.ppermute(array, 'hsplit', [(0, 1), (1, 0)])]
    pallas_call x17 -> x20, Pallas kernels: 26.3 us -> 26.4 us  [call(): pl.pallas_call(kernel, out_shape=out_shape, in_specs=specs or [VMEM] * le...]
  transfers between devices with their start and end apart: 18 -> 22, of which waited for: 11 -> 11; matrix products, arithmetic and copies ran while one was open for 0% -> 0% of each run, Pallas kernels for 28% -> 30%
where the time goes in v4:
time: 69.2 us; the launch traced here: 68 us
  Pallas kernels  26.4 us (38%)
  starting transfers between devices  20.9 us (30%)
  waiting for transfers between devices  20.5 us (30%)
    pallas_call x20, Pallas kernels, call(): pl.pallas_call(kernel, out_shape=out_shape, in_specs=specs or [VMEM] * le...  26.4 us
    ppermute x14, waiting for transfers between devices, exchanged(): return lax.ppermute(array, ('expert', 'hsplit'), route)  20.5 us
    ppermute x14, starting transfers between devices, exchanged(): return lax.ppermute(array, ('expert', 'hsplit'), route)  18.7 us
    ppermute x8, starting transfers between devices, other_core(): return lax.ppermute(array, 'hsplit', [(0, 1), (1, 0)])  2.21 us
  transfers between devices with their start and end apart: 22, of which 11 were waited for; matrix products, arithmetic and copies ran while one was open for 0% of the time, Pallas kernels for 30%

profile of v4, /device:TPU:0, one launch (start us, length us, event | category | flops | bytes accessed | tf_op | source)
XLA Modules:
  0.0 68.0 jit_solution(12443102236713819838)
XLA Ops:
  0.0 1.0 %first_piece.1.refs_0_ = bf16[16,3712]{1,0:T(8,128)(2,1)S(1)} custom-call(bf16[16,7168]{1,0:T(8,128)(2,1)} %tok_in.1, s32[8,16]{1,0:T(8,128)} %bitcast.12, f32[8,16]{1,0:T(8,128)} %bitcast.13), custom_call_target="tpu_custom_call" | custom-call | tf_op jit(solution)/shard_map/first_piece/pallas_call | solution.py:48
  1.0 3.1 %collective-permute-start = (bf16[16,3712]{1,0:T(8,128)(2,1)S(1)}, bf16[16,3712]{1,0:T(8,128)(2,1)S(1)}, u32[]{:S(2)}, u32[]{:S(2)}) collective-permute-start(bf16[16,3712]{1,0:T(8,128)(2,1)S(1)} %first_piece.1.refs_0_), channel_id=1, source_target_pairs={{0,8},{2,10},{4,12},{6,14},{8,0},{10,2},{12,4},{14,6},{16,24},{18,... | collective-permute-start | bytes 356360 | tf_op jit(solution)/shard_map/ppermute | solution.py:20
  4.1 2.6 %collective-permute-start.1 = (bf16[16,3712]{1,0:T(8,128)(2,1)S(1)}, bf16[16,3712]{1,0:T(8,128)(2,1)S(1)}, u32[]{:S(2)}, u32[]{:S(2)}) collective-permute-start(bf16[16,3712]{1,0:T(8,128)(2,1)S(1)} %first_piece.1.refs_0_), channel_id=1, source_target_pairs={{0,16},{2,18},{4,20},{6,22},{8,24},{10,26},{12,28},{14,30},{16,0},... | collective-permute-start | bytes 356360 | tf_op jit(solution)/shard_map/ppermute | solution.py:20
  6.6 0.0 collective-permute-start.2
  6.6 3.1 %fetch_1.1 = (bf16[3584,1024]{1,0:T(8,128)(2,1)S(1)}, f32[8,128]{1,0:T(8,128)S(1)}) custom-call(bf16[7168,1024]{1,0:T(8,128)(2,1)} %bitcast.8), custom_call_target="tpu_custom_call" | custom-call | bytes 44040192 | tf_op jit(solution)/shard_map/fetch_1/pallas_call | solution.py:48
  9.7 0.0 collective-permute-done.refs_1_
  9.8 1.3 %collective-permute-done.1.refs_2_ = bf16[16,3712]{1,0:T(8,128)(2,1)S(1)} collective-permute-done((bf16[16,3712]{1,0:T(8,128)(2,1)S(1)}, bf16[16,3712]{1,0:T(8,128)(2,1)S(1)}, u32[]{:S(2)}, u32[]{:S(2)}) %collective-permute-start.1) | collective-permute-done | bytes 118816 | tf_op jit(solution)/shard_map/ppermute | solution.py:20
  11.1 2.4 %collective-permute-done.2.refs_3_ = bf16[16,3712]{1,0:T(8,128)(2,1)S(1)} collective-permute-done((bf16[16,3712]{1,0:T(8,128)(2,1)S(1)}, bf16[16,3712]{1,0:T(8,128)(2,1)S(1)}, u32[]{:S(2)}, u32[]{:S(2)}) %collective-permute-start.2) | collective-permute-done | bytes 118816 | tf_op jit(solution)/shard_map/ppermute | solution.py:20
  13.5 1.5 %collective-permute-start.3 = (bf16[64,3712]{1,0:T(8,128)(2,1)S(1)}, bf16[64,3712]{1,0:T(8,128)(2,1)S(1)}, u32[]{:S(2)}, u32[]{:S(2)}) collective-permute-start(bf16[64,3712]{1,0:T(8,128)(2,1)S(1)} %second.1.refs_0_.refs_10_), channel_id=1, source_target_pairs={{0,2},{2,0},{4,6},{6,4},{8,10},{10,8},{12,14},{14,12},{16,18},{18,... | collective-permute-start | bytes 1425416 | tf_op jit(solution)/shard_map/ppermute | solution.py:20
  15.0 1.8 %collective-permute-start.5 = (bf16[64,3712]{1,0:T(8,128)(2,1)S(1)}, bf16[64,3712]{1,0:T(8,128)(2,1)S(1)}, u32[]{:S(2)}, u32[]{:S(2)}) collective-permute-start(bf16[64,3712]{1,0:T(8,128)(2,1)S(1)} %second.1.refs_0_.refs_10_), channel_id=1, source_target_pairs={{0,4},{2,6},{4,0},{6,2},{8,12},{10,14},{12,8},{14,10},{16,20},{18,... | collective-permute-start | bytes 1425416 | tf_op jit(solution)/shard_map/ppermute | solution.py:20
  16.9 5.2 %fetch_2.1 = (bf16[3584,1024]{1,0:T(8,128)(2,1)S(1)}, bf16[3584,1024]{1,0:T(8,128)(2,1)S(1)}, f32[8,128]{1,0:T(8,128)S(1)}) custom-call(bf16[7168,1024]{1,0:T(8,128)(2,1)} %bitcast.10, bf16[7168,1024]{1,0:T(8,128)(2,1)} %bitcast.9), custom_call_target="tpu_custom_call" | custom-call | bytes 88080384 | tf_op jit(solution)/shard_map/fetch_2/pallas_call | solution.py:48
  22.1 0.1 collective-permute-start.7
  22.1 0.1 collective-permute-done.3.refs_1_.refs_0_.refs_11_
  22.2 1.4 %collective-permute-done.5.refs_0_ = bf16[64,3712]{1,0:T(8,128)(2,1)S(1)} collective-permute-done((bf16[64,3712]{1,0:T(8,128)(2,1)S(1)}, bf16[64,3712]{1,0:T(8,128)(2,1)S(1)}, u32[]{:S(2)}, u32[]{:S(2)}) %collective-permute-start.5) | collective-permute-done | bytes 475168 | tf_op jit(solution)/shard_map/ppermute | solution.py:20
  23.7 0.9 %collective-permute-start.8 = (bf16[64,3712]{1,0:T(8,128)(2,1)S(1)}, bf16[64,3712]{1,0:T(8,128)(2,1)S(1)}, u32[]{:S(2)}, u32[]{:S(2)}) collective-permute-start(bf16[64,3712]{1,0:T(8,128)(2,1)S(1)} %piece_2.1.refs_1_.refs_12_), channel_id=1, source_target_pairs={{0,1},{1,0},{2,3},{3,2},{4,5},{5,4},{6,7},{7,6},{8,9},{9,8},{10,11... | collective-permute-start | bytes 1425416 | tf_op jit(solution)/shard_map/ppermute | solution.py:32
  24.6 0.5 collective-permute-start.6
  25.1 3.1 %up_own_early.1 = (f32[128,1024]{1,0:T(8,128)S(1)}, f32[128,1024]{1,0:T(8,128)S(1)}, bf16[3584,1024]{1,0:T(8,128)(2,1)S(1)}) custom-call(bf16[64,3712]{1,0:T(8,128)(2,1)S(1)} %second.1.refs_0_.refs_10_, bf16[64,3712]{1,0:T(8,128)(2,1)S(1)} %piece_2.1.refs_1_.refs_12_, bf16[3584,1024]{1,0:T(8,128)(2,1)S(1)} %get-tuple-element.38.refs_2_, ...), custom_call_target="tpu_custom_call" | custom-call | flops 5637144576 | bytes 44040192 | tf_op jit(solution)/shard_map/up_own_early/pallas_call | solution.py:48
  28.2 3.1 %up_far_early.1 = (f32[128,1024]{1,0:T(8,128)S(1)}, f32[128,1024]{1,0:T(8,128)S(1)}, bf16[1024,3584]{1,0:T(8,128)(2,1)S(1)}) custom-call(bf16[64,3712]{1,0:T(8,128)(2,1)S(1)} %collective-permute-done.7.refs_0_, bf16[64,3712]{1,0:T(8,128)(2,1)S(1)} %collective-permute-done.8.refs_1_, bf16[3584,1024]{1,0:T(8,128)(2,1)S(1)} %get-tuple-element.37.refs_2_, ...), custom_call_target="tpu_custom_call" | custom-call | flops 5637144576 | bytes 44040192 | tf_op jit(solution)/shard_map/up_far_early/pallas_call | solution.py:48
  31.3 1.9 %collective-permute-done.6.refs_0_ = bf16[64,3712]{1,0:T(8,128)(2,1)S(1)} collective-permute-done((bf16[64,3712]{1,0:T(8,128)(2,1)S(1)}, bf16[64,3712]{1,0:T(8,128)(2,1)S(1)}, u32[]{:S(2)}, u32[]{:S(2)}) %collective-permute-start.6) | collective-permute-done | bytes 475168 | tf_op jit(solution)/shard_map/ppermute | solution.py:20
  33.2 2.3 %up_own_late.1 = (f32[128,1024]{1,0:T(8,128)S(1)}, f32[128,1024]{1,0:T(8,128)S(1)}, bf16[1024,1792]{1,0:T(8,128)(2,1)S(1)}) custom-call(bf16[64,3712]{1,0:T(8,128)(2,1)S(1)} %collective-permute-done.3.refs_1_.refs_0_.refs_11_, bf16[64,3712]{1,0:T(8,128)(2,1)S(1)} %piece_3.1.refs_1_.refs_13_, bf16[3584,1024]{1,0:T(8,128)(2,1)S(1)} %get-tuple-element.38.refs_2_, ...), custom_call_target="tpu_custom_call" | custom-call | flops 5637144576 | bytes 22020096 | tf_op jit(solution)/shard_map/up_own_late/pallas_call | solution.py:48
  35.6 2.9 %hidden.1 = (bf16[256,1024]{1,0:T(8,128)(2,1)S(1)}, bf16[1024,1792]{1,0:T(8,128)(2,1)S(1)}) custom-call(bf16[64,3712]{1,0:T(8,128)(2,1)S(1)} %collective-permute-done.4.refs_0_, bf16[64,3712]{1,0:T(8,128)(2,1)S(1)} %collective-permute-done.9.refs_1_, bf16[3584,1024]{1,0:T(8,128)(2,1)S(1)} %get-tuple-element.37.refs_2_, ...), custom_call_target="tpu_custom_call" | custom-call | flops 5637144576 | bytes 22020096 | tf_op jit(solution)/shard_map/hidden/pallas_call | solution.py:48
  38.5 1.1 %down_far_a.1 = (bf16[64,3584]{1,0:T(8,128)(2,1)S(1)}, bf16[64,3584]{1,0:T(8,128)(2,1)S(1)}) custom-call(bf16[256,1024]{1,0:T(8,128)(2,1)S(1)} %get-tuple-element.47.hid_ref.refs_0_, bf16[1024,3584]{1,0:T(8,128)(2,1)S(1)} %get-tuple-element.50.w_ref), custom_call_target="tpu_custom_call" | custom-call | flops 2818572288 | tf_op jit(solution)/shard_map/down_far_a/pallas_call | solution.py:48
  39.7 0.6 collective-permute-start.13
  40.2 0.1 collective-permute-start.12
  40.3 1.1 %down_far_b.1 = (bf16[64,3584]{1,0:T(8,128)(2,1)S(1)}, bf16[64,3584]{1,0:T(8,128)(2,1)S(1)}) custom-call(bf16[256,1024]{1,0:T(8,128)(2,1)S(1)} %get-tuple-element.47.hid_ref.refs_0_, bf16[1024,3584]{1,0:T(8,128)(2,1)S(1)} %get-tuple-element.50.w_ref, bf16[64,3584]{1,0:T(8,128)(2,1)S(1)} %get-tuple-element.51.rest_0_), custom_call_target="tpu_custom_call" | custom-call | flops 2818572288 | tf_op jit(solution)/shard_map/down_far_b/pallas_call | solution.py:48
  41.4 0.5 collective-permute-start.10
  41.9 0.1 collective-permute-start.11
  42.0 1.1 %down_own_a.1 = (f32[64,3584]{1,0:T(8,128)S(1)}, f32[64,3584]{1,0:T(8,128)S(1)}) custom-call(bf16[256,1024]{1,0:T(8,128)(2,1)S(1)} %get-tuple-element.47.hid_ref.refs_0_, bf16[1024,1792]{1,0:T(8,128)(2,1)S(1)} %get-tuple-element.48.refs_1_, bf16[1024,1792]{1,0:T(8,128)(2,1)S(1)} %get-tuple-element.49.refs_2_, bf16[64,3584]{1,0:T(8,128)(2,1)S(1)} %get-tuple-element.52.refs_3_), custom_call_target="tpu_custom_call" | custom-call | flops 2818572288 | tf_op jit(solution)/shard_map/down_own_a/pallas_call | solution.py:48
  43.2 0.1 sum_3.1
  43.3 0.6 collective-permute-start.17
  43.9 1.5 %collective-permute-start.15 = (bf16[64,1792]{1,0:T(8,128)(2,1)S(1)}, bf16[64,1792]{1,0:T(8,128)(2,1)S(1)}, u32[]{:S(2)}, u32[]{:S(2)}) collective-permute-start(bf16[64,1792]{1,0:T(8,128)(2,1)S(1)} %get-tuple-element.57.refs_2_), channel_id=1, source_target_pairs={{0,2},{2,0},{4,6},{6,4},{8,10},{10,8},{12,14},{14,12},{16,18},{18,... | collective-permute-start | bytes 688136 | tf_op jit(solution)/shard_map/ppermute | solution.py:20
  45.4 0.1 sum_1.1.refs_5_
  45.4 0.6 collective-permute-start.14
  46.0 1.2 %down_own_b.1 = (bf16[64,3584]{1,0:T(8,128)(2,1)S(1)}, bf16[64,3584]{1,0:T(8,128)(2,1)S(1)}) custom-call(bf16[256,1024]{1,0:T(8,128)(2,1)S(1)} %get-tuple-element.47.hid_ref.refs_0_, bf16[1024,1792]{1,0:T(8,128)(2,1)S(1)} %get-tuple-element.48.refs_1_, bf16[1024,1792]{1,0:T(8,128)(2,1)S(1)} %get-tuple-element.49.refs_2_, ...), custom_call_target="tpu_custom_call" | custom-call | flops 2818572288 | tf_op jit(solution)/shard_map/down_own_b/pallas_call | solution.py:48
  47.2 2.1 %collective-permute-done.17.part_ref = bf16[64,1792]{1,0:T(8,128)(2,1)S(1)} collective-permute-done((bf16[64,1792]{1,0:T(8,128)(2,1)S(1)}, bf16[64,1792]{1,0:T(8,128)(2,1)S(1)}, u32[]{:S(2)}, u32[]{:S(2)}) %collective-permute-start.17) | collective-permute-done | bytes 229408 | tf_op jit(solution)/shard_map/ppermute | solution.py:20
  49.4 0.1 sum_2_1.1
  49.4 1.0 %collective-permute-start.18 = (bf16[64,1792]{1,0:T(8,128)(2,1)S(1)}, bf16[64,1792]{1,0:T(8,128)(2,1)S(1)}, u32[]{:S(2)}, u32[]{:S(2)}) collective-permute-start(bf16[64,1792]{1,0:T(8,128)(2,1)S(1)} %sum_2_1.1), channel_id=1, source_target_pairs={{0,4},{2,6},{4,0},{6,2},{8,12},{10,14},{12,8},{14,10},{16,20},{18,... | collective-permute-start | bytes 688136 | tf_op jit(solution)/shard_map/ppermute | solution.py:20
  50.4 1.4 %collective-permute-done.15.part_ref = bf16[64,1792]{1,0:T(8,128)(2,1)S(1)} collective-permute-done((bf16[64,1792]{1,0:T(8,128)(2,1)S(1)}, bf16[64,1792]{1,0:T(8,128)(2,1)S(1)}, u32[]{:S(2)}, u32[]{:S(2)}) %collective-permute-start.15) | collective-permute-done | bytes 229408 | tf_op jit(solution)/shard_map/ppermute | solution.py:20
  51.8 0.1 sum_2_0.1
  51.9 1.0 %collective-permute-start.16 = (bf16[64,1792]{1,0:T(8,128)(2,1)S(1)}, bf16[64,1792]{1,0:T(8,128)(2,1)S(1)}, u32[]{:S(2)}, u32[]{:S(2)}) collective-permute-start(bf16[64,1792]{1,0:T(8,128)(2,1)S(1)} %sum_2_0.1), channel_id=1, source_target_pairs={{0,4},{2,6},{4,0},{6,2},{8,12},{10,14},{12,8},{14,10},{16,20},{18,... | collective-permute-start | bytes 688136 | tf_op jit(solution)/shard_map/ppermute | solution.py:20
  52.9 2.6 %collective-permute-done.18.refs_3_ = bf16[64,1792]{1,0:T(8,128)(2,1)S(1)} collective-permute-done((bf16[64,1792]{1,0:T(8,128)(2,1)S(1)}, bf16[64,1792]{1,0:T(8,128)(2,1)S(1)}, u32[]{:S(2)}, u32[]{:S(2)}) %collective-permute-start.18) | collective-permute-done | bytes 229408 | tf_op jit(solution)/shard_map/ppermute | solution.py:20
  55.5 2.5 %collective-permute-done.16.refs_2_ = bf16[64,1792]{1,0:T(8,128)(2,1)S(1)} collective-permute-done((bf16[64,1792]{1,0:T(8,128)(2,1)S(1)}, bf16[64,1792]{1,0:T(8,128)(2,1)S(1)}, u32[]{:S(2)}, u32[]{:S(2)}) %collective-permute-start.16) | collective-permute-done | bytes 229408 | tf_op jit(solution)/shard_map/ppermute | solution.py:20
  58.0 0.2 sum_split.1
  58.1 2.5 %collective-permute-start.19 = (bf16[16,3584]{1,0:T(8,128)(2,1)S(1)}, bf16[16,3584]{1,0:T(8,128)(2,1)S(1)}, u32[]{:S(2)}, u32[]{:S(2)}) collective-permute-start(bf16[16,3584]{1,0:T(8,128)(2,1)S(1)} %get-tuple-element.62), channel_id=1, source_target_pairs={{0,24},{2,26},{4,28},{6,30},{8,16},{10,18},{12,20},{14,22},{16,8},... | collective-permute-start | bytes 344072 | tf_op jit(solution)/shard_map/ppermute | solution.py:20
  60.7 1.9 %collective-permute-start.21 = (bf16[16,3584]{1,0:T(8,128)(2,1)S(1)}, bf16[16,3584]{1,0:T(8,128)(2,1)S(1)}, u32[]{:S(2)}, u32[]{:S(2)}) collective-permute-start(bf16[16,3584]{1,0:T(8,128)(2,1)S(1)} %get-tuple-element.64), channel_id=1, source_target_pairs={{0,8},{2,10},{4,12},{6,14},{8,0},{10,2},{12,4},{14,6},{16,24},{18,... | collective-permute-start | bytes 344072 | tf_op jit(solution)/shard_map/ppermute | solution.py:20
  62.6 2.4 %collective-permute-done.19.refs_1_ = bf16[16,3584]{1,0:T(8,128)(2,1)S(1)} collective-permute-done((bf16[16,3584]{1,0:T(8,128)(2,1)S(1)}, bf16[16,3584]{1,0:T(8,128)(2,1)S(1)}, u32[]{:S(2)}, u32[]{:S(2)}) %collective-permute-start.19) | collective-permute-done | bytes 114720 | tf_op jit(solution)/shard_map/ppermute | solution.py:20
  64.9 2.4 %collective-permute-done.20.refs_2_ = bf16[16,3584]{1,0:T(8,128)(2,1)S(1)} collective-permute-done((bf16[16,3584]{1,0:T(8,128)(2,1)S(1)}, bf16[16,3584]{1,0:T(8,128)(2,1)S(1)}, u32[]{:S(2)}, u32[]{:S(2)}) %collective-permute-start.20) | collective-permute-done | bytes 114720 | tf_op jit(solution)/shard_map/ppermute | solution.py:20
  67.3 0.7 %sum_out.1 = bf16[16,3584]{1,0:T(8,128)(2,1)} custom-call(bf16[16,3584]{1,0:T(8,128)(2,1)S(1)} %get-tuple-element.61.refs_0_, bf16[16,3584]{1,0:T(8,128)(2,1)S(1)} %collective-permute-done.19.refs_1_, bf16[16,3584]{1,0:T(8,128)(2,1)S(1)} %collective-permute-done.20.refs_2_, bf16[16,3584]{1,0:T(8,128)(2,1)S(1)} %collective-permute-done.21.refs_3_), custom_call_target="tpu_custom_call" | custom-call | tf_op jit(solution)/shard_map/sum_out/pallas_call | solution.py:48
  (16 shorter events, 0.1 us)
Async XLA Ops:
  1.0 8.8 %collective-permute-start = (bf16[16,3712]{1,0:T(8,128)(2,1)S(1)}, bf16[16,3712]{1,0:T(8,128)(2,1)S(1)}, u32[]{:S(2)}, u32[]{:S(2)}) collective-permute-start(bf16[16,3712]{1,0:T(8,128)(2,1)S(1)} %first_piece.1.refs_0_), channel_id=1, source_target_pairs={{0,8},{2,10},{4,12},{6,14},{8,0},{10,2},{12,4},{14,6},{16,24},{18,... | collective-permute-start | bytes 356360 | tf_op jit(solution)/shard_map/ppermute | solution.py:20
  4.1 7.0 %collective-permute-start.1 = (bf16[16,3712]{1,0:T(8,128)(2,1)S(1)}, bf16[16,3712]{1,0:T(8,128)(2,1)S(1)}, u32[]{:S(2)}, u32[]{:S(2)}) collective-permute-start(bf16[16,3712]{1,0:T(8,128)(2,1)S(1)} %first_piece.1.refs_0_), channel_id=1, source_target_pairs={{0,16},{2,18},{4,20},{6,22},{8,24},{10,26},{12,28},{14,30},{16,0},... | collective-permute-start | bytes 356360 | tf_op jit(solution)/shard_map/ppermute | solution.py:20
  6.6 6.8 %collective-permute-start.2 = (bf16[16,3712]{1,0:T(8,128)(2,1)S(1)}, bf16[16,3712]{1,0:T(8,128)(2,1)S(1)}, u32[]{:S(2)}, u32[]{:S(2)}) collective-permute-start(bf16[16,3712]{1,0:T(8,128)(2,1)S(1)} %first_piece.1.refs_0_), channel_id=1, source_target_pairs={{0,24},{2,26},{4,28},{6,30},{8,16},{10,18},{12,20},{14,22},{16,8},... | collective-permute-start | bytes 356360 | tf_op jit(solution)/shard_map/ppermute | solution.py:20
  13.5 8.7 %collective-permute-start.3 = (bf16[64,3712]{1,0:T(8,128)(2,1)S(1)}, bf16[64,3712]{1,0:T(8,128)(2,1)S(1)}, u32[]{:S(2)}, u32[]{:S(2)}) collective-permute-start(bf16[64,3712]{1,0:T(8,128)(2,1)S(1)} %second.1.refs_0_.refs_10_), channel_id=1, source_target_pairs={{0,2},{2,0},{4,6},{6,4},{8,10},{10,8},{12,14},{14,12},{16,18},{18,... | collective-permute-start | bytes 1425416 | tf_op jit(solution)/shard_map/ppermute | solution.py:20
  15.0 8.7 %collective-permute-start.5 = (bf16[64,3712]{1,0:T(8,128)(2,1)S(1)}, bf16[64,3712]{1,0:T(8,128)(2,1)S(1)}, u32[]{:S(2)}, u32[]{:S(2)}) collective-permute-start(bf16[64,3712]{1,0:T(8,128)(2,1)S(1)} %second.1.refs_0_.refs_10_), channel_id=1, source_target_pairs={{0,4},{2,6},{4,0},{6,2},{8,12},{10,14},{12,8},{14,10},{16,20},{18,... | collective-permute-start | bytes 1425416 | tf_op jit(solution)/shard_map/ppermute | solution.py:20
  22.1 6.1 %collective-permute-start.7 = (bf16[64,3712]{1,0:T(8,128)(2,1)S(1)}, bf16[64,3712]{1,0:T(8,128)(2,1)S(1)}, u32[]{:S(2)}, u32[]{:S(2)}) collective-permute-start(bf16[64,3712]{1,0:T(8,128)(2,1)S(1)} %second.1.refs_0_.refs_10_), channel_id=1, source_target_pairs={{0,1},{1,0},{2,3},{3,2},{4,5},{5,4},{6,7},{7,6},{8,9},{9,8},{10,11... | collective-permute-start | bytes 1425416 | tf_op jit(solution)/shard_map/ppermute | solution.py:32
  23.7 4.5 %collective-permute-start.8 = (bf16[64,3712]{1,0:T(8,128)(2,1)S(1)}, bf16[64,3712]{1,0:T(8,128)(2,1)S(1)}, u32[]{:S(2)}, u32[]{:S(2)}) collective-permute-start(bf16[64,3712]{1,0:T(8,128)(2,1)S(1)} %piece_2.1.refs_1_.refs_12_), channel_id=1, source_target_pairs={{0,1},{1,0},{2,3},{3,2},{4,5},{5,4},{6,7},{7,6},{8,9},{9,8},{10,11... | collective-permute-start | bytes 1425416 | tf_op jit(solution)/shard_map/ppermute | solution.py:32
  24.6 8.7 %collective-permute-start.6 = (bf16[64,3712]{1,0:T(8,128)(2,1)S(1)}, bf16[64,3712]{1,0:T(8,128)(2,1)S(1)}, u32[]{:S(2)}, u32[]{:S(2)}) collective-permute-start(bf16[64,3712]{1,0:T(8,128)(2,1)S(1)} %piece_2.1.refs_1_.refs_12_), channel_id=1, source_target_pairs={{0,2},{2,0},{4,6},{6,4},{8,10},{10,8},{12,14},{14,12},{16,18},{18,... | collective-permute-start | bytes 1425416 | tf_op jit(solution)/shard_map/ppermute | solution.py:20
  25.1 10.5 %collective-permute-start.4 = (bf16[64,3712]{1,0:T(8,128)(2,1)S(1)}, bf16[64,3712]{1,0:T(8,128)(2,1)S(1)}, u32[]{:S(2)}, u32[]{:S(2)}) collective-permute-start(bf16[64,3712]{1,0:T(8,128)(2,1)S(1)} %collective-permute-done.3.refs_1_.refs_0_.refs_11_), channel_id=1, source_target_pairs={{0,1},{1,0},{2,3},{3,2},{4,5},{5,4},{6,7},{7,6},{8,9},{9,8},{10,11... | collective-permute-start | bytes 1425416 | tf_op jit(solution)/shard_map/ppermute | solution.py:32
  33.2 2.3 %collective-permute-start.9 = (bf16[64,3712]{1,0:T(8,128)(2,1)S(1)}, bf16[64,3712]{1,0:T(8,128)(2,1)S(1)}, u32[]{:S(2)}, u32[]{:S(2)}) collective-permute-start(bf16[64,3712]{1,0:T(8,128)(2,1)S(1)} %piece_3.1.refs_1_.refs_13_), channel_id=1, source_target_pairs={{0,1},{1,0},{2,3},{3,2},{4,5},{5,4},{6,7},{7,6},{8,9},{9,8},{10,11... | collective-permute-start | bytes 1425416 | tf_op jit(solution)/shard_map/ppermute | solution.py:32
  39.7 3.5 %collective-permute-start.13 = (bf16[64,3584]{1,0:T(8,128)(2,1)S(1)}, bf16[64,3584]{1,0:T(8,128)(2,1)S(1)}, u32[]{:S(2)}, u32[]{:S(2)}) collective-permute-start(bf16[64,3584]{1,0:T(8,128)(2,1)S(1)} %get-tuple-element.51.rest_0_), channel_id=1, source_target_pairs={{0,1},{1,0},{2,3},{3,2},{4,5},{5,4},{6,7},{7,6},{8,9},{9,8},{10,11... | collective-permute-start | bytes 1376264 | tf_op jit(solution)/shard_map/ppermute | solution.py:32
  40.2 5.1 %collective-permute-start.12 = (bf16[64,3584]{1,0:T(8,128)(2,1)S(1)}, bf16[64,3584]{1,0:T(8,128)(2,1)S(1)}, u32[]{:S(2)}, u32[]{:S(2)}) collective-permute-start(bf16[64,3584]{1,0:T(8,128)(2,1)S(1)} %get-tuple-element.55), channel_id=1, source_target_pairs={{0,1},{1,0},{2,3},{3,2},{4,5},{5,4},{6,7},{7,6},{8,9},{9,8},{10,11... | collective-permute-start | bytes 1376264 | tf_op jit(solution)/shard_map/ppermute | solution.py:32
  41.4 4.6 %collective-permute-start.10 = (bf16[64,3584]{1,0:T(8,128)(2,1)S(1)}, bf16[64,3584]{1,0:T(8,128)(2,1)S(1)}, u32[]{:S(2)}, u32[]{:S(2)}) collective-permute-start(bf16[64,3584]{1,0:T(8,128)(2,1)S(1)} %get-tuple-element.52.refs_3_), channel_id=1, source_target_pairs={{0,1},{1,0},{2,3},{3,2},{4,5},{5,4},{6,7},{7,6},{8,9},{9,8},{10,11... | collective-permute-start | bytes 1376264 | tf_op jit(solution)/shard_map/ppermute | solution.py:32
  41.9 4.1 %collective-permute-start.11 = (bf16[64,3584]{1,0:T(8,128)(2,1)S(1)}, bf16[64,3584]{1,0:T(8,128)(2,1)S(1)}, u32[]{:S(2)}, u32[]{:S(2)}) collective-permute-start(bf16[64,3584]{1,0:T(8,128)(2,1)S(1)} %get-tuple-element.53), channel_id=1, source_target_pairs={{0,1},{1,0},{2,3},{3,2},{4,5},{5,4},{6,7},{7,6},{8,9},{9,8},{10,11... | collective-permute-start | bytes 1376264 | tf_op jit(solution)/shard_map/ppermute | solution.py:32
  43.3 6.1 %collective-permute-start.17 = (bf16[64,1792]{1,0:T(8,128)(2,1)S(1)}, bf16[64,1792]{1,0:T(8,128)(2,1)S(1)}, u32[]{:S(2)}, u32[]{:S(2)}) collective-permute-start(bf16[64,1792]{1,0:T(8,128)(2,1)S(1)} %get-tuple-element.58.refs_3_), channel_id=1, source_target_pairs={{0,2},{2,0},{4,6},{6,4},{8,10},{10,8},{12,14},{14,12},{16,18},{18,... | collective-permute-start | bytes 688136 | tf_op jit(solution)/shard_map/ppermute | solution.py:20
  43.9 8.0 %collective-permute-start.15 = (bf16[64,1792]{1,0:T(8,128)(2,1)S(1)}, bf16[64,1792]{1,0:T(8,128)(2,1)S(1)}, u32[]{:S(2)}, u32[]{:S(2)}) collective-permute-start(bf16[64,1792]{1,0:T(8,128)(2,1)S(1)} %get-tuple-element.57.refs_2_), channel_id=1, source_target_pairs={{0,2},{2,0},{4,6},{6,4},{8,10},{10,8},{12,14},{14,12},{16,18},{18,... | collective-permute-start | bytes 688136 | tf_op jit(solution)/shard_map/ppermute | solution.py:20
  45.4 12.5 %collective-permute-start.14 = (bf16[64,3584]{1,0:T(8,128)(2,1)S(1)}, bf16[64,3584]{1,0:T(8,128)(2,1)S(1)}, u32[]{:S(2)}, u32[]{:S(2)}) collective-permute-start(bf16[64,3584]{1,0:T(8,128)(2,1)S(1)} %sum_1.1.refs_5_), channel_id=1, source_target_pairs={{0,2},{2,0},{4,6},{6,4},{8,10},{10,8},{12,14},{14,12},{16,18},{18,... | collective-permute-start | bytes 1376264 | tf_op jit(solution)/shard_map/ppermute | solution.py:20
  49.4 6.1 %collective-permute-start.18 = (bf16[64,1792]{1,0:T(8,128)(2,1)S(1)}, bf16[64,1792]{1,0:T(8,128)(2,1)S(1)}, u32[]{:S(2)}, u32[]{:S(2)}) collective-permute-start(bf16[64,1792]{1,0:T(8,128)(2,1)S(1)} %sum_2_1.1), channel_id=1, source_target_pairs={{0,4},{2,6},{4,0},{6,2},{8,12},{10,14},{12,8},{14,10},{16,20},{18,... | collective-permute-start | bytes 688136 | tf_op jit(solution)/shard_map/ppermute | solution.py:20
  51.9 6.1 %collective-permute-start.16 = (bf16[64,1792]{1,0:T(8,128)(2,1)S(1)}, bf16[64,1792]{1,0:T(8,128)(2,1)S(1)}, u32[]{:S(2)}, u32[]{:S(2)}) collective-permute-start(bf16[64,1792]{1,0:T(8,128)(2,1)S(1)} %sum_2_0.1), channel_id=1, source_target_pairs={{0,4},{2,6},{4,0},{6,2},{8,12},{10,14},{12,8},{14,10},{16,20},{18,... | collective-permute-start | bytes 688136 | tf_op jit(solution)/shard_map/ppermute | solution.py:20
  58.1 6.8 %collective-permute-start.19 = (bf16[16,3584]{1,0:T(8,128)(2,1)S(1)}, bf16[16,3584]{1,0:T(8,128)(2,1)S(1)}, u32[]{:S(2)}, u32[]{:S(2)}) collective-permute-start(bf16[16,3584]{1,0:T(8,128)(2,1)S(1)} %get-tuple-element.62), channel_id=1, source_target_pairs={{0,24},{2,26},{4,28},{6,30},{8,16},{10,18},{12,20},{14,22},{16,8},... | collective-permute-start | bytes 344072 | tf_op jit(solution)/shard_map/ppermute | solution.py:20
  60.7 6.7 %collective-permute-start.20 = (bf16[16,3584]{1,0:T(8,128)(2,1)S(1)}, bf16[16,3584]{1,0:T(8,128)(2,1)S(1)}, u32[]{:S(2)}, u32[]{:S(2)}) collective-permute-start(bf16[16,3584]{1,0:T(8,128)(2,1)S(1)} %get-tuple-element.63), channel_id=1, source_target_pairs={{0,16},{2,18},{4,20},{6,22},{8,24},{10,26},{12,28},{14,30},{16,0},... | collective-permute-start | bytes 344072 | tf_op jit(solution)/shard_map/ppermute | solution.py:20
  60.7 6.7 %collective-permute-start.21 = (bf16[16,3584]{1,0:T(8,128)(2,1)S(1)}, bf16[16,3584]{1,0:T(8,128)(2,1)S(1)}, u32[]{:S(2)}, u32[]{:S(2)}) collective-permute-start(bf16[16,3584]{1,0:T(8,128)(2,1)S(1)} %get-tuple-element.64), channel_id=1, source_target_pairs={{0,8},{2,10},{4,12},{6,14},{8,0},{10,2},{12,4},{14,6},{16,24},{18,... | collective-permute-start | bytes 344072 | tf_op jit(solution)/shard_map/ppermute | solution.py:20

commit v5 on v4

--- a/solution.py
+++ b/solution.py
@@ -64,19 +64,23 @@
     args = [pltpu.with_memory_space_constraint(w[0], pltpu.HBM) for w in wanted]
     specs = [HBM] * len(wanted)
     outs = []
-    for weight, axis, _, _, span in wanted:
+    for weight, axis, _, _, span, *columns in wanted:
         shape = list(weight.shape)
         shape[axis] = span
+        if columns:
+            shape[1] = columns[1]
         outs.append(kept(*shape))
 
     def copies(in_refs, out_refs, sems):
         found = []
-        for n, (weight, axis, own, start, span) in enumerate(wanted):
+        for n, (weight, axis, own, start, span, *columns) in enumerate(wanted):
             core = lax.axis_index("hsplit")
             core_at = core if own else 1 - core
             at = pl.multiple_of(core_at * (weight.shape[axis] // 2) + start, LANES)
             ref = in_refs[n]
             part = ref.at[:, pl.ds(at, span)] if axis else ref.at[pl.ds(at, span)]
+            if columns:
+                part = part.at[:, pl.ds(*columns)]
             found.append(pltpu.make_async_copy(part, out_refs[n], sems.at[n]))
         return found
 
@@ -169,22 +173,48 @@
     )
 
 
-def joined(parts, done, name):
+def joined(parts, cut, done, name):
     rows, width = parts[0].shape
-
-    def kernel(*refs):
+    total = len(parts) * rows
+
+    def kernel(*refs):
+        whole_ref, left_ref, right_ref = refs[-3:]
         for k in range(len(parts)):
-            refs[-1][k * rows : (k + 1) * rows] = refs[k][...]
-
-    return call(kernel, kept(len(parts) * rows, width), (*parts, done), name)
+            at = slice(k * rows, (k + 1) * rows)
+            whole_ref[at] = refs[k][...]
+            left_ref[at] = refs[k][:, :cut]
+            right_ref[at] = refs[k][:, cut:]
+
+    shapes = [kept(total, width), kept(total, cut), kept(total, width - cut)]
+    return call(kernel, shapes, (*parts, done), name)
+
+
+def flat(pieces):
+    return [part for piece in pieces for part in piece]
+
+
+def stacked(refs, pieces, depth):
+    at, found = 0, []
+    for piece in pieces:
+        left, values = depth, []
+        for part in piece:
+            width = min(left, part.shape[1])
+            values.append(refs[at][:, :width])
+            left -= width
+            at += 1
+        found.append(jnp.concatenate(values, axis=1) if len(values) > 1 else values[0])
+    return jnp.concatenate(found, axis=0)
 
 
 def up_own(pieces, weights, wanted, before, name):
-    units = weights[0].shape[1]
-    depth = weights[0].shape[0]
-    rows = sum(p.shape[0] for p in pieces)
+    units = sum(weight.shape[1] for weight in weights[0])
+    depth = weights[0][0].shape[0]
+    rows = sum(piece[0].shape[0] for piece in pieces)
+    parts = flat(pieces)
+    up_at = len(parts) + len(weights[0])
+    weights_at = (slice(len(parts), up_at), slice(up_at, up_at + len(weights[1])))
     more, more_specs, fetched, scratch, moved, copies = fetches(wanted)
-    fixed = list(pieces) + list(weights) + list(before)
+    fixed = parts + flat(weights) + list(before)
     args = fixed + more
     shapes = [kept(rows, units, jnp.float32) for _ in range(2)]
 
@@ -197,11 +227,9 @@
         def compute():
             for n in range(units // TILE):
                 columns = slice(n * TILE, (n + 1) * TILE)
-                x = jnp.concatenate([refs[p][:, :depth] for p in range(len(pieces))], axis=0)
+                x = stacked(refs, pieces, depth)
                 for which in range(2):
-                    outs[which][:, columns] = jnp.dot(
-                        x, refs[len(pieces) + which][:, columns], preferred_element_type=jnp.float32
-                    )
+                    outs[which][:, columns] = product(x, refs[weights_at[which]], n * TILE)
 
         beside(found, compute)
 
@@ -213,12 +241,15 @@
 
 
 def hidden_call(pieces, last, weights, own_sums, far_sums, extras, wanted):
-    units = weights[0].shape[1]
-    depth = weights[0].shape[0]
-    rows = pieces[0].shape[0]
+    units = sum(weight.shape[1] for weight in weights[0])
+    depth = weights[0][0].shape[0]
+    rows = pieces[0][0].shape[0]
+    parts = flat(pieces)
+    up_at = len(parts) + len(weights[0])
+    weights_at = (slice(len(parts), up_at), slice(up_at, up_at + len(weights[1])))
     block_rows = rows // INNER
     more, more_specs, fetched, scratch, moved, copies = fetches(wanted)
-    fixed = list(pieces) + list(weights)
+    fixed = parts + flat(weights)
     sums_at = len(fixed)
     for _, gate, up in own_sums + far_sums:
         fixed += [gate, up]
@@ -233,7 +264,7 @@
         found = copies(refs[len(fixed) : len(args)], refs[len(args) + 1 : -2], refs[-2])
         def compute():
             extra = jnp.concatenate(
-                [refs[extras_at + k][:, depth:] for k in range(INNER)], axis=0
+                [refs[extras_at + k][:, -LANES:] for k in range(INNER)], axis=0
             ).astype(jnp.float32)
             lane = lax.broadcasted_iota(jnp.int32, extra.shape, 1)
             expert = lax.axis_index("expert")
@@ -243,12 +274,10 @@
 
             for n in range(units // TILE):
                 columns = slice(n * TILE, (n + 1) * TILE)
-                x = jnp.concatenate([refs[p][:, :depth] for p in range(len(pieces))], axis=0)
+                x = stacked(refs, pieces, depth)
                 both = []
                 for which in range(2):
-                    product = jnp.dot(
-                        x, refs[len(pieces) + which][:, columns], preferred_element_type=jnp.float32
-                    )
+                    last_sum = product(x, refs[weights_at[which]], n * TILE)
                     own, far = {}, {}
                     for n_sum, (held, _, _) in enumerate(own_sums):
                         for at, k in enumerate(held):
@@ -256,7 +285,7 @@
                     for n_sum, (held, _, _) in enumerate(far_sums):
                         for at, k in enumerate(held):
                             far[k] = (refs[sums_at + 2 * (len(own_sums) + n_sum) + which], at)
-                    parts = []
+                    blocks = []
                     for jj in range(INNER):
                         for ii in range(INNER):
                             ref, at = own[jj]
@@ -268,9 +297,9 @@
                                 other = ref[at : at + block_rows, columns]
                             else:
                                 at = last.index(ii) * rows + jj * block_rows
-                                other = product[at : at + block_rows]
-                            parts.append(mine_part + other)
-                    both.append(jnp.concatenate(parts, axis=0))
+                                other = last_sum[at : at + block_rows]
+                            blocks.append(mine_part + other)
+                    both.append(jnp.concatenate(blocks, axis=0))
                 gate, up = both
                 scale = jnp.concatenate([scale_ref[...]] * (TILE // LANES), axis=1)
                 hidden = gate / (1.0 + jnp.exp(-gate)) * up * scale
@@ -294,22 +323,23 @@
         at -= weight.shape[1]
 
 
-def down_far(hidden, weight, held, name, before=()):
+def down_far(hidden, weights, held, name, before=()):
     tokens, units = hidden.shape
     rows = tokens // INNER
     block_rows = rows // INNER
-    span = weight.shape[1]
-
-    def kernel(hid_ref, w_ref, *rest):
+    span = sum(weight.shape[1] for weight in weights)
+
+    def kernel(hid_ref, *rest):
+        weight_refs, rest = rest[: len(weights)], rest[len(weights) :]
         at = [jj * rows + k * block_rows for k in held for jj in range(INNER)]
         x = jnp.concatenate([hid_ref[a : a + block_rows] for a in at], axis=0)
         for at in range(0, span, TILE):
-            total = product(x, [w_ref], at).astype(jnp.bfloat16)
+            total = product(x, weight_refs, at).astype(jnp.bfloat16)
             for n in range(len(held)):
                 rest[len(before) + n][:, at : at + TILE] = total[n * rows : (n + 1) * rows]
 
     return call(
-        kernel, [kept(rows, span) for _ in held], (hidden, weight, *before), name,
+        kernel, [kept(rows, span) for _ in held], (hidden, *weights, *before), name,
         flops=2 * len(held) * rows * units * span,
     )
 
@@ -404,39 +434,48 @@
     firsts = {0: first}
     for k in (3, 2, 1):
         firsts[k] = first_hop(first, k)
-    (gate_mine,), done = fetch([(gate_weight, 0, True, 0, half)], "fetch_1")
-    second = joined([firsts[k] for k in range(INNER)], done, "second")
-    pieces = {0: second, 2: second_hop(second, 2), 1: second_hop(second, 1)}
-    (up_mine, gate_other), done = fetch(
-        [(up_weight, 0, True, 0, half), (gate_weight, 0, False, 0, half)], "fetch_2"
-    )
-    pieces[2] = tied(pieces[2], (pieces[1], done), "piece_2")
-    pieces[3] = second_hop(pieces[2], 1)
-    far = {k: other_core(pieces[k]) for k in (0, 2, 1)}
-
+    side = half // 2
+    (gate_mine, down_other_left), done = fetch(
+        [(gate_weight, 0, True, 0, half), (down_weight, 1, False, 0, side)], "fetch_1"
+    )
+    second, left, right = joined([firsts[k] for k in range(INNER)], side, done, "second")
+    pieces = {0: (second,), 2: [second_hop(left, 2), second_hop(right, 2)], 1: (second_hop(second, 1),)}
+    first_units = up_weight.shape[1] // 2
+    (up_mine, gate_other, up_other_left), done = fetch(
+        [
+            (up_weight, 0, True, 0, half),
+            (gate_weight, 0, False, 0, half),
+            (up_weight, 0, False, 0, half, 0, first_units),
+        ],
+        "fetch_2",
+    )
+    pieces[2][0] = tied(pieces[2][0], (*pieces[1], done), "piece_2")
+    relays = [second_hop(part, 1) for part in pieces[2]]
+    far = {k: [other_core(part) for part in pieces[k]] for k in (0, 2, 1)}
     early, late = (0, 2), (1, 3)
-    own_early, (up_other,) = up_own(
-        [pieces[k] for k in early], (gate_mine, up_mine), [(up_weight, 0, False, 0, half)], (),
-        "up_own_early",
-    )
-    far_early, (down_other,) = up_own(
-        [far[k] for k in early], (gate_other, up_other), [(down_weight, 1, False, 0, half)], (),
-        "up_far_early",
-    )
-    pieces[3] = tied(pieces[3], far_early[:1], "piece_3")
-    far[3] = other_core(pieces[3])
-    side = half // 2
+    mine = ((gate_mine,), (up_mine,))
+    own_early, (up_other_right,) = up_own(
+        [pieces[k] for k in early], mine,
+        [(up_weight, 0, False, 0, half, first_units, first_units)], (), "up_own_early",
+    )
+    other = ((gate_other,), (up_other_left, up_other_right))
+    far_early, (down_other_right,) = up_own(
+        [far[k] for k in early], other, [(down_weight, 1, False, side, side)], (), "up_far_early"
+    )
+    down_other = (down_other_left, down_other_right)
+    pieces[3] = [relays[0], tied(relays[1], far_early[:1], "piece_3")]
+    far[3] = [other_core(part) for part in pieces[3]]
     own_late, (down_left,) = up_own(
-        [pieces[k] for k in late], (gate_mine, up_mine), [(down_weight, 1, True, 0, side)],
+        [pieces[k] for k in late], mine, [(down_weight, 1, True, 0, side)],
         (), "up_own_late",
     )
     hidden, (down_right,) = hidden_call(
         [far[k] for k in late],
         late,
-        (gate_other, up_other),
+        other,
         [(early, *own_early), (late, *own_late)],
         [(early, *far_early)],
-        [pieces[k] for k in range(INNER)],
+        [pieces[k][-1] for k in range(INNER)],
         [(down_weight, 1, True, side, side)],
     )
 

time: 69.2 us -> 67.7 us (0.978)
  waiting for transfers between devices: 20.5 us -> 16.3 us
  starting transfers between devices: 20.9 us -> 24.1 us
    ppermute x14 -> x16, waiting for transfers between devices: 20.5 us -> 16.3 us  [exchanged(): return lax.ppermute(array, ('expert', 'hsplit'), route)]
    ppermute x14 -> x16, starting transfers between devices: 18.7 us -> 21.6 us  [exchanged(): return lax.ppermute(array, ('expert', 'hsplit'), route)]
    ppermute x8 -> x10, starting transfers between devices: 2.21 us -> 2.51 us  [other_core(): return lax.ppermute(array, 'hsplit', [(0, 1), (1, 0)])]
  transfers between devices with their start and end apart: 22 -> 26, of which waited for: 11 -> 9; matrix products, arithmetic and copies ran while one was open for 0% -> 0% of each run, Pallas kernels for 30% -> 31%
where the time goes in v5:
time: 67.7 us; the launch traced here: 66.9 us
  Pallas kernels  26.2 us (39%)
  starting transfers between devices  24.1 us (36%)
  waiting for transfers between devices  16.3 us (24%)
    pallas_call x20, Pallas kernels, call(): pl.pallas_call(kernel, out_shape=out_shape, in_specs=specs or [VMEM] * le...  26.2 us
    ppermute x16, starting transfers between devices, exchanged(): return lax.ppermute(array, ('expert', 'hsplit'), route)  21.6 us
    ppermute x16, waiting for transfers between devices, exchanged(): return lax.ppermute(array, ('expert', 'hsplit'), route)  16.3 us
    ppermute x10, starting transfers between devices, other_core(): return lax.ppermute(array, 'hsplit', [(0, 1), (1, 0)])  2.51 us
  transfers between devices with their start and end apart: 26, of which 9 were waited for; matrix products, arithmetic and copies ran while one was open for 0% of the time, Pallas kernels for 31%

profile of v5, /device:TPU:0, one launch (start us, length us, event | category | flops | bytes accessed | tf_op | source)
XLA Modules:
  0.0 66.9 jit_solution(14700326774145439829)
XLA Ops:
  0.0 1.0 %first_piece.1.refs_0_ = bf16[16,3712]{1,0:T(8,128)(2,1)S(1)} custom-call(bf16[16,7168]{1,0:T(8,128)(2,1)} %tok_in.1, s32[8,16]{1,0:T(8,128)} %bitcast.14, f32[8,16]{1,0:T(8,128)} %bitcast.15), custom_call_target="tpu_custom_call" | custom-call | tf_op jit(solution)/shard_map/first_piece/pallas_call | solution.py:48
  1.0 3.1 %collective-permute-start = (bf16[16,3712]{1,0:T(8,128)(2,1)S(1)}, bf16[16,3712]{1,0:T(8,128)(2,1)S(1)}, u32[]{:S(2)}, u32[]{:S(2)}) collective-permute-start(bf16[16,3712]{1,0:T(8,128)(2,1)S(1)} %first_piece.1.refs_0_), channel_id=1, source_target_pairs={{0,8},{2,10},{4,12},{6,14},{8,0},{10,2},{12,4},{14,6},{16,24},{18,... | collective-permute-start | bytes 356360 | tf_op jit(solution)/shard_map/ppermute | solution.py:20
  4.1 2.6 %collective-permute-start.1 = (bf16[16,3712]{1,0:T(8,128)(2,1)S(1)}, bf16[16,3712]{1,0:T(8,128)(2,1)S(1)}, u32[]{:S(2)}, u32[]{:S(2)}) collective-permute-start(bf16[16,3712]{1,0:T(8,128)(2,1)S(1)} %first_piece.1.refs_0_), channel_id=1, source_target_pairs={{0,16},{2,18},{4,20},{6,22},{8,24},{10,26},{12,28},{14,30},{16,0},... | collective-permute-start | bytes 356360 | tf_op jit(solution)/shard_map/ppermute | solution.py:20
  6.6 4.1 %fetch_1.1 = (bf16[3584,1024]{1,0:T(8,128)(2,1)S(1)}, bf16[1024,1792]{1,0:T(8,128)(2,1)S(1)}, f32[8,128]{1,0:T(8,128)S(1)}) custom-call(bf16[7168,1024]{1,0:T(8,128)(2,1)} %bitcast.12, bf16[1024,7168]{1,0:T(8,128)(2,1)} %bitcast.5), custom_call_target="tpu_custom_call" | custom-call | bytes 66060288 | tf_op jit(solution)/shard_map/fetch_1/pallas_call | solution.py:48
  10.8 0.3 collective-permute-done.1.refs_2_
  11.1 2.4 %collective-permute-done.2.refs_3_ = bf16[16,3712]{1,0:T(8,128)(2,1)S(1)} collective-permute-done((bf16[16,3712]{1,0:T(8,128)(2,1)S(1)}, bf16[16,3712]{1,0:T(8,128)(2,1)S(1)}, u32[]{:S(2)}, u32[]{:S(2)}) %collective-permute-start.2) | collective-permute-done | bytes 118816 | tf_op jit(solution)/shard_map/ppermute | solution.py:20
  13.5 1.5 %collective-permute-start.3 = (bf16[64,3712]{1,0:T(8,128)(2,1)S(1)}, bf16[64,3712]{1,0:T(8,128)(2,1)S(1)}, u32[]{:S(2)}, u32[]{:S(2)}) collective-permute-start(bf16[64,3712]{1,0:T(8,128)(2,1)S(1)} %get-tuple-element.41.refs_0_.refs_12_), channel_id=1, source_target_pairs={{0,2},{2,0},{4,6},{6,4},{8,10},{10,8},{12,14},{14,12},{16,18},{18,... | collective-permute-start | bytes 1425416 | tf_op jit(solution)/shard_map/ppermute | solution.py:20
  15.1 1.5 %collective-permute-start.8 = (bf16[64,1920]{1,0:T(8,128)(2,1)S(1)}, bf16[64,1920]{1,0:T(8,128)(2,1)S(1)}, u32[]{:S(2)}, u32[]{:S(2)}) collective-permute-start(bf16[64,1920]{1,0:T(8,128)(2,1)S(1)} %get-tuple-element.44), channel_id=1, source_target_pairs={{0,4},{2,6},{4,0},{6,2},{8,12},{10,14},{12,8},{14,10},{16,20},{18,... | collective-permute-start | bytes 737288 | tf_op jit(solution)/shard_map/ppermute | solution.py:20
  16.6 0.5 collective-permute-start.5
  17.1 6.2 %fetch_2.1 = (bf16[3584,1024]{1,0:T(8,128)(2,1)S(1)}, bf16[3584,1024]{1,0:T(8,128)(2,1)S(1)}, bf16[3584,512]{1,0:T(8,128)(2,1)S(1)}, f32[8,128]{1,0:T(8,128)S(1)}) custom-call(bf16[7168,1024]{1,0:T(8,128)(2,1)} %bitcast.9, bf16[7168,1024]{1,0:T(8,128)(2,1)} %bitcast.13, bf16[7168,1024]{1,0:T(8,128)(2,1)} %bitcast.10), custom_call_target="tpu_custom_call" | custom-call | bytes 110100480 | tf_op jit(solution)/shard_map/fetch_2/pallas_call | solution.py:48
  23.3 0.1 collective-permute-start.10
  23.4 0.5 collective-permute-start.12
  23.9 0.6 collective-permute-start.9
  24.5 0.1 collective-permute-start.11
  24.6 1.4 %collective-permute-start.6 = (bf16[64,1792]{1,0:T(8,128)(2,1)S(1)}, bf16[64,1792]{1,0:T(8,128)(2,1)S(1)}, u32[]{:S(2)}, u32[]{:S(2)}) collective-permute-start(bf16[64,1792]{1,0:T(8,128)(2,1)S(1)} %piece_2.1.refs_1_), channel_id=1, source_target_pairs={{0,2},{2,0},{4,6},{6,4},{8,10},{10,8},{12,14},{14,12},{16,18},{18,... | collective-permute-start | bytes 688136 | tf_op jit(solution)/shard_map/ppermute | solution.py:20
  26.0 2.3 %up_own_early.1 = (f32[128,1024]{1,0:T(8,128)S(1)}, f32[128,1024]{1,0:T(8,128)S(1)}, bf16[3584,512]{1,0:T(8,128)(2,1)S(1)}) custom-call(bf16[64,3712]{1,0:T(8,128)(2,1)S(1)} %get-tuple-element.41.refs_0_.refs_12_, bf16[64,1792]{1,0:T(8,128)(2,1)S(1)} %piece_2.1.refs_1_, bf16[64,1920]{1,0:T(8,128)(2,1)S(1)} %collective-permute-done.8.refs_2_.refs_14_, ...), custom_call_target="tpu_custom_call" | custom-call | flops 5637144576 | bytes 22020096 | tf_op jit(solution)/shard_map/up_own_early/pallas_call | solution.py:48
  28.3 0.1 collective-permute-start.4
  28.4 2.1 %up_far_early.1 = (f32[128,1024]{1,0:T(8,128)S(1)}, f32[128,1024]{1,0:T(8,128)S(1)}, bf16[1024,1792]{1,0:T(8,128)(2,1)S(1)}) custom-call(bf16[64,3712]{1,0:T(8,128)(2,1)S(1)} %collective-permute-done.10.refs_0_, bf16[64,1792]{1,0:T(8,128)(2,1)S(1)} %collective-permute-done.11.refs_1_, bf16[64,1920]{1,0:T(8,128)(2,1)S(1)} %collective-permute-done.12.refs_2_, ...), custom_call_target="tpu_custom_call" | custom-call | flops 5637144576 | bytes 22020096 | tf_op jit(solution)/shard_map/up_far_early/pallas_call | solution.py:48
  30.6 0.5 collective-permute-start.13
  31.1 1.5 %collective-permute-done.6.refs_1_ = bf16[64,1792]{1,0:T(8,128)(2,1)S(1)} collective-permute-done((bf16[64,1792]{1,0:T(8,128)(2,1)S(1)}, bf16[64,1792]{1,0:T(8,128)(2,1)S(1)}, u32[]{:S(2)}, u32[]{:S(2)}) %collective-permute-start.6) | collective-permute-done | bytes 229408 | tf_op jit(solution)/shard_map/ppermute | solution.py:20
  32.6 2.2 %up_own_late.1 = (f32[128,1024]{1,0:T(8,128)S(1)}, f32[128,1024]{1,0:T(8,128)S(1)}, bf16[1024,1792]{1,0:T(8,128)(2,1)S(1)}) custom-call(bf16[64,3712]{1,0:T(8,128)(2,1)S(1)} %collective-permute-done.3.refs_1_.refs_0_.refs_13_, bf16[64,1792]{1,0:T(8,128)(2,1)S(1)} %collective-permute-done.6.refs_1_, bf16[64,1920]{1,0:T(8,128)(2,1)S(1)} %piece_3.1.refs_2_.refs_15_, ...), custom_call_target="tpu_custom_call" | custom-call | flops 5637144576 | bytes 22020096 | tf_op jit(solution)/shard_map/up_own_late/pallas_call | solution.py:48
  34.9 2.5 %hidden.1 = (bf16[256,1024]{1,0:T(8,128)(2,1)S(1)}, bf16[1024,1792]{1,0:T(8,128)(2,1)S(1)}) custom-call(bf16[64,3712]{1,0:T(8,128)(2,1)S(1)} %collective-permute-done.4.refs_0_, bf16[64,1792]{1,0:T(8,128)(2,1)S(1)} %collective-permute-done.7.refs_1_, bf16[64,1920]{1,0:T(8,128)(2,1)S(1)} %collective-permute-done.13.refs_2_, ...), custom_call_target="tpu_custom_call" | custom-call | flops 5637144576 | bytes 22020096 | tf_op jit(solution)/shard_map/hidden/pallas_call | solution.py:48
  37.4 1.1 %down_far_a.1 = (bf16[64,3584]{1,0:T(8,128)(2,1)S(1)}, bf16[64,3584]{1,0:T(8,128)(2,1)S(1)}) custom-call(bf16[256,1024]{1,0:T(8,128)(2,1)S(1)} %get-tuple-element.56.hid_ref.refs_0_, bf16[1024,1792]{1,0:T(8,128)(2,1)S(1)} %get-tuple-element.59.rest_0_, bf16[1024,1792]{1,0:T(8,128)(2,1)S(1)} %get-tuple-element.60.rest_1_), custom_call_target="tpu_custom_call" | custom-call | flops 2818572288 | tf_op jit(solution)/shard_map/down_far_a/pallas_call | solution.py:48
  38.5 0.6 collective-permute-start.17
  39.1 0.1 collective-permute-start.16
  39.2 1.1 %down_far_b.1 = (bf16[64,3584]{1,0:T(8,128)(2,1)S(1)}, bf16[64,3584]{1,0:T(8,128)(2,1)S(1)}) custom-call(bf16[256,1024]{1,0:T(8,128)(2,1)S(1)} %get-tuple-element.56.hid_ref.refs_0_, bf16[1024,1792]{1,0:T(8,128)(2,1)S(1)} %get-tuple-element.59.rest_0_, bf16[1024,1792]{1,0:T(8,128)(2,1)S(1)} %get-tuple-element.60.rest_1_, ...), custom_call_target="tpu_custom_call" | custom-call | flops 2818572288 | tf_op jit(solution)/shard_map/down_far_b/pallas_call | solution.py:48
  40.3 0.5 collective-permute-start.14
  40.8 0.1 collective-permute-start.15
  40.9 1.1 %down_own_a.1 = (f32[64,3584]{1,0:T(8,128)S(1)}, f32[64,3584]{1,0:T(8,128)S(1)}) custom-call(bf16[256,1024]{1,0:T(8,128)(2,1)S(1)} %get-tuple-element.56.hid_ref.refs_0_, bf16[1024,1792]{1,0:T(8,128)(2,1)S(1)} %get-tuple-element.57.refs_1_, bf16[1024,1792]{1,0:T(8,128)(2,1)S(1)} %get-tuple-element.58.refs_2_, bf16[64,3584]{1,0:T(8,128)(2,1)S(1)} %get-tuple-element.62.refs_3_), custom_call_target="tpu_custom_call" | custom-call | flops 2818572288 | tf_op jit(solution)/shard_map/down_own_a/pallas_call | solution.py:48
  42.0 0.1 sum_3.1
  42.1 0.6 collective-permute-start.21
  42.8 1.4 %collective-permute-start.19 = (bf16[64,1792]{1,0:T(8,128)(2,1)S(1)}, bf16[64,1792]{1,0:T(8,128)(2,1)S(1)}, u32[]{:S(2)}, u32[]{:S(2)}) collective-permute-start(bf16[64,1792]{1,0:T(8,128)(2,1)S(1)} %get-tuple-element.67.refs_2_), channel_id=1, source_target_pairs={{0,2},{2,0},{4,6},{6,4},{8,10},{10,8},{12,14},{14,12},{16,18},{18,... | collective-permute-start | bytes 688136 | tf_op jit(solution)/shard_map/ppermute | solution.py:20
  44.2 0.1 sum_1.1.refs_5_
  44.3 0.6 collective-permute-start.18
  44.9 1.1 %down_own_b.1 = (bf16[64,3584]{1,0:T(8,128)(2,1)S(1)}, bf16[64,3584]{1,0:T(8,128)(2,1)S(1)}) custom-call(bf16[256,1024]{1,0:T(8,128)(2,1)S(1)} %get-tuple-element.56.hid_ref.refs_0_, bf16[1024,1792]{1,0:T(8,128)(2,1)S(1)} %get-tuple-element.57.refs_1_, bf16[1024,1792]{1,0:T(8,128)(2,1)S(1)} %get-tuple-element.58.refs_2_, ...), custom_call_target="tpu_custom_call" | custom-call | flops 2818572288 | tf_op jit(solution)/shard_map/down_own_b/pallas_call | solution.py:48
  46.1 2.1 %collective-permute-done.21.part_ref = bf16[64,1792]{1,0:T(8,128)(2,1)S(1)} collective-permute-done((bf16[64,1792]{1,0:T(8,128)(2,1)S(1)}, bf16[64,1792]{1,0:T(8,128)(2,1)S(1)}, u32[]{:S(2)}, u32[]{:S(2)}) %collective-permute-start.21) | collective-permute-done | bytes 229408 | tf_op jit(solution)/shard_map/ppermute | solution.py:20
  48.3 1.6 %collective-permute-start.22 = (bf16[64,1792]{1,0:T(8,128)(2,1)S(1)}, bf16[64,1792]{1,0:T(8,128)(2,1)S(1)}, u32[]{:S(2)}, u32[]{:S(2)}) collective-permute-start(bf16[64,1792]{1,0:T(8,128)(2,1)S(1)} %sum_2_1.1), channel_id=1, source_target_pairs={{0,4},{2,6},{4,0},{6,2},{8,12},{10,14},{12,8},{14,10},{16,20},{18,... | collective-permute-start | bytes 688136 | tf_op jit(solution)/shard_map/ppermute | solution.py:20
  49.9 0.8 %collective-permute-done.19.part_ref = bf16[64,1792]{1,0:T(8,128)(2,1)S(1)} collective-permute-done((bf16[64,1792]{1,0:T(8,128)(2,1)S(1)}, bf16[64,1792]{1,0:T(8,128)(2,1)S(1)}, u32[]{:S(2)}, u32[]{:S(2)}) %collective-permute-start.19) | collective-permute-done | bytes 229408 | tf_op jit(solution)/shard_map/ppermute | solution.py:20
  50.7 1.6 %collective-permute-start.20 = (bf16[64,1792]{1,0:T(8,128)(2,1)S(1)}, bf16[64,1792]{1,0:T(8,128)(2,1)S(1)}, u32[]{:S(2)}, u32[]{:S(2)}) collective-permute-start(bf16[64,1792]{1,0:T(8,128)(2,1)S(1)} %sum_2_0.1), channel_id=1, source_target_pairs={{0,4},{2,6},{4,0},{6,2},{8,12},{10,14},{12,8},{14,10},{16,20},{18,... | collective-permute-start | bytes 688136 | tf_op jit(solution)/shard_map/ppermute | solution.py:20
  52.3 2.0 %collective-permute-done.22.refs_3_ = bf16[64,1792]{1,0:T(8,128)(2,1)S(1)} collective-permute-done((bf16[64,1792]{1,0:T(8,128)(2,1)S(1)}, bf16[64,1792]{1,0:T(8,128)(2,1)S(1)}, u32[]{:S(2)}, u32[]{:S(2)}) %collective-permute-start.22) | collective-permute-done | bytes 229408 | tf_op jit(solution)/shard_map/ppermute | solution.py:20
  54.3 2.5 %collective-permute-done.20.refs_2_ = bf16[64,1792]{1,0:T(8,128)(2,1)S(1)} collective-permute-done((bf16[64,1792]{1,0:T(8,128)(2,1)S(1)}, bf16[64,1792]{1,0:T(8,128)(2,1)S(1)}, u32[]{:S(2)}, u32[]{:S(2)}) %collective-permute-start.20) | collective-permute-done | bytes 229408 | tf_op jit(solution)/shard_map/ppermute | solution.py:20
  56.8 0.2 sum_split.1
  57.0 1.5 %collective-permute-start.23 = (bf16[16,3584]{1,0:T(8,128)(2,1)S(1)}, bf16[16,3584]{1,0:T(8,128)(2,1)S(1)}, u32[]{:S(2)}, u32[]{:S(2)}) collective-permute-start(bf16[16,3584]{1,0:T(8,128)(2,1)S(1)} %get-tuple-element.72), channel_id=1, source_target_pairs={{0,24},{2,26},{4,28},{6,30},{8,16},{10,18},{12,20},{14,22},{16,8},... | collective-permute-start | bytes 344072 | tf_op jit(solution)/shard_map/ppermute | solution.py:20
  58.4 0.8 %collective-permute-start.24 = (bf16[16,3584]{1,0:T(8,128)(2,1)S(1)}, bf16[16,3584]{1,0:T(8,128)(2,1)S(1)}, u32[]{:S(2)}, u32[]{:S(2)}) collective-permute-start(bf16[16,3584]{1,0:T(8,128)(2,1)S(1)} %get-tuple-element.73), channel_id=1, source_target_pairs={{0,16},{2,18},{4,20},{6,22},{8,24},{10,26},{12,28},{14,30},{16,0},... | collective-permute-start | bytes 344072 | tf_op jit(solution)/shard_map/ppermute | solution.py:20
  59.2 2.2 %collective-permute-start.25 = (bf16[16,3584]{1,0:T(8,128)(2,1)S(1)}, bf16[16,3584]{1,0:T(8,128)(2,1)S(1)}, u32[]{:S(2)}, u32[]{:S(2)}) collective-permute-start(bf16[16,3584]{1,0:T(8,128)(2,1)S(1)} %get-tuple-element.74), channel_id=1, source_target_pairs={{0,8},{2,10},{4,12},{6,14},{8,0},{10,2},{12,4},{14,6},{16,24},{18,... | collective-permute-start | bytes 344072 | tf_op jit(solution)/shard_map/ppermute | solution.py:20
  61.4 2.4 %collective-permute-done.23.refs_1_ = bf16[16,3584]{1,0:T(8,128)(2,1)S(1)} collective-permute-done((bf16[16,3584]{1,0:T(8,128)(2,1)S(1)}, bf16[16,3584]{1,0:T(8,128)(2,1)S(1)}, u32[]{:S(2)}, u32[]{:S(2)}) %collective-permute-start.23) | collective-permute-done | bytes 114720 | tf_op jit(solution)/shard_map/ppermute | solution.py:20
  63.8 2.4 %collective-permute-done.24.refs_2_ = bf16[16,3584]{1,0:T(8,128)(2,1)S(1)} collective-permute-done((bf16[16,3584]{1,0:T(8,128)(2,1)S(1)}, bf16[16,3584]{1,0:T(8,128)(2,1)S(1)}, u32[]{:S(2)}, u32[]{:S(2)}) %collective-permute-start.24) | collective-permute-done | bytes 114720 | tf_op jit(solution)/shard_map/ppermute | solution.py:20
  66.2 0.7 %sum_out.1 = bf16[16,3584]{1,0:T(8,128)(2,1)} custom-call(bf16[16,3584]{1,0:T(8,128)(2,1)S(1)} %get-tuple-element.71.refs_0_, bf16[16,3584]{1,0:T(8,128)(2,1)S(1)} %collective-permute-done.23.refs_1_, bf16[16,3584]{1,0:T(8,128)(2,1)S(1)} %collective-permute-done.24.refs_2_, bf16[16,3584]{1,0:T(8,128)(2,1)S(1)} %collective-permute-done.25.refs_3_), custom_call_target="tpu_custom_call" | custom-call | tf_op jit(solution)/shard_map/sum_out/pallas_call | solution.py:48
  (24 shorter events, 0.2 us)
Async XLA Ops:
  1.0 9.8 %collective-permute-start = (bf16[16,3712]{1,0:T(8,128)(2,1)S(1)}, bf16[16,3712]{1,0:T(8,128)(2,1)S(1)}, u32[]{:S(2)}, u32[]{:S(2)}) collective-permute-start(bf16[16,3712]{1,0:T(8,128)(2,1)S(1)} %first_piece.1.refs_0_), channel_id=1, source_target_pairs={{0,8},{2,10},{4,12},{6,14},{8,0},{10,2},{12,4},{14,6},{16,24},{18,... | collective-permute-start | bytes 356360 | tf_op jit(solution)/shard_map/ppermute | solution.py:20
  4.1 7.0 %collective-permute-start.1 = (bf16[16,3712]{1,0:T(8,128)(2,1)S(1)}, bf16[16,3712]{1,0:T(8,128)(2,1)S(1)}, u32[]{:S(2)}, u32[]{:S(2)}) collective-permute-start(bf16[16,3712]{1,0:T(8,128)(2,1)S(1)} %first_piece.1.refs_0_), channel_id=1, source_target_pairs={{0,16},{2,18},{4,20},{6,22},{8,24},{10,26},{12,28},{14,30},{16,0},... | collective-permute-start | bytes 356360 | tf_op jit(solution)/shard_map/ppermute | solution.py:20
  6.6 6.8 %collective-permute-start.2 = (bf16[16,3712]{1,0:T(8,128)(2,1)S(1)}, bf16[16,3712]{1,0:T(8,128)(2,1)S(1)}, u32[]{:S(2)}, u32[]{:S(2)}) collective-permute-start(bf16[16,3712]{1,0:T(8,128)(2,1)S(1)} %first_piece.1.refs_0_), channel_id=1, source_target_pairs={{0,24},{2,26},{4,28},{6,30},{8,16},{10,18},{12,20},{14,22},{16,8},... | collective-permute-start | bytes 356360 | tf_op jit(solution)/shard_map/ppermute | solution.py:20
  13.5 11.0 %collective-permute-start.3 = (bf16[64,3712]{1,0:T(8,128)(2,1)S(1)}, bf16[64,3712]{1,0:T(8,128)(2,1)S(1)}, u32[]{:S(2)}, u32[]{:S(2)}) collective-permute-start(bf16[64,3712]{1,0:T(8,128)(2,1)S(1)} %get-tuple-element.41.refs_0_.refs_12_), channel_id=1, source_target_pairs={{0,2},{2,0},{4,6},{6,4},{8,10},{10,8},{12,14},{14,12},{16,18},{18,... | collective-permute-start | bytes 1425416 | tf_op jit(solution)/shard_map/ppermute | solution.py:20
  15.1 8.4 %collective-permute-start.8 = (bf16[64,1920]{1,0:T(8,128)(2,1)S(1)}, bf16[64,1920]{1,0:T(8,128)(2,1)S(1)}, u32[]{:S(2)}, u32[]{:S(2)}) collective-permute-start(bf16[64,1920]{1,0:T(8,128)(2,1)S(1)} %get-tuple-element.44), channel_id=1, source_target_pairs={{0,4},{2,6},{4,0},{6,2},{8,12},{10,14},{12,8},{14,10},{16,20},{18,... | collective-permute-start | bytes 737288 | tf_op jit(solution)/shard_map/ppermute | solution.py:20
  16.6 7.9 %collective-permute-start.5 = (bf16[64,1792]{1,0:T(8,128)(2,1)S(1)}, bf16[64,1792]{1,0:T(8,128)(2,1)S(1)}, u32[]{:S(2)}, u32[]{:S(2)}) collective-permute-start(bf16[64,1792]{1,0:T(8,128)(2,1)S(1)} %get-tuple-element.42), channel_id=1, source_target_pairs={{0,4},{2,6},{4,0},{6,2},{8,12},{10,14},{12,8},{14,10},{16,20},{18,... | collective-permute-start | bytes 688136 | tf_op jit(solution)/shard_map/ppermute | solution.py:20
  23.3 5.0 %collective-permute-start.10 = (bf16[64,3712]{1,0:T(8,128)(2,1)S(1)}, bf16[64,3712]{1,0:T(8,128)(2,1)S(1)}, u32[]{:S(2)}, u32[]{:S(2)}) collective-permute-start(bf16[64,3712]{1,0:T(8,128)(2,1)S(1)} %get-tuple-element.41.refs_0_.refs_12_), channel_id=1, source_target_pairs={{0,1},{1,0},{2,3},{3,2},{4,5},{5,4},{6,7},{7,6},{8,9},{9,8},{10,11... | collective-permute-start | bytes 1425416 | tf_op jit(solution)/shard_map/ppermute | solution.py:32
  23.4 5.0 %collective-permute-start.12 = (bf16[64,1920]{1,0:T(8,128)(2,1)S(1)}, bf16[64,1920]{1,0:T(8,128)(2,1)S(1)}, u32[]{:S(2)}, u32[]{:S(2)}) collective-permute-start(bf16[64,1920]{1,0:T(8,128)(2,1)S(1)} %collective-permute-done.8.refs_2_.refs_14_), channel_id=1, source_target_pairs={{0,1},{1,0},{2,3},{3,2},{4,5},{5,4},{6,7},{7,6},{8,9},{9,8},{10,11... | collective-permute-start | bytes 737288 | tf_op jit(solution)/shard_map/ppermute | solution.py:32
  23.9 6.6 %collective-permute-start.9 = (bf16[64,1920]{1,0:T(8,128)(2,1)S(1)}, bf16[64,1920]{1,0:T(8,128)(2,1)S(1)}, u32[]{:S(2)}, u32[]{:S(2)}) collective-permute-start(bf16[64,1920]{1,0:T(8,128)(2,1)S(1)} %collective-permute-done.8.refs_2_.refs_14_), channel_id=1, source_target_pairs={{0,2},{2,0},{4,6},{6,4},{8,10},{10,8},{12,14},{14,12},{16,18},{18,... | collective-permute-start | bytes 737288 | tf_op jit(solution)/shard_map/ppermute | solution.py:20
  24.5 3.9 %collective-permute-start.11 = (bf16[64,1792]{1,0:T(8,128)(2,1)S(1)}, bf16[64,1792]{1,0:T(8,128)(2,1)S(1)}, u32[]{:S(2)}, u32[]{:S(2)}) collective-permute-start(bf16[64,1792]{1,0:T(8,128)(2,1)S(1)} %piece_2.1.refs_1_), channel_id=1, source_target_pairs={{0,1},{1,0},{2,3},{3,2},{4,5},{5,4},{6,7},{7,6},{8,9},{9,8},{10,11... | collective-permute-start | bytes 688136 | tf_op jit(solution)/shard_map/ppermute | solution.py:32
  24.6 8.0 %collective-permute-start.6 = (bf16[64,1792]{1,0:T(8,128)(2,1)S(1)}, bf16[64,1792]{1,0:T(8,128)(2,1)S(1)}, u32[]{:S(2)}, u32[]{:S(2)}) collective-permute-start(bf16[64,1792]{1,0:T(8,128)(2,1)S(1)} %piece_2.1.refs_1_), channel_id=1, source_target_pairs={{0,2},{2,0},{4,6},{6,4},{8,10},{10,8},{12,14},{14,12},{16,18},{18,... | collective-permute-start | bytes 688136 | tf_op jit(solution)/shard_map/ppermute | solution.py:20
  28.3 6.6 %collective-permute-start.4 = (bf16[64,3712]{1,0:T(8,128)(2,1)S(1)}, bf16[64,3712]{1,0:T(8,128)(2,1)S(1)}, u32[]{:S(2)}, u32[]{:S(2)}) collective-permute-start(bf16[64,3712]{1,0:T(8,128)(2,1)S(1)} %collective-permute-done.3.refs_1_.refs_0_.refs_13_), channel_id=1, source_target_pairs={{0,1},{1,0},{2,3},{3,2},{4,5},{5,4},{6,7},{7,6},{8,9},{9,8},{10,11... | collective-permute-start | bytes 1425416 | tf_op jit(solution)/shard_map/ppermute | solution.py:32
  30.6 4.3 %collective-permute-start.13 = (bf16[64,1920]{1,0:T(8,128)(2,1)S(1)}, bf16[64,1920]{1,0:T(8,128)(2,1)S(1)}, u32[]{:S(2)}, u32[]{:S(2)}) collective-permute-start(bf16[64,1920]{1,0:T(8,128)(2,1)S(1)} %piece_3.1.refs_2_.refs_15_), channel_id=1, source_target_pairs={{0,1},{1,0},{2,3},{3,2},{4,5},{5,4},{6,7},{7,6},{8,9},{9,8},{10,11... | collective-permute-start | bytes 737288 | tf_op jit(solution)/shard_map/ppermute | solution.py:32
  32.6 2.3 %collective-permute-start.7 = (bf16[64,1792]{1,0:T(8,128)(2,1)S(1)}, bf16[64,1792]{1,0:T(8,128)(2,1)S(1)}, u32[]{:S(2)}, u32[]{:S(2)}) collective-permute-start(bf16[64,1792]{1,0:T(8,128)(2,1)S(1)} %collective-permute-done.6.refs_1_), channel_id=1, source_target_pairs={{0,1},{1,0},{2,3},{3,2},{4,5},{5,4},{6,7},{7,6},{8,9},{9,8},{10,11... | collective-permute-start | bytes 688136 | tf_op jit(solution)/shard_map/ppermute | solution.py:32
  38.5 3.5 %collective-permute-start.17 = (bf16[64,3584]{1,0:T(8,128)(2,1)S(1)}, bf16[64,3584]{1,0:T(8,128)(2,1)S(1)}, u32[]{:S(2)}, u32[]{:S(2)}) collective-permute-start(bf16[64,3584]{1,0:T(8,128)(2,1)S(1)} %get-tuple-element.61.rest_2_), channel_id=1, source_target_pairs={{0,1},{1,0},{2,3},{3,2},{4,5},{5,4},{6,7},{7,6},{8,9},{9,8},{10,11... | collective-permute-start | bytes 1376264 | tf_op jit(solution)/shard_map/ppermute | solution.py:32
  39.1 5.1 %collective-permute-start.16 = (bf16[64,3584]{1,0:T(8,128)(2,1)S(1)}, bf16[64,3584]{1,0:T(8,128)(2,1)S(1)}, u32[]{:S(2)}, u32[]{:S(2)}) collective-permute-start(bf16[64,3584]{1,0:T(8,128)(2,1)S(1)} %get-tuple-element.65), channel_id=1, source_target_pairs={{0,1},{1,0},{2,3},{3,2},{4,5},{5,4},{6,7},{7,6},{8,9},{9,8},{10,11... | collective-permute-start | bytes 1376264 | tf_op jit(solution)/shard_map/ppermute | solution.py:32
  40.3 4.6 %collective-permute-start.14 = (bf16[64,3584]{1,0:T(8,128)(2,1)S(1)}, bf16[64,3584]{1,0:T(8,128)(2,1)S(1)}, u32[]{:S(2)}, u32[]{:S(2)}) collective-permute-start(bf16[64,3584]{1,0:T(8,128)(2,1)S(1)} %get-tuple-element.62.refs_3_), channel_id=1, source_target_pairs={{0,1},{1,0},{2,3},{3,2},{4,5},{5,4},{6,7},{7,6},{8,9},{9,8},{10,11... | collective-permute-start | bytes 1376264 | tf_op jit(solution)/shard_map/ppermute | solution.py:32
  40.8 4.1 %collective-permute-start.15 = (bf16[64,3584]{1,0:T(8,128)(2,1)S(1)}, bf16[64,3584]{1,0:T(8,128)(2,1)S(1)}, u32[]{:S(2)}, u32[]{:S(2)}) collective-permute-start(bf16[64,3584]{1,0:T(8,128)(2,1)S(1)} %get-tuple-element.63), channel_id=1, source_target_pairs={{0,1},{1,0},{2,3},{3,2},{4,5},{5,4},{6,7},{7,6},{8,9},{9,8},{10,11... | collective-permute-start | bytes 1376264 | tf_op jit(solution)/shard_map/ppermute | solution.py:32
  42.1 6.1 %collective-permute-start.21 = (bf16[64,1792]{1,0:T(8,128)(2,1)S(1)}, bf16[64,1792]{1,0:T(8,128)(2,1)S(1)}, u32[]{:S(2)}, u32[]{:S(2)}) collective-permute-start(bf16[64,1792]{1,0:T(8,128)(2,1)S(1)} %get-tuple-element.68.refs_3_), channel_id=1, source_target_pairs={{0,2},{2,0},{4,6},{6,4},{8,10},{10,8},{12,14},{14,12},{16,18},{18,... | collective-permute-start | bytes 688136 | tf_op jit(solution)/shard_map/ppermute | solution.py:20
  42.8 7.9 %collective-permute-start.19 = (bf16[64,1792]{1,0:T(8,128)(2,1)S(1)}, bf16[64,1792]{1,0:T(8,128)(2,1)S(1)}, u32[]{:S(2)}, u32[]{:S(2)}) collective-permute-start(bf16[64,1792]{1,0:T(8,128)(2,1)S(1)} %get-tuple-element.67.refs_2_), channel_id=1, source_target_pairs={{0,2},{2,0},{4,6},{6,4},{8,10},{10,8},{12,14},{14,12},{16,18},{18,... | collective-permute-start | bytes 688136 | tf_op jit(solution)/shard_map/ppermute | solution.py:20
  44.3 12.5 %collective-permute-start.18 = (bf16[64,3584]{1,0:T(8,128)(2,1)S(1)}, bf16[64,3584]{1,0:T(8,128)(2,1)S(1)}, u32[]{:S(2)}, u32[]{:S(2)}) collective-permute-start(bf16[64,3584]{1,0:T(8,128)(2,1)S(1)} %sum_1.1.refs_5_), channel_id=1, source_target_pairs={{0,2},{2,0},{4,6},{6,4},{8,10},{10,8},{12,14},{14,12},{16,18},{18,... | collective-permute-start | bytes 1376264 | tf_op jit(solution)/shard_map/ppermute | solution.py:20
  48.3 6.1 %collective-permute-start.22 = (bf16[64,1792]{1,0:T(8,128)(2,1)S(1)}, bf16[64,1792]{1,0:T(8,128)(2,1)S(1)}, u32[]{:S(2)}, u32[]{:S(2)}) collective-permute-start(bf16[64,1792]{1,0:T(8,128)(2,1)S(1)} %sum_2_1.1), channel_id=1, source_target_pairs={{0,4},{2,6},{4,0},{6,2},{8,12},{10,14},{12,8},{14,10},{16,20},{18,... | collective-permute-start | bytes 688136 | tf_op jit(solution)/shard_map/ppermute | solution.py:20
  50.7 6.1 %collective-permute-start.20 = (bf16[64,1792]{1,0:T(8,128)(2,1)S(1)}, bf16[64,1792]{1,0:T(8,128)(2,1)S(1)}, u32[]{:S(2)}, u32[]{:S(2)}) collective-permute-start(bf16[64,1792]{1,0:T(8,128)(2,1)S(1)} %sum_2_0.1), channel_id=1, source_target_pairs={{0,4},{2,6},{4,0},{6,2},{8,12},{10,14},{12,8},{14,10},{16,20},{18,... | collective-permute-start | bytes 688136 | tf_op jit(solution)/shard_map/ppermute | solution.py:20
  57.0 6.8 %collective-permute-start.23 = (bf16[16,3584]{1,0:T(8,128)(2,1)S(1)}, bf16[16,3584]{1,0:T(8,128)(2,1)S(1)}, u32[]{:S(2)}, u32[]{:S(2)}) collective-permute-start(bf16[16,3584]{1,0:T(8,128)(2,1)S(1)} %get-tuple-element.72), channel_id=1, source_target_pairs={{0,24},{2,26},{4,28},{6,30},{8,16},{10,18},{12,20},{14,22},{16,8},... | collective-permute-start | bytes 344072 | tf_op jit(solution)/shard_map/ppermute | solution.py:20
  58.4 7.8 %collective-permute-start.24 = (bf16[16,3584]{1,0:T(8,128)(2,1)S(1)}, bf16[16,3584]{1,0:T(8,128)(2,1)S(1)}, u32[]{:S(2)}, u32[]{:S(2)}) collective-permute-start(bf16[16,3584]{1,0:T(8,128)(2,1)S(1)} %get-tuple-element.73), channel_id=1, source_target_pairs={{0,16},{2,18},{4,20},{6,22},{8,24},{10,26},{12,28},{14,30},{16,0},... | collective-permute-start | bytes 344072 | tf_op jit(solution)/shard_map/ppermute | solution.py:20
  59.2 7.0 %collective-permute-start.25 = (bf16[16,3584]{1,0:T(8,128)(2,1)S(1)}, bf16[16,3584]{1,0:T(8,128)(2,1)S(1)}, u32[]{:S(2)}, u32[]{:S(2)}) collective-permute-start(bf16[16,3584]{1,0:T(8,128)(2,1)S(1)} %get-tuple-element.74), channel_id=1, source_target_pairs={{0,8},{2,10},{4,12},{6,14},{8,0},{10,2},{12,4},{14,6},{16,24},{18,... | collective-permute-start | bytes 344072 | tf_op jit(solution)/shard_map/ppermute | solution.py:20

commit v6 on v5

--- a/solution.py
+++ b/solution.py
@@ -35,7 +35,7 @@
 VMEM = pl.BlockSpec(memory_space=pltpu.VMEM)
 HBM = pl.BlockSpec(memory_space=pltpu.HBM)
 TILE = 256
-WEIGHT = 3
+WEIGHT = 6
 
 
 def kept(rows, columns, dtype=jnp.bfloat16):
@@ -435,19 +435,19 @@
     for k in (3, 2, 1):
         firsts[k] = first_hop(first, k)
     side = half // 2
-    (gate_mine, down_other_left), done = fetch(
-        [(gate_weight, 0, True, 0, half), (down_weight, 1, False, 0, side)], "fetch_1"
+    first_units = up_weight.shape[1] // 2
+    (gate_mine, down_other_left, up_other_left), done = fetch(
+        [
+            (gate_weight, 0, True, 0, half),
+            (down_weight, 1, False, 0, side),
+            (up_weight, 0, False, 0, half, 0, first_units),
+        ],
+        "fetch_1",
     )
     second, left, right = joined([firsts[k] for k in range(INNER)], side, done, "second")
     pieces = {0: (second,), 2: [second_hop(left, 2), second_hop(right, 2)], 1: (second_hop(second, 1),)}
-    first_units = up_weight.shape[1] // 2
-    (up_mine, gate_other, up_other_left), done = fetch(
-        [
-            (up_weight, 0, True, 0, half),
-            (gate_weight, 0, False, 0, half),
-            (up_weight, 0, False, 0, half, 0, first_units),
-        ],
-        "fetch_2",
+    (up_mine, gate_other), done = fetch(
+        [(up_weight, 0, True, 0, half), (gate_weight, 0, False, 0, half)], "fetch_2"
     )
     pieces[2][0] = tied(pieces[2][0], (*pieces[1], done), "piece_2")
     relays = [second_hop(part, 1) for part in pieces[2]]

time: 67.7 us -> 67.4 us (level)
  waiting for transfers between devices: 16.3 us -> 13.8 us
  starting transfers between devices: 24.1 us -> 25.9 us
    ppermute x16, waiting for transfers between devices: 16.3 us -> 13.7 us  [exchanged(): return lax.ppermute(array, ('expert', 'hsplit'), route)]
    ppermute x10, starting transfers between devices: 2.51 us -> 3.85 us  [other_core(): return lax.ppermute(array, 'hsplit', [(0, 1), (1, 0)])]
  transfers between devices with their start and end apart: 26 -> 26, of which waited for: 9 -> 8; matrix products, arithmetic and copies ran while one was open for 0% -> 0% of each run, Pallas kernels for 31% -> 30%
where the time goes in v6:
time: 67.4 us; the launch traced here: 66.2 us
  Pallas kernels  26.3 us (39%)
  starting transfers between devices  25.9 us (38%)
  waiting for transfers between devices  13.8 us (20%)
    pallas_call x20, Pallas kernels, call(): pl.pallas_call(kernel, out_shape=out_shape, in_specs=specs or [VMEM] * le...  26.3 us
    ppermute x16, starting transfers between devices, exchanged(): return lax.ppermute(array, ('expert', 'hsplit'), route)  22 us
    ppermute x16, waiting for transfers between devices, exchanged(): return lax.ppermute(array, ('expert', 'hsplit'), route)  13.7 us
    ppermute x10, starting transfers between devices, other_core(): return lax.ppermute(array, 'hsplit', [(0, 1), (1, 0)])  3.85 us
  transfers between devices with their start and end apart: 26, of which 8 were waited for; matrix products, arithmetic and copies ran while one was open for 0% of the time, Pallas kernels for 30%

profile of v6, /device:TPU:0, one launch (start us, length us, event | category | flops | bytes accessed | tf_op | source)
XLA Modules:
  0.0 66.2 jit_solution(6555914007179440386)
XLA Ops:
  0.0 1.0 %first_piece.1.refs_0_ = bf16[16,3712]{1,0:T(8,128)(2,1)S(1)} custom-call(bf16[16,7168]{1,0:T(8,128)(2,1)} %tok_in.1, s32[8,16]{1,0:T(8,128)} %bitcast.14, f32[8,16]{1,0:T(8,128)} %bitcast.15), custom_call_target="tpu_custom_call" | custom-call | tf_op jit(solution)/shard_map/first_piece/pallas_call | solution.py:48
  1.0 3.1 %collective-permute-start = (bf16[16,3712]{1,0:T(8,128)(2,1)S(1)}, bf16[16,3712]{1,0:T(8,128)(2,1)S(1)}, u32[]{:S(2)}, u32[]{:S(2)}) collective-permute-start(bf16[16,3712]{1,0:T(8,128)(2,1)S(1)} %first_piece.1.refs_0_), channel_id=1, source_target_pairs={{0,8},{2,10},{4,12},{6,14},{8,0},{10,2},{12,4},{14,6},{16,24},{18,... | collective-permute-start | bytes 356360 | tf_op jit(solution)/shard_map/ppermute | solution.py:20
  4.1 2.6 %collective-permute-start.1 = (bf16[16,3712]{1,0:T(8,128)(2,1)S(1)}, bf16[16,3712]{1,0:T(8,128)(2,1)S(1)}, u32[]{:S(2)}, u32[]{:S(2)}) collective-permute-start(bf16[16,3712]{1,0:T(8,128)(2,1)S(1)} %first_piece.1.refs_0_), channel_id=1, source_target_pairs={{0,16},{2,18},{4,20},{6,22},{8,24},{10,26},{12,28},{14,30},{16,0},... | collective-permute-start | bytes 356360 | tf_op jit(solution)/shard_map/ppermute | solution.py:20
  6.6 5.2 %fetch_1.1 = (bf16[3584,1024]{1,0:T(8,128)(2,1)S(1)}, bf16[1024,1792]{1,0:T(8,128)(2,1)S(1)}, bf16[3584,512]{1,0:T(8,128)(2,1)S(1)}, f32[8,128]{1,0:T(8,128)S(1)}) custom-call(bf16[7168,1024]{1,0:T(8,128)(2,1)} %bitcast.5, bf16[1024,7168]{1,0:T(8,128)(2,1)} %bitcast.10, bf16[7168,1024]{1,0:T(8,128)(2,1)} %bitcast.7), custom_call_target="tpu_custom_call" | custom-call | bytes 176160768 | tf_op jit(solution)/shard_map/fetch_1/pallas_call | solution.py:48
  11.9 1.5 %collective-permute-done.2.refs_3_ = bf16[16,3712]{1,0:T(8,128)(2,1)S(1)} collective-permute-done((bf16[16,3712]{1,0:T(8,128)(2,1)S(1)}, bf16[16,3712]{1,0:T(8,128)(2,1)S(1)}, u32[]{:S(2)}, u32[]{:S(2)}) %collective-permute-start.2) | collective-permute-done | bytes 118816 | tf_op jit(solution)/shard_map/ppermute | solution.py:20
  13.4 0.1 second.1
  13.5 1.5 %collective-permute-start.3 = (bf16[64,3712]{1,0:T(8,128)(2,1)S(1)}, bf16[64,3712]{1,0:T(8,128)(2,1)S(1)}, u32[]{:S(2)}, u32[]{:S(2)}) collective-permute-start(bf16[64,3712]{1,0:T(8,128)(2,1)S(1)} %get-tuple-element.41.refs_0_.refs_12_), channel_id=1, source_target_pairs={{0,2},{2,0},{4,6},{6,4},{8,10},{10,8},{12,14},{14,12},{16,18},{18,... | collective-permute-start | bytes 1425416 | tf_op jit(solution)/shard_map/ppermute | solution.py:20
  15.0 1.5 %collective-permute-start.8 = (bf16[64,1920]{1,0:T(8,128)(2,1)S(1)}, bf16[64,1920]{1,0:T(8,128)(2,1)S(1)}, u32[]{:S(2)}, u32[]{:S(2)}) collective-permute-start(bf16[64,1920]{1,0:T(8,128)(2,1)S(1)} %get-tuple-element.44), channel_id=1, source_target_pairs={{0,4},{2,6},{4,0},{6,2},{8,12},{10,14},{12,8},{14,10},{16,20},{18,... | collective-permute-start | bytes 737288 | tf_op jit(solution)/shard_map/ppermute | solution.py:20
  16.6 0.5 collective-permute-start.5
  17.1 5.2 %fetch_2.1 = (bf16[3584,1024]{1,0:T(8,128)(2,1)S(1)}, bf16[3584,1024]{1,0:T(8,128)(2,1)S(1)}, f32[8,128]{1,0:T(8,128)S(1)}) custom-call(bf16[7168,1024]{1,0:T(8,128)(2,1)} %bitcast.8, bf16[7168,1024]{1,0:T(8,128)(2,1)} %bitcast.6), custom_call_target="tpu_custom_call" | custom-call | bytes 176160768 | tf_op jit(solution)/shard_map/fetch_2/pallas_call | solution.py:48
  22.3 0.1 collective-permute-start.10
  22.4 0.5 collective-permute-start.12
  22.8 0.6 collective-permute-start.9
  23.4 0.3 collective-permute-done.5.refs_0_
  23.7 1.5 %collective-permute-start.11 = (bf16[64,1792]{1,0:T(8,128)(2,1)S(1)}, bf16[64,1792]{1,0:T(8,128)(2,1)S(1)}, u32[]{:S(2)}, u32[]{:S(2)}) collective-permute-start(bf16[64,1792]{1,0:T(8,128)(2,1)S(1)} %piece_2.1.refs_1_), channel_id=1, source_target_pairs={{0,1},{1,0},{2,3},{3,2},{4,5},{5,4},{6,7},{7,6},{8,9},{9,8},{10,11... | collective-permute-start | bytes 688136 | tf_op jit(solution)/shard_map/ppermute | solution.py:32
  25.2 1.6 %collective-permute-start.6 = (bf16[64,1792]{1,0:T(8,128)(2,1)S(1)}, bf16[64,1792]{1,0:T(8,128)(2,1)S(1)}, u32[]{:S(2)}, u32[]{:S(2)}) collective-permute-start(bf16[64,1792]{1,0:T(8,128)(2,1)S(1)} %piece_2.1.refs_1_), channel_id=1, source_target_pairs={{0,2},{2,0},{4,6},{6,4},{8,10},{10,8},{12,14},{14,12},{16,18},{18,... | collective-permute-start | bytes 688136 | tf_op jit(solution)/shard_map/ppermute | solution.py:20
  26.8 2.2 %up_own_early.1 = (f32[128,1024]{1,0:T(8,128)S(1)}, f32[128,1024]{1,0:T(8,128)S(1)}, bf16[3584,512]{1,0:T(8,128)(2,1)S(1)}) custom-call(bf16[64,3712]{1,0:T(8,128)(2,1)S(1)} %get-tuple-element.41.refs_0_.refs_12_, bf16[64,1792]{1,0:T(8,128)(2,1)S(1)} %piece_2.1.refs_1_, bf16[64,1920]{1,0:T(8,128)(2,1)S(1)} %collective-permute-done.8.refs_2_.refs_14_, ...), custom_call_target="tpu_custom_call" | custom-call | flops 11274289152 | bytes 44040192 | tf_op jit(solution)/shard_map/up_own_early/pallas_call | solution.py:48
  29.1 0.1 collective-permute-start.4
  29.2 2.2 %up_far_early.1 = (f32[128,1024]{1,0:T(8,128)S(1)}, f32[128,1024]{1,0:T(8,128)S(1)}, bf16[1024,1792]{1,0:T(8,128)(2,1)S(1)}) custom-call(bf16[64,3712]{1,0:T(8,128)(2,1)S(1)} %collective-permute-done.10.refs_0_, bf16[64,1792]{1,0:T(8,128)(2,1)S(1)} %collective-permute-done.11.refs_1_, bf16[64,1920]{1,0:T(8,128)(2,1)S(1)} %collective-permute-done.12.refs_2_, ...), custom_call_target="tpu_custom_call" | custom-call | flops 11274289152 | bytes 44040192 | tf_op jit(solution)/shard_map/up_far_early/pallas_call | solution.py:48
  31.4 0.5 collective-permute-start.13
  32.0 0.1 collective-permute-start.7
  32.0 2.2 %up_own_late.1 = (f32[128,1024]{1,0:T(8,128)S(1)}, f32[128,1024]{1,0:T(8,128)S(1)}, bf16[1024,1792]{1,0:T(8,128)(2,1)S(1)}) custom-call(bf16[64,3712]{1,0:T(8,128)(2,1)S(1)} %collective-permute-done.3.refs_1_.refs_0_.refs_13_, bf16[64,1792]{1,0:T(8,128)(2,1)S(1)} %collective-permute-done.6.refs_1_, bf16[64,1920]{1,0:T(8,128)(2,1)S(1)} %piece_3.1.refs_2_.refs_15_, ...), custom_call_target="tpu_custom_call" | custom-call | flops 11274289152 | bytes 44040192 | tf_op jit(solution)/shard_map/up_own_late/pallas_call | solution.py:48
  34.3 2.5 %hidden.1 = (bf16[256,1024]{1,0:T(8,128)(2,1)S(1)}, bf16[1024,1792]{1,0:T(8,128)(2,1)S(1)}) custom-call(bf16[64,3712]{1,0:T(8,128)(2,1)S(1)} %collective-permute-done.4.refs_0_, bf16[64,1792]{1,0:T(8,128)(2,1)S(1)} %collective-permute-done.7.refs_1_, bf16[64,1920]{1,0:T(8,128)(2,1)S(1)} %collective-permute-done.13.refs_2_, ...), custom_call_target="tpu_custom_call" | custom-call | flops 11274289152 | bytes 44040192 | tf_op jit(solution)/shard_map/hidden/pallas_call | solution.py:48
  36.8 1.1 %down_far_a.1 = (bf16[64,3584]{1,0:T(8,128)(2,1)S(1)}, bf16[64,3584]{1,0:T(8,128)(2,1)S(1)}) custom-call(bf16[256,1024]{1,0:T(8,128)(2,1)S(1)} %get-tuple-element.56.hid_ref.refs_0_, bf16[1024,1792]{1,0:T(8,128)(2,1)S(1)} %get-tuple-element.59.rest_0_, bf16[1024,1792]{1,0:T(8,128)(2,1)S(1)} %get-tuple-element.60.rest_1_), custom_call_target="tpu_custom_call" | custom-call | flops 5637144576 | tf_op jit(solution)/shard_map/down_far_a/pallas_call | solution.py:48
  38.0 1.1 %down_far_b.1 = (bf16[64,3584]{1,0:T(8,128)(2,1)S(1)}, bf16[64,3584]{1,0:T(8,128)(2,1)S(1)}) custom-call(bf16[256,1024]{1,0:T(8,128)(2,1)S(1)} %get-tuple-element.56.hid_ref.refs_0_, bf16[1024,1792]{1,0:T(8,128)(2,1)S(1)} %get-tuple-element.59.rest_0_, bf16[1024,1792]{1,0:T(8,128)(2,1)S(1)} %get-tuple-element.60.rest_1_, ...), custom_call_target="tpu_custom_call" | custom-call | flops 5637144576 | tf_op jit(solution)/shard_map/down_far_b/pallas_call | solution.py:48
  39.1 0.5 collective-permute-start.17
  39.6 0.1 collective-permute-start.16
  39.7 0.4 collective-permute-start.14
  40.1 0.1 collective-permute-start.15
  40.2 1.1 %down_own_a.1 = (f32[64,3584]{1,0:T(8,128)S(1)}, f32[64,3584]{1,0:T(8,128)S(1)}) custom-call(bf16[256,1024]{1,0:T(8,128)(2,1)S(1)} %get-tuple-element.56.hid_ref.refs_0_, bf16[1024,1792]{1,0:T(8,128)(2,1)S(1)} %get-tuple-element.57.refs_1_, bf16[1024,1792]{1,0:T(8,128)(2,1)S(1)} %get-tuple-element.58.refs_2_, bf16[64,3584]{1,0:T(8,128)(2,1)S(1)} %get-tuple-element.62.refs_3_), custom_call_target="tpu_custom_call" | custom-call | flops 5637144576 | tf_op jit(solution)/shard_map/down_own_a/pallas_call | solution.py:48
  41.3 0.1 sum_3.1
  41.4 0.9 %collective-permute-start.21 = (bf16[64,1792]{1,0:T(8,128)(2,1)S(1)}, bf16[64,1792]{1,0:T(8,128)(2,1)S(1)}, u32[]{:S(2)}, u32[]{:S(2)}) collective-permute-start(bf16[64,1792]{1,0:T(8,128)(2,1)S(1)} %get-tuple-element.68.refs_3_), channel_id=1, source_target_pairs={{0,2},{2,0},{4,6},{6,4},{8,10},{10,8},{12,14},{14,12},{16,18},{18,... | collective-permute-start | bytes 688136 | tf_op jit(solution)/shard_map/ppermute | solution.py:20
  42.3 1.2 %collective-permute-start.19 = (bf16[64,1792]{1,0:T(8,128)(2,1)S(1)}, bf16[64,1792]{1,0:T(8,128)(2,1)S(1)}, u32[]{:S(2)}, u32[]{:S(2)}) collective-permute-start(bf16[64,1792]{1,0:T(8,128)(2,1)S(1)} %get-tuple-element.67.refs_2_), channel_id=1, source_target_pairs={{0,2},{2,0},{4,6},{6,4},{8,10},{10,8},{12,14},{14,12},{16,18},{18,... | collective-permute-start | bytes 688136 | tf_op jit(solution)/shard_map/ppermute | solution.py:20
  43.5 0.1 sum_1.1.refs_5_
  43.6 0.9 %collective-permute-start.18 = (bf16[64,3584]{1,0:T(8,128)(2,1)S(1)}, bf16[64,3584]{1,0:T(8,128)(2,1)S(1)}, u32[]{:S(2)}, u32[]{:S(2)}) collective-permute-start(bf16[64,3584]{1,0:T(8,128)(2,1)S(1)} %sum_1.1.refs_5_), channel_id=1, source_target_pairs={{0,2},{2,0},{4,6},{6,4},{8,10},{10,8},{12,14},{14,12},{16,18},{18,... | collective-permute-start | bytes 1376264 | tf_op jit(solution)/shard_map/ppermute | solution.py:20
  44.5 1.1 %down_own_b.1 = (bf16[64,3584]{1,0:T(8,128)(2,1)S(1)}, bf16[64,3584]{1,0:T(8,128)(2,1)S(1)}) custom-call(bf16[256,1024]{1,0:T(8,128)(2,1)S(1)} %get-tuple-element.56.hid_ref.refs_0_, bf16[1024,1792]{1,0:T(8,128)(2,1)S(1)} %get-tuple-element.57.refs_1_, bf16[1024,1792]{1,0:T(8,128)(2,1)S(1)} %get-tuple-element.58.refs_2_, ...), custom_call_target="tpu_custom_call" | custom-call | flops 5637144576 | tf_op jit(solution)/shard_map/down_own_b/pallas_call | solution.py:48
  45.7 1.8 %collective-permute-done.21.part_ref = bf16[64,1792]{1,0:T(8,128)(2,1)S(1)} collective-permute-done((bf16[64,1792]{1,0:T(8,128)(2,1)S(1)}, bf16[64,1792]{1,0:T(8,128)(2,1)S(1)}, u32[]{:S(2)}, u32[]{:S(2)}) %collective-permute-start.21) | collective-permute-done | bytes 229408 | tf_op jit(solution)/shard_map/ppermute | solution.py:20
  47.5 1.6 %collective-permute-start.22 = (bf16[64,1792]{1,0:T(8,128)(2,1)S(1)}, bf16[64,1792]{1,0:T(8,128)(2,1)S(1)}, u32[]{:S(2)}, u32[]{:S(2)}) collective-permute-start(bf16[64,1792]{1,0:T(8,128)(2,1)S(1)} %sum_2_1.1), channel_id=1, source_target_pairs={{0,4},{2,6},{4,0},{6,2},{8,12},{10,14},{12,8},{14,10},{16,20},{18,... | collective-permute-start | bytes 688136 | tf_op jit(solution)/shard_map/ppermute | solution.py:20
  49.1 0.8 %collective-permute-done.19.part_ref = bf16[64,1792]{1,0:T(8,128)(2,1)S(1)} collective-permute-done((bf16[64,1792]{1,0:T(8,128)(2,1)S(1)}, bf16[64,1792]{1,0:T(8,128)(2,1)S(1)}, u32[]{:S(2)}, u32[]{:S(2)}) %collective-permute-start.19) | collective-permute-done | bytes 229408 | tf_op jit(solution)/shard_map/ppermute | solution.py:20
  50.0 1.6 %collective-permute-start.20 = (bf16[64,1792]{1,0:T(8,128)(2,1)S(1)}, bf16[64,1792]{1,0:T(8,128)(2,1)S(1)}, u32[]{:S(2)}, u32[]{:S(2)}) collective-permute-start(bf16[64,1792]{1,0:T(8,128)(2,1)S(1)} %sum_2_0.1), channel_id=1, source_target_pairs={{0,4},{2,6},{4,0},{6,2},{8,12},{10,14},{12,8},{14,10},{16,20},{18,... | collective-permute-start | bytes 688136 | tf_op jit(solution)/shard_map/ppermute | solution.py:20
  51.6 2.0 %collective-permute-done.22.refs_3_ = bf16[64,1792]{1,0:T(8,128)(2,1)S(1)} collective-permute-done((bf16[64,1792]{1,0:T(8,128)(2,1)S(1)}, bf16[64,1792]{1,0:T(8,128)(2,1)S(1)}, u32[]{:S(2)}, u32[]{:S(2)}) %collective-permute-start.22) | collective-permute-done | bytes 229408 | tf_op jit(solution)/shard_map/ppermute | solution.py:20
  53.6 2.5 %collective-permute-done.20.refs_2_ = bf16[64,1792]{1,0:T(8,128)(2,1)S(1)} collective-permute-done((bf16[64,1792]{1,0:T(8,128)(2,1)S(1)}, bf16[64,1792]{1,0:T(8,128)(2,1)S(1)}, u32[]{:S(2)}, u32[]{:S(2)}) %collective-permute-start.20) | collective-permute-done | bytes 229408 | tf_op jit(solution)/shard_map/ppermute | solution.py:20
  56.1 0.2 sum_split.1
  56.3 2.5 %collective-permute-start.23 = (bf16[16,3584]{1,0:T(8,128)(2,1)S(1)}, bf16[16,3584]{1,0:T(8,128)(2,1)S(1)}, u32[]{:S(2)}, u32[]{:S(2)}) collective-permute-start(bf16[16,3584]{1,0:T(8,128)(2,1)S(1)} %get-tuple-element.72), channel_id=1, source_target_pairs={{0,24},{2,26},{4,28},{6,30},{8,16},{10,18},{12,20},{14,22},{16,8},... | collective-permute-start | bytes 344072 | tf_op jit(solution)/shard_map/ppermute | solution.py:20
  58.8 1.9 %collective-permute-start.25 = (bf16[16,3584]{1,0:T(8,128)(2,1)S(1)}, bf16[16,3584]{1,0:T(8,128)(2,1)S(1)}, u32[]{:S(2)}, u32[]{:S(2)}) collective-permute-start(bf16[16,3584]{1,0:T(8,128)(2,1)S(1)} %get-tuple-element.74), channel_id=1, source_target_pairs={{0,8},{2,10},{4,12},{6,14},{8,0},{10,2},{12,4},{14,6},{16,24},{18,... | collective-permute-start | bytes 344072 | tf_op jit(solution)/shard_map/ppermute | solution.py:20
  60.7 2.4 %collective-permute-done.23.refs_1_ = bf16[16,3584]{1,0:T(8,128)(2,1)S(1)} collective-permute-done((bf16[16,3584]{1,0:T(8,128)(2,1)S(1)}, bf16[16,3584]{1,0:T(8,128)(2,1)S(1)}, u32[]{:S(2)}, u32[]{:S(2)}) %collective-permute-start.23) | collective-permute-done | bytes 114720 | tf_op jit(solution)/shard_map/ppermute | solution.py:20
  63.1 2.4 %collective-permute-done.24.refs_2_ = bf16[16,3584]{1,0:T(8,128)(2,1)S(1)} collective-permute-done((bf16[16,3584]{1,0:T(8,128)(2,1)S(1)}, bf16[16,3584]{1,0:T(8,128)(2,1)S(1)}, u32[]{:S(2)}, u32[]{:S(2)}) %collective-permute-start.24) | collective-permute-done | bytes 114720 | tf_op jit(solution)/shard_map/ppermute | solution.py:20
  65.5 0.7 %sum_out.1 = bf16[16,3584]{1,0:T(8,128)(2,1)} custom-call(bf16[16,3584]{1,0:T(8,128)(2,1)S(1)} %get-tuple-element.71.refs_0_, bf16[16,3584]{1,0:T(8,128)(2,1)S(1)} %collective-permute-done.23.refs_1_, bf16[16,3584]{1,0:T(8,128)(2,1)S(1)} %collective-permute-done.24.refs_2_, bf16[16,3584]{1,0:T(8,128)(2,1)S(1)} %collective-permute-done.25.refs_3_), custom_call_target="tpu_custom_call" | custom-call | tf_op jit(solution)/shard_map/sum_out/pallas_call | solution.py:48
  (24 shorter events, 0.2 us)
Async XLA Ops:
  1.0 10.9 %collective-permute-start = (bf16[16,3712]{1,0:T(8,128)(2,1)S(1)}, bf16[16,3712]{1,0:T(8,128)(2,1)S(1)}, u32[]{:S(2)}, u32[]{:S(2)}) collective-permute-start(bf16[16,3712]{1,0:T(8,128)(2,1)S(1)} %first_piece.1.refs_0_), channel_id=1, source_target_pairs={{0,8},{2,10},{4,12},{6,14},{8,0},{10,2},{12,4},{14,6},{16,24},{18,... | collective-permute-start | bytes 356360 | tf_op jit(solution)/shard_map/ppermute | solution.py:20
  4.1 7.9 %collective-permute-start.1 = (bf16[16,3712]{1,0:T(8,128)(2,1)S(1)}, bf16[16,3712]{1,0:T(8,128)(2,1)S(1)}, u32[]{:S(2)}, u32[]{:S(2)}) collective-permute-start(bf16[16,3712]{1,0:T(8,128)(2,1)S(1)} %first_piece.1.refs_0_), channel_id=1, source_target_pairs={{0,16},{2,18},{4,20},{6,22},{8,24},{10,26},{12,28},{14,30},{16,0},... | collective-permute-start | bytes 356360 | tf_op jit(solution)/shard_map/ppermute | solution.py:20
  6.6 6.8 %collective-permute-start.2 = (bf16[16,3712]{1,0:T(8,128)(2,1)S(1)}, bf16[16,3712]{1,0:T(8,128)(2,1)S(1)}, u32[]{:S(2)}, u32[]{:S(2)}) collective-permute-start(bf16[16,3712]{1,0:T(8,128)(2,1)S(1)} %first_piece.1.refs_0_), channel_id=1, source_target_pairs={{0,24},{2,26},{4,28},{6,30},{8,16},{10,18},{12,20},{14,22},{16,8},... | collective-permute-start | bytes 356360 | tf_op jit(solution)/shard_map/ppermute | solution.py:20
  13.5 10.2 %collective-permute-start.3 = (bf16[64,3712]{1,0:T(8,128)(2,1)S(1)}, bf16[64,3712]{1,0:T(8,128)(2,1)S(1)}, u32[]{:S(2)}, u32[]{:S(2)}) collective-permute-start(bf16[64,3712]{1,0:T(8,128)(2,1)S(1)} %get-tuple-element.41.refs_0_.refs_12_), channel_id=1, source_target_pairs={{0,2},{2,0},{4,6},{6,4},{8,10},{10,8},{12,14},{14,12},{16,18},{18,... | collective-permute-start | bytes 1425416 | tf_op jit(solution)/shard_map/ppermute | solution.py:20
  15.0 7.3 %collective-permute-start.8 = (bf16[64,1920]{1,0:T(8,128)(2,1)S(1)}, bf16[64,1920]{1,0:T(8,128)(2,1)S(1)}, u32[]{:S(2)}, u32[]{:S(2)}) collective-permute-start(bf16[64,1920]{1,0:T(8,128)(2,1)S(1)} %get-tuple-element.44), channel_id=1, source_target_pairs={{0,4},{2,6},{4,0},{6,2},{8,12},{10,14},{12,8},{14,10},{16,20},{18,... | collective-permute-start | bytes 737288 | tf_op jit(solution)/shard_map/ppermute | solution.py:20
  16.6 7.1 %collective-permute-start.5 = (bf16[64,1792]{1,0:T(8,128)(2,1)S(1)}, bf16[64,1792]{1,0:T(8,128)(2,1)S(1)}, u32[]{:S(2)}, u32[]{:S(2)}) collective-permute-start(bf16[64,1792]{1,0:T(8,128)(2,1)S(1)} %get-tuple-element.42), channel_id=1, source_target_pairs={{0,4},{2,6},{4,0},{6,2},{8,12},{10,14},{12,8},{14,10},{16,20},{18,... | collective-permute-start | bytes 688136 | tf_op jit(solution)/shard_map/ppermute | solution.py:20
  22.3 6.8 %collective-permute-start.10 = (bf16[64,3712]{1,0:T(8,128)(2,1)S(1)}, bf16[64,3712]{1,0:T(8,128)(2,1)S(1)}, u32[]{:S(2)}, u32[]{:S(2)}) collective-permute-start(bf16[64,3712]{1,0:T(8,128)(2,1)S(1)} %get-tuple-element.41.refs_0_.refs_12_), channel_id=1, source_target_pairs={{0,1},{1,0},{2,3},{3,2},{4,5},{5,4},{6,7},{7,6},{8,9},{9,8},{10,11... | collective-permute-start | bytes 1425416 | tf_op jit(solution)/shard_map/ppermute | solution.py:32
  22.4 6.8 %collective-permute-start.12 = (bf16[64,1920]{1,0:T(8,128)(2,1)S(1)}, bf16[64,1920]{1,0:T(8,128)(2,1)S(1)}, u32[]{:S(2)}, u32[]{:S(2)}) collective-permute-start(bf16[64,1920]{1,0:T(8,128)(2,1)S(1)} %collective-permute-done.8.refs_2_.refs_14_), channel_id=1, source_target_pairs={{0,1},{1,0},{2,3},{3,2},{4,5},{5,4},{6,7},{7,6},{8,9},{9,8},{10,11... | collective-permute-start | bytes 737288 | tf_op jit(solution)/shard_map/ppermute | solution.py:32
  22.8 8.5 %collective-permute-start.9 = (bf16[64,1920]{1,0:T(8,128)(2,1)S(1)}, bf16[64,1920]{1,0:T(8,128)(2,1)S(1)}, u32[]{:S(2)}, u32[]{:S(2)}) collective-permute-start(bf16[64,1920]{1,0:T(8,128)(2,1)S(1)} %collective-permute-done.8.refs_2_.refs_14_), channel_id=1, source_target_pairs={{0,2},{2,0},{4,6},{6,4},{8,10},{10,8},{12,14},{14,12},{16,18},{18,... | collective-permute-start | bytes 737288 | tf_op jit(solution)/shard_map/ppermute | solution.py:20
  23.7 5.5 %collective-permute-start.11 = (bf16[64,1792]{1,0:T(8,128)(2,1)S(1)}, bf16[64,1792]{1,0:T(8,128)(2,1)S(1)}, u32[]{:S(2)}, u32[]{:S(2)}) collective-permute-start(bf16[64,1792]{1,0:T(8,128)(2,1)S(1)} %piece_2.1.refs_1_), channel_id=1, source_target_pairs={{0,1},{1,0},{2,3},{3,2},{4,5},{5,4},{6,7},{7,6},{8,9},{9,8},{10,11... | collective-permute-start | bytes 688136 | tf_op jit(solution)/shard_map/ppermute | solution.py:32
  25.2 6.7 %collective-permute-start.6 = (bf16[64,1792]{1,0:T(8,128)(2,1)S(1)}, bf16[64,1792]{1,0:T(8,128)(2,1)S(1)}, u32[]{:S(2)}, u32[]{:S(2)}) collective-permute-start(bf16[64,1792]{1,0:T(8,128)(2,1)S(1)} %piece_2.1.refs_1_), channel_id=1, source_target_pairs={{0,2},{2,0},{4,6},{6,4},{8,10},{10,8},{12,14},{14,12},{16,18},{18,... | collective-permute-start | bytes 688136 | tf_op jit(solution)/shard_map/ppermute | solution.py:20
  29.1 5.2 %collective-permute-start.4 = (bf16[64,3712]{1,0:T(8,128)(2,1)S(1)}, bf16[64,3712]{1,0:T(8,128)(2,1)S(1)}, u32[]{:S(2)}, u32[]{:S(2)}) collective-permute-start(bf16[64,3712]{1,0:T(8,128)(2,1)S(1)} %collective-permute-done.3.refs_1_.refs_0_.refs_13_), channel_id=1, source_target_pairs={{0,1},{1,0},{2,3},{3,2},{4,5},{5,4},{6,7},{7,6},{8,9},{9,8},{10,11... | collective-permute-start | bytes 1425416 | tf_op jit(solution)/shard_map/ppermute | solution.py:32
  31.4 2.9 %collective-permute-start.13 = (bf16[64,1920]{1,0:T(8,128)(2,1)S(1)}, bf16[64,1920]{1,0:T(8,128)(2,1)S(1)}, u32[]{:S(2)}, u32[]{:S(2)}) collective-permute-start(bf16[64,1920]{1,0:T(8,128)(2,1)S(1)} %piece_3.1.refs_2_.refs_15_), channel_id=1, source_target_pairs={{0,1},{1,0},{2,3},{3,2},{4,5},{5,4},{6,7},{7,6},{8,9},{9,8},{10,11... | collective-permute-start | bytes 737288 | tf_op jit(solution)/shard_map/ppermute | solution.py:32
  32.0 2.3 %collective-permute-start.7 = (bf16[64,1792]{1,0:T(8,128)(2,1)S(1)}, bf16[64,1792]{1,0:T(8,128)(2,1)S(1)}, u32[]{:S(2)}, u32[]{:S(2)}) collective-permute-start(bf16[64,1792]{1,0:T(8,128)(2,1)S(1)} %collective-permute-done.6.refs_1_), channel_id=1, source_target_pairs={{0,1},{1,0},{2,3},{3,2},{4,5},{5,4},{6,7},{7,6},{8,9},{9,8},{10,11... | collective-permute-start | bytes 688136 | tf_op jit(solution)/shard_map/ppermute | solution.py:32
  39.1 2.2 %collective-permute-start.17 = (bf16[64,3584]{1,0:T(8,128)(2,1)S(1)}, bf16[64,3584]{1,0:T(8,128)(2,1)S(1)}, u32[]{:S(2)}, u32[]{:S(2)}) collective-permute-start(bf16[64,3584]{1,0:T(8,128)(2,1)S(1)} %get-tuple-element.61.rest_2_), channel_id=1, source_target_pairs={{0,1},{1,0},{2,3},{3,2},{4,5},{5,4},{6,7},{7,6},{8,9},{9,8},{10,11... | collective-permute-start | bytes 1376264 | tf_op jit(solution)/shard_map/ppermute | solution.py:32
  39.6 3.9 %collective-permute-start.16 = (bf16[64,3584]{1,0:T(8,128)(2,1)S(1)}, bf16[64,3584]{1,0:T(8,128)(2,1)S(1)}, u32[]{:S(2)}, u32[]{:S(2)}) collective-permute-start(bf16[64,3584]{1,0:T(8,128)(2,1)S(1)} %get-tuple-element.65), channel_id=1, source_target_pairs={{0,1},{1,0},{2,3},{3,2},{4,5},{5,4},{6,7},{7,6},{8,9},{9,8},{10,11... | collective-permute-start | bytes 1376264 | tf_op jit(solution)/shard_map/ppermute | solution.py:32
  39.7 4.9 %collective-permute-start.14 = (bf16[64,3584]{1,0:T(8,128)(2,1)S(1)}, bf16[64,3584]{1,0:T(8,128)(2,1)S(1)}, u32[]{:S(2)}, u32[]{:S(2)}) collective-permute-start(bf16[64,3584]{1,0:T(8,128)(2,1)S(1)} %get-tuple-element.62.refs_3_), channel_id=1, source_target_pairs={{0,1},{1,0},{2,3},{3,2},{4,5},{5,4},{6,7},{7,6},{8,9},{9,8},{10,11... | collective-permute-start | bytes 1376264 | tf_op jit(solution)/shard_map/ppermute | solution.py:32
  40.1 4.4 %collective-permute-start.15 = (bf16[64,3584]{1,0:T(8,128)(2,1)S(1)}, bf16[64,3584]{1,0:T(8,128)(2,1)S(1)}, u32[]{:S(2)}, u32[]{:S(2)}) collective-permute-start(bf16[64,3584]{1,0:T(8,128)(2,1)S(1)} %get-tuple-element.63), channel_id=1, source_target_pairs={{0,1},{1,0},{2,3},{3,2},{4,5},{5,4},{6,7},{7,6},{8,9},{9,8},{10,11... | collective-permute-start | bytes 1376264 | tf_op jit(solution)/shard_map/ppermute | solution.py:32
  41.4 6.1 %collective-permute-start.21 = (bf16[64,1792]{1,0:T(8,128)(2,1)S(1)}, bf16[64,1792]{1,0:T(8,128)(2,1)S(1)}, u32[]{:S(2)}, u32[]{:S(2)}) collective-permute-start(bf16[64,1792]{1,0:T(8,128)(2,1)S(1)} %get-tuple-element.68.refs_3_), channel_id=1, source_target_pairs={{0,2},{2,0},{4,6},{6,4},{8,10},{10,8},{12,14},{14,12},{16,18},{18,... | collective-permute-start | bytes 688136 | tf_op jit(solution)/shard_map/ppermute | solution.py:20
  42.3 7.6 %collective-permute-start.19 = (bf16[64,1792]{1,0:T(8,128)(2,1)S(1)}, bf16[64,1792]{1,0:T(8,128)(2,1)S(1)}, u32[]{:S(2)}, u32[]{:S(2)}) collective-permute-start(bf16[64,1792]{1,0:T(8,128)(2,1)S(1)} %get-tuple-element.67.refs_2_), channel_id=1, source_target_pairs={{0,2},{2,0},{4,6},{6,4},{8,10},{10,8},{12,14},{14,12},{16,18},{18,... | collective-permute-start | bytes 688136 | tf_op jit(solution)/shard_map/ppermute | solution.py:20
  43.6 12.5 %collective-permute-start.18 = (bf16[64,3584]{1,0:T(8,128)(2,1)S(1)}, bf16[64,3584]{1,0:T(8,128)(2,1)S(1)}, u32[]{:S(2)}, u32[]{:S(2)}) collective-permute-start(bf16[64,3584]{1,0:T(8,128)(2,1)S(1)} %sum_1.1.refs_5_), channel_id=1, source_target_pairs={{0,2},{2,0},{4,6},{6,4},{8,10},{10,8},{12,14},{14,12},{16,18},{18,... | collective-permute-start | bytes 1376264 | tf_op jit(solution)/shard_map/ppermute | solution.py:20
  47.5 6.1 %collective-permute-start.22 = (bf16[64,1792]{1,0:T(8,128)(2,1)S(1)}, bf16[64,1792]{1,0:T(8,128)(2,1)S(1)}, u32[]{:S(2)}, u32[]{:S(2)}) collective-permute-start(bf16[64,1792]{1,0:T(8,128)(2,1)S(1)} %sum_2_1.1), channel_id=1, source_target_pairs={{0,4},{2,6},{4,0},{6,2},{8,12},{10,14},{12,8},{14,10},{16,20},{18,... | collective-permute-start | bytes 688136 | tf_op jit(solution)/shard_map/ppermute | solution.py:20
  50.0 6.1 %collective-permute-start.20 = (bf16[64,1792]{1,0:T(8,128)(2,1)S(1)}, bf16[64,1792]{1,0:T(8,128)(2,1)S(1)}, u32[]{:S(2)}, u32[]{:S(2)}) collective-permute-start(bf16[64,1792]{1,0:T(8,128)(2,1)S(1)} %sum_2_0.1), channel_id=1, source_target_pairs={{0,4},{2,6},{4,0},{6,2},{8,12},{10,14},{12,8},{14,10},{16,20},{18,... | collective-permute-start | bytes 688136 | tf_op jit(solution)/shard_map/ppermute | solution.py:20
  56.3 6.8 %collective-permute-start.23 = (bf16[16,3584]{1,0:T(8,128)(2,1)S(1)}, bf16[16,3584]{1,0:T(8,128)(2,1)S(1)}, u32[]{:S(2)}, u32[]{:S(2)}) collective-permute-start(bf16[16,3584]{1,0:T(8,128)(2,1)S(1)} %get-tuple-element.72), channel_id=1, source_target_pairs={{0,24},{2,26},{4,28},{6,30},{8,16},{10,18},{12,20},{14,22},{16,8},... | collective-permute-start | bytes 344072 | tf_op jit(solution)/shard_map/ppermute | solution.py:20
  58.8 6.7 %collective-permute-start.24 = (bf16[16,3584]{1,0:T(8,128)(2,1)S(1)}, bf16[16,3584]{1,0:T(8,128)(2,1)S(1)}, u32[]{:S(2)}, u32[]{:S(2)}) collective-permute-start(bf16[16,3584]{1,0:T(8,128)(2,1)S(1)} %get-tuple-element.73), channel_id=1, source_target_pairs={{0,16},{2,18},{4,20},{6,22},{8,24},{10,26},{12,28},{14,30},{16,0},... | collective-permute-start | bytes 344072 | tf_op jit(solution)/shard_map/ppermute | solution.py:20
  58.8 6.7 %collective-permute-start.25 = (bf16[16,3584]{1,0:T(8,128)(2,1)S(1)}, bf16[16,3584]{1,0:T(8,128)(2,1)S(1)}, u32[]{:S(2)}, u32[]{:S(2)}) collective-permute-start(bf16[16,3584]{1,0:T(8,128)(2,1)S(1)} %get-tuple-element.74), channel_id=1, source_target_pairs={{0,8},{2,10},{4,12},{6,14},{8,0},{10,2},{12,4},{14,6},{16,24},{18,... | collective-permute-start | bytes 344072 | tf_op jit(solution)/shard_map/ppermute | solution.py:20

commit v7 on v6

--- a/solution.py
+++ b/solution.py
@@ -35,7 +35,7 @@
 VMEM = pl.BlockSpec(memory_space=pltpu.VMEM)
 HBM = pl.BlockSpec(memory_space=pltpu.HBM)
 TILE = 256
-WEIGHT = 6
+WEIGHT = 3
 
 
 def kept(rows, columns, dtype=jnp.bfloat16):
@@ -480,15 +480,16 @@
     )
 
     down_mine = (down_left, down_right)
-    received, before = {}, ()
-    for held, name in (((3, 1), "a"), ((2, 0), "b")):
-        partial = down_far(hidden, down_other, held, "down_far_" + name, before)
-        for k, part in zip(held, partial):
-            received[k] = other_core(part)
-        before = (partial[0],)
+    partial = {}
+    partial[3], partial[1] = down_far(hidden, down_other, (3, 1), "down_far_a")
+    partial[2], partial[0] = down_far(hidden, down_other, (2, 0), "down_far_b", (partial[3],))
+    before = (partial[2],)
+    received = {3: other_core(partial[3])}
     mine_3, mine_1 = down_own(hidden, down_mine, (), (3, 1), "down_own_a", before)
     sides_3 = add((mine_3, received[3]), "sum_3", [side, half - side])
     passed = [second_hop(part, 1) for part in sides_3]
+    for k in (1, 2, 0):
+        received[k] = other_core(tied(partial[k], sides_3, "far_%d" % k))
     (sum_1,) = add((mine_1, received[1]), "sum_1", before=sides_3)
     sum_2, sum_0 = down_own(hidden, down_mine, (received[2], received[0]), (2, 0), "down_own_b", (sum_1,))
     sum_1 = second_hop(sum_1, 1)

time: 67.4 us -> 67.3 us (level)
    pallas_call x20 -> x23, Pallas kernels: 26.3 us -> 26.3 us  [call(): pl.pallas_call(kernel, out_shape=out_shape, in_specs=specs or [VMEM] * le...]
  transfers between devices with their start and end apart: 26 -> 26, of which waited for: 8 -> 8; matrix products, arithmetic and copies ran while one was open for 0% -> 0% of each run, Pallas kernels for 30% -> 31%
where the time goes in v7:
time: 67.3 us; the launch traced here: 66.2 us
  Pallas kernels  26.3 us (39%)
  starting transfers between devices  26 us (39%)
  waiting for transfers between devices  13.7 us (20%)
    pallas_call x23, Pallas kernels, call(): pl.pallas_call(kernel, out_shape=out_shape, in_specs=specs or [VMEM] * le...  26.3 us
    ppermute x16, starting transfers between devices, exchanged(): return lax.ppermute(array, ('expert', 'hsplit'), route)  22 us
    ppermute x16, waiting for transfers between devices, exchanged(): return lax.ppermute(array, ('expert', 'hsplit'), route)  13.7 us
    ppermute x10, starting transfers between devices, other_core(): return lax.ppermute(array, 'hsplit', [(0, 1), (1, 0)])  3.95 us
  transfers between devices with their start and end apart: 26, of which 8 were waited for; matrix products, arithmetic and copies ran while one was open for 0% of the time, Pallas kernels for 31%

profile of v7, /device:TPU:0, one launch (start us, length us, event | category | flops | bytes accessed | tf_op | source)
XLA Modules:
  0.0 66.2 jit_solution(16047406044607470706)
XLA Ops:
  0.0 1.0 %first_piece.1.refs_0_ = bf16[16,3712]{1,0:T(8,128)(2,1)S(1)} custom-call(bf16[16,7168]{1,0:T(8,128)(2,1)} %tok_in.1, s32[8,16]{1,0:T(8,128)} %bitcast.14, f32[8,16]{1,0:T(8,128)} %bitcast.15), custom_call_target="tpu_custom_call" | custom-call | tf_op jit(solution)/shard_map/first_piece/pallas_call | solution.py:48
  1.0 3.1 %collective-permute-start = (bf16[16,3712]{1,0:T(8,128)(2,1)S(1)}, bf16[16,3712]{1,0:T(8,128)(2,1)S(1)}, u32[]{:S(2)}, u32[]{:S(2)}) collective-permute-start(bf16[16,3712]{1,0:T(8,128)(2,1)S(1)} %first_piece.1.refs_0_), channel_id=1, source_target_pairs={{0,8},{2,10},{4,12},{6,14},{8,0},{10,2},{12,4},{14,6},{16,24},{18,... | collective-permute-start | bytes 356360 | tf_op jit(solution)/shard_map/ppermute | solution.py:20
  4.1 2.6 %collective-permute-start.1 = (bf16[16,3712]{1,0:T(8,128)(2,1)S(1)}, bf16[16,3712]{1,0:T(8,128)(2,1)S(1)}, u32[]{:S(2)}, u32[]{:S(2)}) collective-permute-start(bf16[16,3712]{1,0:T(8,128)(2,1)S(1)} %first_piece.1.refs_0_), channel_id=1, source_target_pairs={{0,16},{2,18},{4,20},{6,22},{8,24},{10,26},{12,28},{14,30},{16,0},... | collective-permute-start | bytes 356360 | tf_op jit(solution)/shard_map/ppermute | solution.py:20
  6.6 5.2 %fetch_1.1 = (bf16[3584,1024]{1,0:T(8,128)(2,1)S(1)}, bf16[1024,1792]{1,0:T(8,128)(2,1)S(1)}, bf16[3584,512]{1,0:T(8,128)(2,1)S(1)}, f32[8,128]{1,0:T(8,128)S(1)}) custom-call(bf16[7168,1024]{1,0:T(8,128)(2,1)} %bitcast.12, bf16[1024,7168]{1,0:T(8,128)(2,1)} %bitcast.5, bf16[7168,1024]{1,0:T(8,128)(2,1)} %bitcast.9), custom_call_target="tpu_custom_call" | custom-call | bytes 88080384 | tf_op jit(solution)/shard_map/fetch_1/pallas_call | solution.py:48
  11.9 1.5 %collective-permute-done.2.refs_3_ = bf16[16,3712]{1,0:T(8,128)(2,1)S(1)} collective-permute-done((bf16[16,3712]{1,0:T(8,128)(2,1)S(1)}, bf16[16,3712]{1,0:T(8,128)(2,1)S(1)}, u32[]{:S(2)}, u32[]{:S(2)}) %collective-permute-start.2) | collective-permute-done | bytes 118816 | tf_op jit(solution)/shard_map/ppermute | solution.py:20
  13.4 0.1 second.1
  13.5 1.5 %collective-permute-start.3 = (bf16[64,3712]{1,0:T(8,128)(2,1)S(1)}, bf16[64,3712]{1,0:T(8,128)(2,1)S(1)}, u32[]{:S(2)}, u32[]{:S(2)}) collective-permute-start(bf16[64,3712]{1,0:T(8,128)(2,1)S(1)} %get-tuple-element.41.refs_0_.refs_12_), channel_id=1, source_target_pairs={{0,2},{2,0},{4,6},{6,4},{8,10},{10,8},{12,14},{14,12},{16,18},{18,... | collective-permute-start | bytes 1425416 | tf_op jit(solution)/shard_map/ppermute | solution.py:20
  15.0 1.5 %collective-permute-start.8 = (bf16[64,1920]{1,0:T(8,128)(2,1)S(1)}, bf16[64,1920]{1,0:T(8,128)(2,1)S(1)}, u32[]{:S(2)}, u32[]{:S(2)}) collective-permute-start(bf16[64,1920]{1,0:T(8,128)(2,1)S(1)} %get-tuple-element.44), channel_id=1, source_target_pairs={{0,4},{2,6},{4,0},{6,2},{8,12},{10,14},{12,8},{14,10},{16,20},{18,... | collective-permute-start | bytes 737288 | tf_op jit(solution)/shard_map/ppermute | solution.py:20
  16.6 0.5 collective-permute-start.5
  17.1 5.2 %fetch_2.1 = (bf16[3584,1024]{1,0:T(8,128)(2,1)S(1)}, bf16[3584,1024]{1,0:T(8,128)(2,1)S(1)}, f32[8,128]{1,0:T(8,128)S(1)}) custom-call(bf16[7168,1024]{1,0:T(8,128)(2,1)} %bitcast.10, bf16[7168,1024]{1,0:T(8,128)(2,1)} %bitcast.13), custom_call_target="tpu_custom_call" | custom-call | bytes 88080384 | tf_op jit(solution)/shard_map/fetch_2/pallas_call | solution.py:48
  22.3 0.1 collective-permute-start.10
  22.4 0.5 collective-permute-start.12
  22.8 0.6 collective-permute-start.9
  23.4 0.3 collective-permute-done.5.refs_0_
  23.7 1.5 %collective-permute-start.11 = (bf16[64,1792]{1,0:T(8,128)(2,1)S(1)}, bf16[64,1792]{1,0:T(8,128)(2,1)S(1)}, u32[]{:S(2)}, u32[]{:S(2)}) collective-permute-start(bf16[64,1792]{1,0:T(8,128)(2,1)S(1)} %piece_2.1.refs_1_), channel_id=1, source_target_pairs={{0,1},{1,0},{2,3},{3,2},{4,5},{5,4},{6,7},{7,6},{8,9},{9,8},{10,11... | collective-permute-start | bytes 688136 | tf_op jit(solution)/shard_map/ppermute | solution.py:32
  25.2 1.6 %collective-permute-start.6 = (bf16[64,1792]{1,0:T(8,128)(2,1)S(1)}, bf16[64,1792]{1,0:T(8,128)(2,1)S(1)}, u32[]{:S(2)}, u32[]{:S(2)}) collective-permute-start(bf16[64,1792]{1,0:T(8,128)(2,1)S(1)} %piece_2.1.refs_1_), channel_id=1, source_target_pairs={{0,2},{2,0},{4,6},{6,4},{8,10},{10,8},{12,14},{14,12},{16,18},{18,... | collective-permute-start | bytes 688136 | tf_op jit(solution)/shard_map/ppermute | solution.py:20
  26.8 2.3 %up_own_early.1 = (f32[128,1024]{1,0:T(8,128)S(1)}, f32[128,1024]{1,0:T(8,128)S(1)}, bf16[3584,512]{1,0:T(8,128)(2,1)S(1)}) custom-call(bf16[64,3712]{1,0:T(8,128)(2,1)S(1)} %get-tuple-element.41.refs_0_.refs_12_, bf16[64,1792]{1,0:T(8,128)(2,1)S(1)} %piece_2.1.refs_1_, bf16[64,1920]{1,0:T(8,128)(2,1)S(1)} %collective-permute-done.8.refs_2_.refs_14_, ...), custom_call_target="tpu_custom_call" | custom-call | flops 5637144576 | bytes 22020096 | tf_op jit(solution)/shard_map/up_own_early/pallas_call | solution.py:48
  29.2 0.1 collective-permute-start.4
  29.3 2.1 %up_far_early.1 = (f32[128,1024]{1,0:T(8,128)S(1)}, f32[128,1024]{1,0:T(8,128)S(1)}, bf16[1024,1792]{1,0:T(8,128)(2,1)S(1)}) custom-call(bf16[64,3712]{1,0:T(8,128)(2,1)S(1)} %collective-permute-done.10.refs_0_, bf16[64,1792]{1,0:T(8,128)(2,1)S(1)} %collective-permute-done.11.refs_1_, bf16[64,1920]{1,0:T(8,128)(2,1)S(1)} %collective-permute-done.12.refs_2_, ...), custom_call_target="tpu_custom_call" | custom-call | flops 5637144576 | bytes 22020096 | tf_op jit(solution)/shard_map/up_far_early/pallas_call | solution.py:48
  31.4 0.5 collective-permute-start.13
  31.9 0.1 collective-permute-start.7
  32.0 2.2 %up_own_late.1 = (f32[128,1024]{1,0:T(8,128)S(1)}, f32[128,1024]{1,0:T(8,128)S(1)}, bf16[1024,1792]{1,0:T(8,128)(2,1)S(1)}) custom-call(bf16[64,3712]{1,0:T(8,128)(2,1)S(1)} %collective-permute-done.3.refs_1_.refs_0_.refs_13_, bf16[64,1792]{1,0:T(8,128)(2,1)S(1)} %collective-permute-done.6.refs_1_, bf16[64,1920]{1,0:T(8,128)(2,1)S(1)} %piece_3.1.refs_2_.refs_15_, ...), custom_call_target="tpu_custom_call" | custom-call | flops 5637144576 | bytes 22020096 | tf_op jit(solution)/shard_map/up_own_late/pallas_call | solution.py:48
  34.3 2.5 %hidden.1 = (bf16[256,1024]{1,0:T(8,128)(2,1)S(1)}, bf16[1024,1792]{1,0:T(8,128)(2,1)S(1)}) custom-call(bf16[64,3712]{1,0:T(8,128)(2,1)S(1)} %collective-permute-done.4.refs_0_, bf16[64,1792]{1,0:T(8,128)(2,1)S(1)} %collective-permute-done.7.refs_1_, bf16[64,1920]{1,0:T(8,128)(2,1)S(1)} %collective-permute-done.13.refs_2_, ...), custom_call_target="tpu_custom_call" | custom-call | flops 5637144576 | bytes 22020096 | tf_op jit(solution)/shard_map/hidden/pallas_call | solution.py:48
  36.8 1.1 %down_far_a.1 = (bf16[64,3584]{1,0:T(8,128)(2,1)S(1)}, bf16[64,3584]{1,0:T(8,128)(2,1)S(1)}) custom-call(bf16[256,1024]{1,0:T(8,128)(2,1)S(1)} %get-tuple-element.56.hid_ref.refs_0_, bf16[1024,1792]{1,0:T(8,128)(2,1)S(1)} %get-tuple-element.59.rest_0_, bf16[1024,1792]{1,0:T(8,128)(2,1)S(1)} %get-tuple-element.60.rest_1_), custom_call_target="tpu_custom_call" | custom-call | flops 2818572288 | tf_op jit(solution)/shard_map/down_far_a/pallas_call | solution.py:48
  37.9 0.5 collective-permute-start.14
  38.4 1.1 %down_far_b.1 = (bf16[64,3584]{1,0:T(8,128)(2,1)S(1)}, bf16[64,3584]{1,0:T(8,128)(2,1)S(1)}) custom-call(bf16[256,1024]{1,0:T(8,128)(2,1)S(1)} %get-tuple-element.56.hid_ref.refs_0_, bf16[1024,1792]{1,0:T(8,128)(2,1)S(1)} %get-tuple-element.59.rest_0_, bf16[1024,1792]{1,0:T(8,128)(2,1)S(1)} %get-tuple-element.60.rest_1_, ...), custom_call_target="tpu_custom_call" | custom-call | flops 2818572288 | tf_op jit(solution)/shard_map/down_far_b/pallas_call | solution.py:48
  39.6 1.1 %down_own_a.1 = (f32[64,3584]{1,0:T(8,128)S(1)}, f32[64,3584]{1,0:T(8,128)S(1)}) custom-call(bf16[256,1024]{1,0:T(8,128)(2,1)S(1)} %get-tuple-element.56.hid_ref.refs_0_, bf16[1024,1792]{1,0:T(8,128)(2,1)S(1)} %get-tuple-element.57.refs_1_, bf16[1024,1792]{1,0:T(8,128)(2,1)S(1)} %get-tuple-element.58.refs_2_, ...), custom_call_target="tpu_custom_call" | custom-call | flops 2818572288 | tf_op jit(solution)/shard_map/down_own_a/pallas_call | solution.py:48
  40.7 0.1 sum_3.1
  40.8 0.1 collective-permute-start.17
  41.0 0.4 collective-permute-start.16
  41.4 0.1 collective-permute-start.15
  41.5 0.9 %collective-permute-start.21 = (bf16[64,1792]{1,0:T(8,128)(2,1)S(1)}, bf16[64,1792]{1,0:T(8,128)(2,1)S(1)}, u32[]{:S(2)}, u32[]{:S(2)}) collective-permute-start(bf16[64,1792]{1,0:T(8,128)(2,1)S(1)} %get-tuple-element.65.refs_2_.refs_3_), channel_id=1, source_target_pairs={{0,2},{2,0},{4,6},{6,4},{8,10},{10,8},{12,14},{14,12},{16,18},{18,... | collective-permute-start | bytes 688136 | tf_op jit(solution)/shard_map/ppermute | solution.py:20
  42.4 1.1 %collective-permute-start.19 = (bf16[64,1792]{1,0:T(8,128)(2,1)S(1)}, bf16[64,1792]{1,0:T(8,128)(2,1)S(1)}, u32[]{:S(2)}, u32[]{:S(2)}) collective-permute-start(bf16[64,1792]{1,0:T(8,128)(2,1)S(1)} %get-tuple-element.64.refs_1_.refs_2_), channel_id=1, source_target_pairs={{0,2},{2,0},{4,6},{6,4},{8,10},{10,8},{12,14},{14,12},{16,18},{18,... | collective-permute-start | bytes 688136 | tf_op jit(solution)/shard_map/ppermute | solution.py:20
  43.5 0.1 sum_1.1.refs_5_
  43.6 1.0 %collective-permute-start.18 = (bf16[64,3584]{1,0:T(8,128)(2,1)S(1)}, bf16[64,3584]{1,0:T(8,128)(2,1)S(1)}, u32[]{:S(2)}, u32[]{:S(2)}) collective-permute-start(bf16[64,3584]{1,0:T(8,128)(2,1)S(1)} %sum_1.1.refs_5_), channel_id=1, source_target_pairs={{0,2},{2,0},{4,6},{6,4},{8,10},{10,8},{12,14},{14,12},{16,18},{18,... | collective-permute-start | bytes 1376264 | tf_op jit(solution)/shard_map/ppermute | solution.py:20
  44.6 1.1 %down_own_b.1 = (bf16[64,3584]{1,0:T(8,128)(2,1)S(1)}, bf16[64,3584]{1,0:T(8,128)(2,1)S(1)}) custom-call(bf16[256,1024]{1,0:T(8,128)(2,1)S(1)} %get-tuple-element.56.hid_ref.refs_0_, bf16[1024,1792]{1,0:T(8,128)(2,1)S(1)} %get-tuple-element.57.refs_1_, bf16[1024,1792]{1,0:T(8,128)(2,1)S(1)} %get-tuple-element.58.refs_2_, ...), custom_call_target="tpu_custom_call" | custom-call | flops 2818572288 | tf_op jit(solution)/shard_map/down_own_b/pallas_call | solution.py:48
  45.7 1.8 %collective-permute-done.21.part_ref = bf16[64,1792]{1,0:T(8,128)(2,1)S(1)} collective-permute-done((bf16[64,1792]{1,0:T(8,128)(2,1)S(1)}, bf16[64,1792]{1,0:T(8,128)(2,1)S(1)}, u32[]{:S(2)}, u32[]{:S(2)}) %collective-permute-start.21) | collective-permute-done | bytes 229408 | tf_op jit(solution)/shard_map/ppermute | solution.py:20
  47.6 1.6 %collective-permute-start.22 = (bf16[64,1792]{1,0:T(8,128)(2,1)S(1)}, bf16[64,1792]{1,0:T(8,128)(2,1)S(1)}, u32[]{:S(2)}, u32[]{:S(2)}) collective-permute-start(bf16[64,1792]{1,0:T(8,128)(2,1)S(1)} %sum_2_1.1), channel_id=1, source_target_pairs={{0,4},{2,6},{4,0},{6,2},{8,12},{10,14},{12,8},{14,10},{16,20},{18,... | collective-permute-start | bytes 688136 | tf_op jit(solution)/shard_map/ppermute | solution.py:20
  49.2 0.8 %collective-permute-done.19.part_ref = bf16[64,1792]{1,0:T(8,128)(2,1)S(1)} collective-permute-done((bf16[64,1792]{1,0:T(8,128)(2,1)S(1)}, bf16[64,1792]{1,0:T(8,128)(2,1)S(1)}, u32[]{:S(2)}, u32[]{:S(2)}) %collective-permute-start.19) | collective-permute-done | bytes 229408 | tf_op jit(solution)/shard_map/ppermute | solution.py:20
  50.0 1.6 %collective-permute-start.20 = (bf16[64,1792]{1,0:T(8,128)(2,1)S(1)}, bf16[64,1792]{1,0:T(8,128)(2,1)S(1)}, u32[]{:S(2)}, u32[]{:S(2)}) collective-permute-start(bf16[64,1792]{1,0:T(8,128)(2,1)S(1)} %sum_2_0.1), channel_id=1, source_target_pairs={{0,4},{2,6},{4,0},{6,2},{8,12},{10,14},{12,8},{14,10},{16,20},{18,... | collective-permute-start | bytes 688136 | tf_op jit(solution)/shard_map/ppermute | solution.py:20
  51.6 2.0 %collective-permute-done.22.refs_3_ = bf16[64,1792]{1,0:T(8,128)(2,1)S(1)} collective-permute-done((bf16[64,1792]{1,0:T(8,128)(2,1)S(1)}, bf16[64,1792]{1,0:T(8,128)(2,1)S(1)}, u32[]{:S(2)}, u32[]{:S(2)}) %collective-permute-start.22) | collective-permute-done | bytes 229408 | tf_op jit(solution)/shard_map/ppermute | solution.py:20
  53.7 2.5 %collective-permute-done.20.refs_2_ = bf16[64,1792]{1,0:T(8,128)(2,1)S(1)} collective-permute-done((bf16[64,1792]{1,0:T(8,128)(2,1)S(1)}, bf16[64,1792]{1,0:T(8,128)(2,1)S(1)}, u32[]{:S(2)}, u32[]{:S(2)}) %collective-permute-start.20) | collective-permute-done | bytes 229408 | tf_op jit(solution)/shard_map/ppermute | solution.py:20
  56.1 0.2 sum_split.1
  56.3 2.5 %collective-permute-start.23 = (bf16[16,3584]{1,0:T(8,128)(2,1)S(1)}, bf16[16,3584]{1,0:T(8,128)(2,1)S(1)}, u32[]{:S(2)}, u32[]{:S(2)}) collective-permute-start(bf16[16,3584]{1,0:T(8,128)(2,1)S(1)} %get-tuple-element.72), channel_id=1, source_target_pairs={{0,24},{2,26},{4,28},{6,30},{8,16},{10,18},{12,20},{14,22},{16,8},... | collective-permute-start | bytes 344072 | tf_op jit(solution)/shard_map/ppermute | solution.py:20
  58.8 1.9 %collective-permute-start.25 = (bf16[16,3584]{1,0:T(8,128)(2,1)S(1)}, bf16[16,3584]{1,0:T(8,128)(2,1)S(1)}, u32[]{:S(2)}, u32[]{:S(2)}) collective-permute-start(bf16[16,3584]{1,0:T(8,128)(2,1)S(1)} %get-tuple-element.74), channel_id=1, source_target_pairs={{0,8},{2,10},{4,12},{6,14},{8,0},{10,2},{12,4},{14,6},{16,24},{18,... | collective-permute-start | bytes 344072 | tf_op jit(solution)/shard_map/ppermute | solution.py:20
  60.7 2.3 %collective-permute-done.23.refs_1_ = bf16[16,3584]{1,0:T(8,128)(2,1)S(1)} collective-permute-done((bf16[16,3584]{1,0:T(8,128)(2,1)S(1)}, bf16[16,3584]{1,0:T(8,128)(2,1)S(1)}, u32[]{:S(2)}, u32[]{:S(2)}) %collective-permute-start.23) | collective-permute-done | bytes 114720 | tf_op jit(solution)/shard_map/ppermute | solution.py:20
  63.1 2.4 %collective-permute-done.24.refs_2_ = bf16[16,3584]{1,0:T(8,128)(2,1)S(1)} collective-permute-done((bf16[16,3584]{1,0:T(8,128)(2,1)S(1)}, bf16[16,3584]{1,0:T(8,128)(2,1)S(1)}, u32[]{:S(2)}, u32[]{:S(2)}) %collective-permute-start.24) | collective-permute-done | bytes 114720 | tf_op jit(solution)/shard_map/ppermute | solution.py:20
  65.5 0.7 %sum_out.1 = bf16[16,3584]{1,0:T(8,128)(2,1)} custom-call(bf16[16,3584]{1,0:T(8,128)(2,1)S(1)} %get-tuple-element.71.refs_0_, bf16[16,3584]{1,0:T(8,128)(2,1)S(1)} %collective-permute-done.23.refs_1_, bf16[16,3584]{1,0:T(8,128)(2,1)S(1)} %collective-permute-done.24.refs_2_, bf16[16,3584]{1,0:T(8,128)(2,1)S(1)} %collective-permute-done.25.refs_3_), custom_call_target="tpu_custom_call" | custom-call | tf_op jit(solution)/shard_map/sum_out/pallas_call | solution.py:48
  (27 shorter events, 0.2 us)
Async XLA Ops:
  1.0 10.9 %collective-permute-start = (bf16[16,3712]{1,0:T(8,128)(2,1)S(1)}, bf16[16,3712]{1,0:T(8,128)(2,1)S(1)}, u32[]{:S(2)}, u32[]{:S(2)}) collective-permute-start(bf16[16,3712]{1,0:T(8,128)(2,1)S(1)} %first_piece.1.refs_0_), channel_id=1, source_target_pairs={{0,8},{2,10},{4,12},{6,14},{8,0},{10,2},{12,4},{14,6},{16,24},{18,... | collective-permute-start | bytes 356360 | tf_op jit(solution)/shard_map/ppermute | solution.py:20
  4.1 7.9 %collective-permute-start.1 = (bf16[16,3712]{1,0:T(8,128)(2,1)S(1)}, bf16[16,3712]{1,0:T(8,128)(2,1)S(1)}, u32[]{:S(2)}, u32[]{:S(2)}) collective-permute-start(bf16[16,3712]{1,0:T(8,128)(2,1)S(1)} %first_piece.1.refs_0_), channel_id=1, source_target_pairs={{0,16},{2,18},{4,20},{6,22},{8,24},{10,26},{12,28},{14,30},{16,0},... | collective-permute-start | bytes 356360 | tf_op jit(solution)/shard_map/ppermute | solution.py:20
  6.6 6.8 %collective-permute-start.2 = (bf16[16,3712]{1,0:T(8,128)(2,1)S(1)}, bf16[16,3712]{1,0:T(8,128)(2,1)S(1)}, u32[]{:S(2)}, u32[]{:S(2)}) collective-permute-start(bf16[16,3712]{1,0:T(8,128)(2,1)S(1)} %first_piece.1.refs_0_), channel_id=1, source_target_pairs={{0,24},{2,26},{4,28},{6,30},{8,16},{10,18},{12,20},{14,22},{16,8},... | collective-permute-start | bytes 356360 | tf_op jit(solution)/shard_map/ppermute | solution.py:20
  13.5 10.2 %collective-permute-start.3 = (bf16[64,3712]{1,0:T(8,128)(2,1)S(1)}, bf16[64,3712]{1,0:T(8,128)(2,1)S(1)}, u32[]{:S(2)}, u32[]{:S(2)}) collective-permute-start(bf16[64,3712]{1,0:T(8,128)(2,1)S(1)} %get-tuple-element.41.refs_0_.refs_12_), channel_id=1, source_target_pairs={{0,2},{2,0},{4,6},{6,4},{8,10},{10,8},{12,14},{14,12},{16,18},{18,... | collective-permute-start | bytes 1425416 | tf_op jit(solution)/shard_map/ppermute | solution.py:20
  15.0 7.3 %collective-permute-start.8 = (bf16[64,1920]{1,0:T(8,128)(2,1)S(1)}, bf16[64,1920]{1,0:T(8,128)(2,1)S(1)}, u32[]{:S(2)}, u32[]{:S(2)}) collective-permute-start(bf16[64,1920]{1,0:T(8,128)(2,1)S(1)} %get-tuple-element.44), channel_id=1, source_target_pairs={{0,4},{2,6},{4,0},{6,2},{8,12},{10,14},{12,8},{14,10},{16,20},{18,... | collective-permute-start | bytes 737288 | tf_op jit(solution)/shard_map/ppermute | solution.py:20
  16.6 7.1 %collective-permute-start.5 = (bf16[64,1792]{1,0:T(8,128)(2,1)S(1)}, bf16[64,1792]{1,0:T(8,128)(2,1)S(1)}, u32[]{:S(2)}, u32[]{:S(2)}) collective-permute-start(bf16[64,1792]{1,0:T(8,128)(2,1)S(1)} %get-tuple-element.42), channel_id=1, source_target_pairs={{0,4},{2,6},{4,0},{6,2},{8,12},{10,14},{12,8},{14,10},{16,20},{18,... | collective-permute-start | bytes 688136 | tf_op jit(solution)/shard_map/ppermute | solution.py:20
  22.3 6.9 %collective-permute-start.10 = (bf16[64,3712]{1,0:T(8,128)(2,1)S(1)}, bf16[64,3712]{1,0:T(8,128)(2,1)S(1)}, u32[]{:S(2)}, u32[]{:S(2)}) collective-permute-start(bf16[64,3712]{1,0:T(8,128)(2,1)S(1)} %get-tuple-element.41.refs_0_.refs_12_), channel_id=1, source_target_pairs={{0,1},{1,0},{2,3},{3,2},{4,5},{5,4},{6,7},{7,6},{8,9},{9,8},{10,11... | collective-permute-start | bytes 1425416 | tf_op jit(solution)/shard_map/ppermute | solution.py:32
  22.4 6.9 %collective-permute-start.12 = (bf16[64,1920]{1,0:T(8,128)(2,1)S(1)}, bf16[64,1920]{1,0:T(8,128)(2,1)S(1)}, u32[]{:S(2)}, u32[]{:S(2)}) collective-permute-start(bf16[64,1920]{1,0:T(8,128)(2,1)S(1)} %collective-permute-done.8.refs_2_.refs_14_), channel_id=1, source_target_pairs={{0,1},{1,0},{2,3},{3,2},{4,5},{5,4},{6,7},{7,6},{8,9},{9,8},{10,11... | collective-permute-start | bytes 737288 | tf_op jit(solution)/shard_map/ppermute | solution.py:32
  22.8 8.5 %collective-permute-start.9 = (bf16[64,1920]{1,0:T(8,128)(2,1)S(1)}, bf16[64,1920]{1,0:T(8,128)(2,1)S(1)}, u32[]{:S(2)}, u32[]{:S(2)}) collective-permute-start(bf16[64,1920]{1,0:T(8,128)(2,1)S(1)} %collective-permute-done.8.refs_2_.refs_14_), channel_id=1, source_target_pairs={{0,2},{2,0},{4,6},{6,4},{8,10},{10,8},{12,14},{14,12},{16,18},{18,... | collective-permute-start | bytes 737288 | tf_op jit(solution)/shard_map/ppermute | solution.py:20
  23.7 5.5 %collective-permute-start.11 = (bf16[64,1792]{1,0:T(8,128)(2,1)S(1)}, bf16[64,1792]{1,0:T(8,128)(2,1)S(1)}, u32[]{:S(2)}, u32[]{:S(2)}) collective-permute-start(bf16[64,1792]{1,0:T(8,128)(2,1)S(1)} %piece_2.1.refs_1_), channel_id=1, source_target_pairs={{0,1},{1,0},{2,3},{3,2},{4,5},{5,4},{6,7},{7,6},{8,9},{9,8},{10,11... | collective-permute-start | bytes 688136 | tf_op jit(solution)/shard_map/ppermute | solution.py:32
  25.2 6.7 %collective-permute-start.6 = (bf16[64,1792]{1,0:T(8,128)(2,1)S(1)}, bf16[64,1792]{1,0:T(8,128)(2,1)S(1)}, u32[]{:S(2)}, u32[]{:S(2)}) collective-permute-start(bf16[64,1792]{1,0:T(8,128)(2,1)S(1)} %piece_2.1.refs_1_), channel_id=1, source_target_pairs={{0,2},{2,0},{4,6},{6,4},{8,10},{10,8},{12,14},{14,12},{16,18},{18,... | collective-permute-start | bytes 688136 | tf_op jit(solution)/shard_map/ppermute | solution.py:20
  29.2 5.1 %collective-permute-start.4 = (bf16[64,3712]{1,0:T(8,128)(2,1)S(1)}, bf16[64,3712]{1,0:T(8,128)(2,1)S(1)}, u32[]{:S(2)}, u32[]{:S(2)}) collective-permute-start(bf16[64,3712]{1,0:T(8,128)(2,1)S(1)} %collective-permute-done.3.refs_1_.refs_0_.refs_13_), channel_id=1, source_target_pairs={{0,1},{1,0},{2,3},{3,2},{4,5},{5,4},{6,7},{7,6},{8,9},{9,8},{10,11... | collective-permute-start | bytes 1425416 | tf_op jit(solution)/shard_map/ppermute | solution.py:32
  31.4 2.9 %collective-permute-start.13 = (bf16[64,1920]{1,0:T(8,128)(2,1)S(1)}, bf16[64,1920]{1,0:T(8,128)(2,1)S(1)}, u32[]{:S(2)}, u32[]{:S(2)}) collective-permute-start(bf16[64,1920]{1,0:T(8,128)(2,1)S(1)} %piece_3.1.refs_2_.refs_15_), channel_id=1, source_target_pairs={{0,1},{1,0},{2,3},{3,2},{4,5},{5,4},{6,7},{7,6},{8,9},{9,8},{10,11... | collective-permute-start | bytes 737288 | tf_op jit(solution)/shard_map/ppermute | solution.py:32
  31.9 2.3 %collective-permute-start.7 = (bf16[64,1792]{1,0:T(8,128)(2,1)S(1)}, bf16[64,1792]{1,0:T(8,128)(2,1)S(1)}, u32[]{:S(2)}, u32[]{:S(2)}) collective-permute-start(bf16[64,1792]{1,0:T(8,128)(2,1)S(1)} %collective-permute-done.6.refs_1_), channel_id=1, source_target_pairs={{0,1},{1,0},{2,3},{3,2},{4,5},{5,4},{6,7},{7,6},{8,9},{9,8},{10,11... | collective-permute-start | bytes 688136 | tf_op jit(solution)/shard_map/ppermute | solution.py:32
  37.9 2.8 %collective-permute-start.14 = (bf16[64,3584]{1,0:T(8,128)(2,1)S(1)}, bf16[64,3584]{1,0:T(8,128)(2,1)S(1)}, u32[]{:S(2)}, u32[]{:S(2)}) collective-permute-start(bf16[64,3584]{1,0:T(8,128)(2,1)S(1)} %get-tuple-element.61.rest_2_), channel_id=1, source_target_pairs={{0,1},{1,0},{2,3},{3,2},{4,5},{5,4},{6,7},{7,6},{8,9},{9,8},{10,11... | collective-permute-start | bytes 1376264 | tf_op jit(solution)/shard_map/ppermute | solution.py:32
  40.8 2.7 %collective-permute-start.17 = (bf16[64,3584]{1,0:T(8,128)(2,1)S(1)}, bf16[64,3584]{1,0:T(8,128)(2,1)S(1)}, u32[]{:S(2)}, u32[]{:S(2)}) collective-permute-start(bf16[64,3584]{1,0:T(8,128)(2,1)S(1)} %far_1.1), channel_id=1, source_target_pairs={{0,1},{1,0},{2,3},{3,2},{4,5},{5,4},{6,7},{7,6},{8,9},{9,8},{10,11... | collective-permute-start | bytes 1376264 | tf_op jit(solution)/shard_map/ppermute | solution.py:32
  41.0 3.6 %collective-permute-start.16 = (bf16[64,3584]{1,0:T(8,128)(2,1)S(1)}, bf16[64,3584]{1,0:T(8,128)(2,1)S(1)}, u32[]{:S(2)}, u32[]{:S(2)}) collective-permute-start(bf16[64,3584]{1,0:T(8,128)(2,1)S(1)} %far_0.1), channel_id=1, source_target_pairs={{0,1},{1,0},{2,3},{3,2},{4,5},{5,4},{6,7},{7,6},{8,9},{9,8},{10,11... | collective-permute-start | bytes 1376264 | tf_op jit(solution)/shard_map/ppermute | solution.py:32
  41.4 3.2 %collective-permute-start.15 = (bf16[64,3584]{1,0:T(8,128)(2,1)S(1)}, bf16[64,3584]{1,0:T(8,128)(2,1)S(1)}, u32[]{:S(2)}, u32[]{:S(2)}) collective-permute-start(bf16[64,3584]{1,0:T(8,128)(2,1)S(1)} %far_2.1), channel_id=1, source_target_pairs={{0,1},{1,0},{2,3},{3,2},{4,5},{5,4},{6,7},{7,6},{8,9},{9,8},{10,11... | collective-permute-start | bytes 1376264 | tf_op jit(solution)/shard_map/ppermute | solution.py:32
  41.5 6.0 %collective-permute-start.21 = (bf16[64,1792]{1,0:T(8,128)(2,1)S(1)}, bf16[64,1792]{1,0:T(8,128)(2,1)S(1)}, u32[]{:S(2)}, u32[]{:S(2)}) collective-permute-start(bf16[64,1792]{1,0:T(8,128)(2,1)S(1)} %get-tuple-element.65.refs_2_.refs_3_), channel_id=1, source_target_pairs={{0,2},{2,0},{4,6},{6,4},{8,10},{10,8},{12,14},{14,12},{16,18},{18,... | collective-permute-start | bytes 688136 | tf_op jit(solution)/shard_map/ppermute | solution.py:20
  42.4 7.6 %collective-permute-start.19 = (bf16[64,1792]{1,0:T(8,128)(2,1)S(1)}, bf16[64,1792]{1,0:T(8,128)(2,1)S(1)}, u32[]{:S(2)}, u32[]{:S(2)}) collective-permute-start(bf16[64,1792]{1,0:T(8,128)(2,1)S(1)} %get-tuple-element.64.refs_1_.refs_2_), channel_id=1, source_target_pairs={{0,2},{2,0},{4,6},{6,4},{8,10},{10,8},{12,14},{14,12},{16,18},{18,... | collective-permute-start | bytes 688136 | tf_op jit(solution)/shard_map/ppermute | solution.py:20
  43.6 12.5 %collective-permute-start.18 = (bf16[64,3584]{1,0:T(8,128)(2,1)S(1)}, bf16[64,3584]{1,0:T(8,128)(2,1)S(1)}, u32[]{:S(2)}, u32[]{:S(2)}) collective-permute-start(bf16[64,3584]{1,0:T(8,128)(2,1)S(1)} %sum_1.1.refs_5_), channel_id=1, source_target_pairs={{0,2},{2,0},{4,6},{6,4},{8,10},{10,8},{12,14},{14,12},{16,18},{18,... | collective-permute-start | bytes 1376264 | tf_op jit(solution)/shard_map/ppermute | solution.py:20
  47.6 6.1 %collective-permute-start.22 = (bf16[64,1792]{1,0:T(8,128)(2,1)S(1)}, bf16[64,1792]{1,0:T(8,128)(2,1)S(1)}, u32[]{:S(2)}, u32[]{:S(2)}) collective-permute-start(bf16[64,1792]{1,0:T(8,128)(2,1)S(1)} %sum_2_1.1), channel_id=1, source_target_pairs={{0,4},{2,6},{4,0},{6,2},{8,12},{10,14},{12,8},{14,10},{16,20},{18,... | collective-permute-start | bytes 688136 | tf_op jit(solution)/shard_map/ppermute | solution.py:20
  50.0 6.1 %collective-permute-start.20 = (bf16[64,1792]{1,0:T(8,128)(2,1)S(1)}, bf16[64,1792]{1,0:T(8,128)(2,1)S(1)}, u32[]{:S(2)}, u32[]{:S(2)}) collective-permute-start(bf16[64,1792]{1,0:T(8,128)(2,1)S(1)} %sum_2_0.1), channel_id=1, source_target_pairs={{0,4},{2,6},{4,0},{6,2},{8,12},{10,14},{12,8},{14,10},{16,20},{18,... | collective-permute-start | bytes 688136 | tf_op jit(solution)/shard_map/ppermute | solution.py:20
  56.3 6.8 %collective-permute-start.23 = (bf16[16,3584]{1,0:T(8,128)(2,1)S(1)}, bf16[16,3584]{1,0:T(8,128)(2,1)S(1)}, u32[]{:S(2)}, u32[]{:S(2)}) collective-permute-start(bf16[16,3584]{1,0:T(8,128)(2,1)S(1)} %get-tuple-element.72), channel_id=1, source_target_pairs={{0,24},{2,26},{4,28},{6,30},{8,16},{10,18},{12,20},{14,22},{16,8},... | collective-permute-start | bytes 344072 | tf_op jit(solution)/shard_map/ppermute | solution.py:20
  58.8 6.7 %collective-permute-start.24 = (bf16[16,3584]{1,0:T(8,128)(2,1)S(1)}, bf16[16,3584]{1,0:T(8,128)(2,1)S(1)}, u32[]{:S(2)}, u32[]{:S(2)}) collective-permute-start(bf16[16,3584]{1,0:T(8,128)(2,1)S(1)} %get-tuple-element.73), channel_id=1, source_target_pairs={{0,16},{2,18},{4,20},{6,22},{8,24},{10,26},{12,28},{14,30},{16,0},... | collective-permute-start | bytes 344072 | tf_op jit(solution)/shard_map/ppermute | solution.py:20
  58.8 6.7 %collective-permute-start.25 = (bf16[16,3584]{1,0:T(8,128)(2,1)S(1)}, bf16[16,3584]{1,0:T(8,128)(2,1)S(1)}, u32[]{:S(2)}, u32[]{:S(2)}) collective-permute-start(bf16[16,3584]{1,0:T(8,128)(2,1)S(1)} %get-tuple-element.74), channel_id=1, source_target_pairs={{0,8},{2,10},{4,12},{6,14},{8,0},{10,2},{12,4},{14,6},{16,24},{18,... | collective-permute-start | bytes 344072 | tf_op jit(solution)/shard_map/ppermute | solution.py:20
